TPU v7x, 128 devices: a whole 4x4x4 slice. The times are simulated.
128 devices in a mesh: px: 8 (over z_lo, y), py: 16 (over z_hi, x, core).
Axes of the slice: x: 4, y: 4, z: 4 (z_hi: 2, z_lo: 2; z = z_hi * 2 + z_lo), core: 2. Of those that a mesh axis runs over, the one named last changes fastest.
Arguments:
- velocity: float32 [3, 32, 256, 512], P(None, 'px', 'py'), may hold values from -4 to 4
- first_weight: bfloat16 [64, 81], replicated, may hold values from -0.625 to 0.625
- mid_weight: bfloat16 [64, 64], replicated, may hold values from -0.75 to 0.75
- last_weight: bfloat16 [6, 64], replicated, may hold values from -0.75 to 0.75
- offsets: int32 [32, 256], P('px', 'py'), may hold values from 0 to 256
Outputs:
- final_velocity: float32 [3, 32, 256, 512], P(None, 'px', 'py')
- grad_first: float32 [64, 81], replicated
- grad_mid: float32 [64, 64], replicated
- grad_last: float32 [6, 64], replicated
All inputs are finite; a program needn't handle non-finite values.
Results may differ from a plain program's by a relative error of at most 0.0003.
Values may be sent and summed in bfloat16 or wider, within the bound.
No kernel may reach another device: no remote copies, remote signals or barrier semaphores. Data moves between devices by JAX's collectives and lax.ppermute only.
A program may use at most 192 MiB of HBM per device.

v0:
```python
import jax
import jax.numpy as jnp
import numpy as np
from jax import lax
from jax.experimental import pallas as pl
from jax.experimental.pallas import tpu as pltpu
from jax.sharding import PartitionSpec as P

f32, bf16 = jnp.float32, jnp.bfloat16
AXES = ("px", "py")
LANES = 640
ROWS = 40
WINDOW = 256
NT = (((1,), (1,)), ((), ()))


def selections():
    pick = np.zeros((512, 216), np.float32)
    pick_target = np.zeros((256, 96), np.float32)
    for y in range(16):
        for c in range(3):
            for ox in range(3):
                for oy in range(3):
                    pick[y * 32 + c * 9 + ox * 3 + oy, (c * 3 + ox) * 24 + y + oy + 3] = 1
        for c in range(6):
            pick_target[y * 16 + c, c * 16 + y] = 1
    back = np.zeros((96, 128), np.float32)
    for oz in range(3):
        for c in range(3):
            for o in range(9):
                back[oz * 32 + c * 9 + o, c * 27 + o * 3 + oz] = 1
    return pick, pick_target, back


def dot(a, b):
    return jnp.dot(a, b, preferred_element_type=f32)


def dot_cells(a, b):
    return lax.dot_general(a, b, NT, preferred_element_type=f32)


def shift_z(value):
    return pltpu.roll(value, LANES - 1, 1) - pltpu.roll(value, 1, 1)


def differences(field, plane, row):
    here = pl.ds(row, 8)
    center = [field[c, plane, here, :] for c in range(3)]
    along_x = [field[c, plane + 1, here, :] - field[c, plane - 1, here, :] for c in range(3)]
    along_y = [field[c, plane, pl.ds(row + 1, 8), :] - field[c, plane, pl.ds(row - 1, 8), :] for c in range(3)]
    along_z = [shift_z(center[c]) for c in range(3)]
    return center, (along_x, along_y, along_z)


def stress_rows(field, plane, tau, tau_plane, row):
    _, d = differences(field, plane, row)
    xy, xz, yz = d[0][1] + d[1][0], d[0][2] + d[2][0], d[1][2] + d[2][1]
    diagonal = d[0][0] * d[0][0] + d[1][1] * d[1][1] + d[2][2] * d[2][2]
    mixed = xy * xy + xz * xz + yz * yz
    nu = 0.05 + 0.04 * jnp.sqrt(0.5 * diagonal + 0.25 * mixed)
    half = -0.5 * nu
    rows = pl.ds(row, 8)
    for c in range(3):
        tau[c, tau_plane, rows, :] = -nu * d[c][c]
    tau[3, tau_plane, rows, :] = half * xy
    tau[4, tau_plane, rows, :] = half * xz
    tau[5, tau_plane, rows, :] = half * yz


def step_rows(field, plane, tau, tau_plane, row):
    center, d = differences(field, plane, row)
    here = pl.ds(row, 8)

    def tau_x(c):
        return tau[c, tau_plane + 1, here, :] - tau[c, tau_plane - 1, here, :]

    def tau_y(c):
        return tau[c, tau_plane, pl.ds(row + 1, 8), :] - tau[c, tau_plane, pl.ds(row - 1, 8), :]

    def tau_z(c):
        return shift_z(tau[c, tau_plane, here, :])

    parts = ((0, 3, 4), (3, 1, 5), (4, 5, 2))
    out = []
    for j in range(3):
        a, b, c = parts[j]
        total = tau_x(a) + tau_y(b) + tau_z(c)
        total += center[0] * d[0][j] + center[1] * d[1][j] + center[2] * d[2][j]
        new = center[j] - 0.05 * total
        out.append(new + 0.005 if j == 0 else new)
    return out


def closure(field, base, tau, tau_base, offs, pick, pick_target, tile, tile_target, weights, totals):
    w1, w2, w2t, w3, w3t = weights
    g1, g2, g3 = totals

    def step(x, _):
        rows = [field[c, base + x + ox - 1, 8:32, 0:512] for c in range(3) for ox in range(3)]
        tile[:, 128:640] = dot(pick[...], jnp.concatenate(rows, 0).astype(bf16)).astype(bf16)
        rows = [tau[c, tau_base + x, 12:28, 0:512].astype(bf16) for c in range(6)]
        tile_target[:, 128:640] = dot(pick_target[...], jnp.concatenate(rows, 0)).astype(bf16)
        columns, targets = [], []
        for y in range(16):
            start = offs[x, y] + 127
            base_lane = pl.multiple_of(lax.shift_right_logical(start, 7) * 128, 128)
            turn = (512 - (start & 127)) & 511
            window = pltpu.roll(tile[y * 32 : y * 32 + 32, pl.ds(base_lane, 512)], turn, 1)
            columns.append(jnp.concatenate([window[:, 0:256], window[:, 1:257], window[:, 2:258]], 0))
            target = pltpu.roll(tile_target[y * 16 : y * 16 + 16, pl.ds(base_lane, 512)], turn, 1)
            targets.append(target[:, 1:257])
        cols = jnp.concatenate(columns, 1)
        target = jnp.concatenate(targets, 1)
        h1 = dot(w1[...], cols)
        t1 = jnp.tanh(h1)
        q1 = h1 * t1
        a1 = (h1 + q1).astype(bf16)
        s1 = (1.0 + t1) * (1.0 + (h1 - q1))
        h2 = dot(w2[...], a1)
        t2 = jnp.tanh(h2)
        q2 = h2 * t2
        a2 = (h2 + q2).astype(bf16)
        s2 = (1.0 + t2) * (1.0 + (h2 - q2))
        misfit = dot(w3[...], jnp.concatenate([a2, target], 0)).astype(bf16)
        b2 = (dot(w3t[...], misfit) * s2).astype(bf16)
        b1 = (dot(w2t[...], b2) * s1).astype(bf16)
        g3[...] += dot_cells(misfit, a2)
        g2[...] += dot_cells(b2, a1)
        g1[...] += dot_cells(b1, cols)
        return 0

    lax.fori_loop(0, 4, step, 0)


def kernel(
    offs, own, x_low, x_high, y_low, y_high, w1, w2, w2t, w3, w3t, pick, pick_target, back,
    final, packed, field, middle, tau, tile, tile_target, g1, g2, g3,
):
    zeros = jnp.zeros((ROWS, 128), f32)
    line = jnp.zeros((1, LANES), f32)
    for c in range(3):
        for p in range(12):
            field[c, p, :, 512:640] = zeros
            field[c, p, 7:8, :] = line
            field[c, p, 32:33, :] = line
            source, q = ((x_low, p), (own, p - 4), (x_high, p - 8))[p // 4]
            field[c, p, 12:28, 0:512] = source[c, q]
            field[c, p, 8:12, 0:512] = y_low[c, p]
            field[c, p, 28:32, 0:512] = y_high[c, p]
    for c in range(6):
        for p in range(10):
            tau[c, p, 7:8, :] = line
            tau[c, p, 32:33, :] = line
    for target in (tile, tile_target):
        edge = jnp.zeros((target.shape[0], 128), bf16)
        target[:, 0:128] = edge
        target[:, 640:768] = edge
    g1[...] = jnp.zeros_like(g1)
    g2[...] = jnp.zeros_like(g2)
    g3[...] = jnp.zeros_like(g3)
    weights, totals = (w1, w2, w2t, w3, w3t), (g1, g2, g3)

    def stress_zero(p, _):
        for row in (8, 16, 24):
            stress_rows(field, p + 1, tau, p, row)
        return 0

    lax.fori_loop(0, 10, stress_zero, 0)
    closure(field, 4, tau, 3, offs, pick, pick_target, tile, tile_target, weights, totals)

    inside = lax.broadcasted_iota(jnp.int32, (8, LANES), 1) < 512

    def advance_middle(p, _):
        for row in (8, 16, 24):
            new = step_rows(field, p + 2, tau, p + 1, row)
            for c in range(3):
                middle[c, p, pl.ds(row, 8), :] = jnp.where(inside, new[c], 0.0)
        return 0

    lax.fori_loop(0, 8, advance_middle, 0)

    def stress_one(p, _):
        for row in (8, 16, 24):
            stress_rows(middle, p + 1, tau, p, row)
        return 0

    lax.fori_loop(0, 6, stress_one, 0)
    closure(middle, 2, tau, 1, offs, pick, pick_target, tile, tile_target, weights, totals)

    def advance_final(p, _):
        for row in (12, 20):
            new = step_rows(middle, p + 2, tau, p + 1, row)
            for c in range(3):
                final[c, p, row - 12 : row - 4, :] = new[c][:, 0:512]
        return 0

    lax.fori_loop(0, 4, advance_final, 0)
    scale = 0.5**22
    packed[0:64, :] = scale * jnp.dot(
        g1[...], back[...], preferred_element_type=f32, precision=lax.Precision.HIGHEST
    )
    packed[64:96, :] = scale * jnp.concatenate([g2[0:32, :], g2[32:64, :]], 1)
    packed[96:104, :] = scale * jnp.concatenate([g3[0:8, :], jnp.zeros((8, 64), f32)], 1)


def run_kernel(offsets, own, x_low, x_high, y_low, y_high, w1, w2, w2t, w3, w3t):
    pick, pick_target, back = selections()
    vmem = pl.BlockSpec(memory_space=pltpu.VMEM)
    smem = pl.BlockSpec(memory_space=pltpu.SMEM)
    return pl.pallas_call(
        kernel,
        in_specs=[smem] + [vmem] * 13,
        out_specs=[vmem] * 2,
        out_shape=[
            jax.ShapeDtypeStruct((3, 4, 16, 512), f32),
            jax.ShapeDtypeStruct((104, 128), f32),
        ],
        scratch_shapes=[
            pltpu.VMEM((3, 12, ROWS, LANES), f32),
            pltpu.VMEM((3, 8, ROWS, LANES), f32),
            pltpu.VMEM((6, 10, ROWS, LANES), f32),
            pltpu.VMEM((512, 768), bf16),
            pltpu.VMEM((256, 768), bf16),
            pltpu.VMEM((64, 96), f32),
            pltpu.VMEM((64, 64), f32),
            pltpu.VMEM((16, 64), f32),
        ],
        compiler_params=pltpu.CompilerParams(vmem_limit_bytes=56 * 2**20),
    )(
        offsets, own, x_low, x_high, y_low, y_high, w1, w2, w2t, w3, w3t,
        jnp.asarray(pick, bf16), jnp.asarray(pick_target, bf16), jnp.asarray(back, f32),
    )


def pairs(move):
    return [(i * 16 + j, (move(i, j)[0] % 8) * 16 + move(i, j)[1] % 16) for i in range(8) for j in range(16)]


def partner(k, odd_up):
    if not odd_up:
        return k ^ 1
    return (k + 1) % 4 if k % 2 else (k - 1) % 4


def swap_core(i, j):
    return (i, j ^ 1)


def swap_y(odd_up):
    return lambda i, j: (i & 4 | partner(i & 3, odd_up), j)


def swap_x(odd_up):
    return lambda i, j: (i, j & 9 | partner(j >> 1 & 3, odd_up) << 1)


def swap_z(odd_up):
    def move(i, j):
        z = partner((j >> 3) * 2 + (i >> 2), odd_up)
        return ((z & 1) * 4 + (i & 3), (z >> 1) * 8 + (j & 7))

    return move


def sum_everywhere(value):
    for move in (swap_core, swap_y(0), swap_y(1), swap_x(0), swap_x(1), swap_z(0), swap_z(1)):
        value = value + lax.ppermute(value, AXES, pairs(move))
    return value


def body(velocity, first_weight, mid_weight, last_weight, offsets):
    up = pairs(lambda i, j: (i + 1, j))
    down = pairs(lambda i, j: (i - 1, j))
    x_low = lax.ppermute(velocity, AXES, up)
    x_high = lax.ppermute(velocity, AXES, down)
    wide = jnp.concatenate([x_low, velocity, x_high], 1)
    y_low = lax.ppermute(wide[:, :, 12:, :], AXES, pairs(lambda i, j: (i, j + 1)))
    y_high = lax.ppermute(wide[:, :, :4, :], AXES, pairs(lambda i, j: (i, j - 1)))

    half = jnp.asarray(0.5, bf16)
    w1 = jnp.transpose(first_weight.reshape(64, 27, 3), (0, 2, 1))
    w1 = (jnp.pad(w1, ((0, 0), (0, 0), (0, 5))) * half).reshape(64, 96)
    w2 = mid_weight * half
    w2t = mid_weight.T * half
    w3 = jnp.pad(last_weight, ((0, 10), (0, 0)))
    w3t = w3.T * half
    w3 = jnp.concatenate([w3, -jnp.eye(16, dtype=bf16)], 1)
    final, packed = run_kernel(offsets, velocity, x_low, x_high, y_low, y_high, w1, w2, w2t, w3, w3t)
    total = sum_everywhere(packed)
    grad_mid = jnp.concatenate([total[64:96, :64], total[64:96, 64:]], 0)
    return final, total[:64, :81], grad_mid, total[96:102, :64]


def solution(mesh):
    in_specs = (P(None, "px", "py", None), P(), P(), P(), P("px", "py"))
    out_specs = (P(None, "px", "py", None), P(), P(), P())
    return jax.shard_map(body, mesh=mesh, in_specs=in_specs, out_specs=out_specs, check_vma=False)
```

profile of v0, /device:TPU:0, one launch (start us, length us, event | category | flops | bytes accessed | tf_op | source)
XLA Modules:
  0.0 88.9 jit_solution(2446411679882691221)
XLA Ops:
  0.6 1.7 %collective-permute-start = (f32[3,4,16,512]{3,2,1,0:T(8,128)}, f32[3,4,16,512]{3,2,1,0:T(8,128)S(1)}, u32[]{:S(2)}, u32[]{:S(2)}) collective-permute-start(f32[3,4,16,512]{3,2,1,0:T(8,128)} %own.1), channel_id=1, source_target_pairs={{0,16},{1,17},{2,18},{3,19},{4,20},{5,21},{6,22},{7,23},{8,24},{9,... | collective-permute-start | bytes 1179656 | tf_op jit(solution)/shard_map/ppermute | solution.py:275
  2.4 2.9 %collective-permute-start.1 = (f32[3,4,16,512]{3,2,1,0:T(8,128)}, f32[3,4,16,512]{3,2,1,0:T(8,128)S(1)}, u32[]{:S(2)}, u32[]{:S(2)}) collective-permute-start(f32[3,4,16,512]{3,2,1,0:T(8,128)} %own.1), channel_id=1, source_target_pairs={{0,112},{1,113},{2,114},{3,115},{4,116},{5,117},{6,118},{7,119},{8... | collective-permute-start | bytes 1179656 | tf_op jit(solution)/shard_map/ppermute | solution.py:276
  5.2 0.8 copy.33
  6.7 0.7 copy.37.w2
  7.4 0.8 copy.34
  8.2 0.8 copy.31
  9.1 0.7 copy.36.w1
  9.8 4.6 %collective-permute-done.x_low = f32[3,4,16,512]{3,2,1,0:T(8,128)S(1)} collective-permute-done((f32[3,4,16,512]{3,2,1,0:T(8,128)}, f32[3,4,16,512]{3,2,1,0:T(8,128)S(1)}, u32[]{:S(2)}, u32[]{:S(2)}) %collective-permute-start) | collective-permute-done | bytes 393248 | tf_op jit(solution)/shard_map/ppermute | solution.py:275
  15.5 5.3 %collective-permute-start.3 = (f32[3,12,4,512]{3,2,1,0:T(4,128)S(1)}, f32[3,12,4,512]{3,2,1,0:T(4,128)S(1)}, u32[]{:S(2)}, u32[]{:S(2)}) collective-permute-start(f32[3,12,4,512]{3,2,1,0:T(4,128)S(1)} %get-tuple-element.8), channel_id=1, source_target_pairs={{0,15},{1,0},{2,1},{3,2},{4,3},{5,4},{6,5},{7,6},{8,7},{9,8},{10,9... | collective-permute-start | bytes 884744 | tf_op jit(solution)/shard_map/ppermute | solution.py:279
  22.1 3.1 %collective-permute-done.2.y_low = f32[3,12,4,512]{3,2,1,0:T(4,128)S(1)} collective-permute-done((f32[3,12,4,512]{3,2,1,0:T(4,128)S(1)}, f32[3,12,4,512]{3,2,1,0:T(4,128)S(1)}, u32[]{:S(2)}, u32[]{:S(2)}) %collective-permute-start.2) | collective-permute-done | bytes 294944 | tf_op jit(solution)/shard_map/ppermute | solution.py:278
  25.2 0.7 copy-done.3
  26.0 27.1 %shard_map.111 = (f32[3,4,16,512]{3,2,1,0:T(8,128)}, f32[104,128]{1,0:T(8,128)}) custom-call(s32[4,16]{1,0:T(4,128)} %offs.1, f32[3,4,16,512]{3,2,1,0:T(8,128)} %own.1, f32[3,4,16,512]{3,2,1,0:T(8,128)} %copy-done.1, f32[3,4,16,512]{3,2,1,0:T(8,128)} %copy-done.2, f32[3,12,4,512]{3,2,1,0:T(4,128)} %copy-done.3, f32[3,12,4,512]{3,2,1,0:T(4,128)} %copy-done.4, ...), custom_call_target="tpu_custom_call" | custom-call | tf_op jit(solution)/shard_map/pallas_call | solution.py:211
  53.2 1.4 %collective-permute-done.4 = f32[104,128]{1,0:T(8,128)S(1)} collective-permute-done((f32[104,128]{1,0:T(8,128)}, f32[104,128]{1,0:T(8,128)S(1)}, u32[]{:S(2)}, u32[]{:S(2)}) %collective-permute-start.4) | collective-permute-done | bytes 53280 | tf_op jit(solution)/shard_map/ppermute | solution.py:268
  54.6 0.8 add.25
  55.4 4.1 %collective-permute-done.5 = f32[104,128]{1,0:T(8,128)S(1)} collective-permute-done((f32[104,128]{1,0:T(8,128)S(1)}, f32[104,128]{1,0:T(8,128)S(1)}, u32[]{:S(2)}, u32[]{:S(2)}) %collective-permute-start.5) | collective-permute-done | bytes 53280 | tf_op jit(solution)/shard_map/ppermute | solution.py:268
  59.6 3.2 %collective-permute-start.6 = (f32[104,128]{1,0:T(8,128)S(1)}, f32[104,128]{1,0:T(8,128)S(1)}, u32[]{:S(2)}, u32[]{:S(2)}) collective-permute-start(f32[104,128]{1,0:T(8,128)S(1)} %add.26), channel_id=1, source_target_pairs={{0,48},{1,49},{2,50},{3,51},{4,52},{5,53},{6,54},{7,55},{8,56},{9,... | collective-permute-start | bytes 159752 | tf_op jit(solution)/shard_map/ppermute | solution.py:268
  62.8 2.2 %collective-permute-done.6 = f32[104,128]{1,0:T(8,128)S(1)} collective-permute-done((f32[104,128]{1,0:T(8,128)S(1)}, f32[104,128]{1,0:T(8,128)S(1)}, u32[]{:S(2)}, u32[]{:S(2)}) %collective-permute-start.6) | collective-permute-done | bytes 53280 | tf_op jit(solution)/shard_map/ppermute | solution.py:268
  65.1 4.1 %collective-permute-done.7 = f32[104,128]{1,0:T(8,128)S(1)} collective-permute-done((f32[104,128]{1,0:T(8,128)S(1)}, f32[104,128]{1,0:T(8,128)S(1)}, u32[]{:S(2)}, u32[]{:S(2)}) %collective-permute-start.7) | collective-permute-done | bytes 53280 | tf_op jit(solution)/shard_map/ppermute | solution.py:268
  69.2 6.0 %collective-permute-start.8 = (f32[104,128]{1,0:T(8,128)S(1)}, f32[104,128]{1,0:T(8,128)S(1)}, u32[]{:S(2)}, u32[]{:S(2)}) collective-permute-start(f32[104,128]{1,0:T(8,128)S(1)} %add.28), channel_id=1, source_target_pairs={{0,6},{1,7},{2,4},{3,5},{4,2},{5,3},{6,0},{7,1},{8,14},{9,15},{10,... | collective-permute-start | bytes 159752 | tf_op jit(solution)/shard_map/ppermute | solution.py:268
  75.2 2.1 %collective-permute-done.8 = f32[104,128]{1,0:T(8,128)S(1)} collective-permute-done((f32[104,128]{1,0:T(8,128)S(1)}, f32[104,128]{1,0:T(8,128)S(1)}, u32[]{:S(2)}, u32[]{:S(2)}) %collective-permute-start.8) | collective-permute-done | bytes 53280 | tf_op jit(solution)/shard_map/ppermute | solution.py:268
  77.4 0.9 collective-permute-start.9
  78.2 3.3 %collective-permute-done.9 = f32[104,128]{1,0:T(8,128)S(1)} collective-permute-done((f32[104,128]{1,0:T(8,128)S(1)}, f32[104,128]{1,0:T(8,128)S(1)}, u32[]{:S(2)}, u32[]{:S(2)}) %collective-permute-start.9) | collective-permute-done | bytes 53280 | tf_op jit(solution)/shard_map/ppermute | solution.py:268
  81.6 0.9 %collective-permute-start.10 = (f32[104,128]{1,0:T(8,128)S(1)}, f32[104,128]{1,0:T(8,128)S(1)}, u32[]{:S(2)}, u32[]{:S(2)}) collective-permute-start(f32[104,128]{1,0:T(8,128)S(1)} %add.30), channel_id=1, source_target_pairs={{0,72},{1,73},{2,74},{3,75},{4,76},{5,77},{6,78},{7,79},{8,64},{9,... | collective-permute-start | bytes 159752 | tf_op jit(solution)/shard_map/ppermute | solution.py:268
  82.5 4.5 %collective-permute-done.10 = f32[104,128]{1,0:T(8,128)S(1)} collective-permute-done((f32[104,128]{1,0:T(8,128)S(1)}, f32[104,128]{1,0:T(8,128)S(1)}, u32[]{:S(2)}, u32[]{:S(2)}) %collective-permute-start.10) | collective-permute-done | bytes 53280 | tf_op jit(solution)/shard_map/ppermute | solution.py:268
  (38 shorter events, 5.1 us)
Async XLA Ops:
  0.6 13.9 %copy-start = (f32[3,4,16,512]{3,2,1,0:T(8,128)S(1)}, f32[3,4,16,512]{3,2,1,0:T(8,128)}, u32[]{:S(2)}) copy-start(f32[3,4,16,512]{3,2,1,0:T(8,128)} %own.1) | copy-start | bytes 1179652
  0.6 13.8 %collective-permute-start = (f32[3,4,16,512]{3,2,1,0:T(8,128)}, f32[3,4,16,512]{3,2,1,0:T(8,128)S(1)}, u32[]{:S(2)}, u32[]{:S(2)}) collective-permute-start(f32[3,4,16,512]{3,2,1,0:T(8,128)} %own.1), channel_id=1, source_target_pairs={{0,16},{1,17},{2,18},{3,19},{4,20},{5,21},{6,22},{7,23},{8,24},{9,... | collective-permute-start | bytes 1179656 | tf_op jit(solution)/shard_map/ppermute | solution.py:275
  2.4 12.2 %collective-permute-start.1 = (f32[3,4,16,512]{3,2,1,0:T(8,128)}, f32[3,4,16,512]{3,2,1,0:T(8,128)S(1)}, u32[]{:S(2)}, u32[]{:S(2)}) collective-permute-start(f32[3,4,16,512]{3,2,1,0:T(8,128)} %own.1), channel_id=1, source_target_pairs={{0,112},{1,113},{2,114},{3,115},{4,116},{5,117},{6,118},{7,119},{8... | collective-permute-start | bytes 1179656 | tf_op jit(solution)/shard_map/ppermute | solution.py:276
  14.5 0.7 copy-start.1
  14.6 10.6 %copy-start.2 = (f32[3,4,16,512]{3,2,1,0:T(8,128)}, f32[3,4,16,512]{3,2,1,0:T(8,128)S(1)}, u32[]{:S(2)}) copy-start(f32[3,4,16,512]{3,2,1,0:T(8,128)S(1)} %collective-permute-done.1.x_high) | copy-start | bytes 1179652
  15.4 9.8 %collective-permute-start.2 = (f32[3,12,4,512]{3,2,1,0:T(4,128)S(1)}, f32[3,12,4,512]{3,2,1,0:T(4,128)S(1)}, u32[]{:S(2)}, u32[]{:S(2)}) collective-permute-start(f32[3,12,4,512]{3,2,1,0:T(4,128)S(1)} %get-tuple-element.9), channel_id=1, source_target_pairs={{0,1},{1,2},{2,3},{3,4},{4,5},{5,6},{6,7},{7,8},{8,9},{9,10},{10,1... | collective-permute-start | bytes 884744 | tf_op jit(solution)/shard_map/ppermute | solution.py:278
  15.5 9.8 %collective-permute-start.3 = (f32[3,12,4,512]{3,2,1,0:T(4,128)S(1)}, f32[3,12,4,512]{3,2,1,0:T(4,128)S(1)}, u32[]{:S(2)}, u32[]{:S(2)}) collective-permute-start(f32[3,12,4,512]{3,2,1,0:T(4,128)S(1)} %get-tuple-element.8), channel_id=1, source_target_pairs={{0,15},{1,0},{2,1},{3,2},{4,3},{5,4},{6,5},{7,6},{8,7},{9,8},{10,9... | collective-permute-start | bytes 884744 | tf_op jit(solution)/shard_map/ppermute | solution.py:279
  25.2 0.7 copy-start.3
  25.2 0.8 copy-start.4
  53.2 1.4 %collective-permute-start.4 = (f32[104,128]{1,0:T(8,128)}, f32[104,128]{1,0:T(8,128)S(1)}, u32[]{:S(2)}, u32[]{:S(2)}) collective-permute-start(f32[104,128]{1,0:T(8,128)} %get-tuple-element.7), channel_id=1, source_target_pairs={{0,1},{1,0},{2,3},{3,2},{4,5},{5,4},{6,7},{7,6},{8,9},{9,8},{10,11... | collective-permute-start | bytes 159752 | tf_op jit(solution)/shard_map/ppermute | solution.py:268
  55.4 4.1 %collective-permute-start.5 = (f32[104,128]{1,0:T(8,128)S(1)}, f32[104,128]{1,0:T(8,128)S(1)}, u32[]{:S(2)}, u32[]{:S(2)}) collective-permute-start(f32[104,128]{1,0:T(8,128)S(1)} %add.25), channel_id=1, source_target_pairs={{0,16},{1,17},{2,18},{3,19},{4,20},{5,21},{6,22},{7,23},{8,24},{9,... | collective-permute-start | bytes 159752 | tf_op jit(solution)/shard_map/ppermute | solution.py:268
  59.6 5.4 %collective-permute-start.6 = (f32[104,128]{1,0:T(8,128)S(1)}, f32[104,128]{1,0:T(8,128)S(1)}, u32[]{:S(2)}, u32[]{:S(2)}) collective-permute-start(f32[104,128]{1,0:T(8,128)S(1)} %add.26), channel_id=1, source_target_pairs={{0,48},{1,49},{2,50},{3,51},{4,52},{5,53},{6,54},{7,55},{8,56},{9,... | collective-permute-start | bytes 159752 | tf_op jit(solution)/shard_map/ppermute | solution.py:268
  65.0 4.2 %collective-permute-start.7 = (f32[104,128]{1,0:T(8,128)S(1)}, f32[104,128]{1,0:T(8,128)S(1)}, u32[]{:S(2)}, u32[]{:S(2)}) collective-permute-start(f32[104,128]{1,0:T(8,128)S(1)} %add.27), channel_id=1, source_target_pairs={{0,2},{1,3},{2,0},{3,1},{4,6},{5,7},{6,4},{7,5},{8,10},{9,11},{10,... | collective-permute-start | bytes 159752 | tf_op jit(solution)/shard_map/ppermute | solution.py:268
  69.2 8.1 %collective-permute-start.8 = (f32[104,128]{1,0:T(8,128)S(1)}, f32[104,128]{1,0:T(8,128)S(1)}, u32[]{:S(2)}, u32[]{:S(2)}) collective-permute-start(f32[104,128]{1,0:T(8,128)S(1)} %add.28), channel_id=1, source_target_pairs={{0,6},{1,7},{2,4},{3,5},{4,2},{5,3},{6,0},{7,1},{8,14},{9,15},{10,... | collective-permute-start | bytes 159752 | tf_op jit(solution)/shard_map/ppermute | solution.py:268
  77.4 4.2 %collective-permute-start.9 = (f32[104,128]{1,0:T(8,128)S(1)}, f32[104,128]{1,0:T(8,128)S(1)}, u32[]{:S(2)}, u32[]{:S(2)}) collective-permute-start(f32[104,128]{1,0:T(8,128)S(1)} %add.29), channel_id=1, source_target_pairs={{0,64},{1,65},{2,66},{3,67},{4,68},{5,69},{6,70},{7,71},{8,72},{9,... | collective-permute-start | bytes 159752 | tf_op jit(solution)/shard_map/ppermute | solution.py:268
  81.6 5.4 %collective-permute-start.10 = (f32[104,128]{1,0:T(8,128)S(1)}, f32[104,128]{1,0:T(8,128)S(1)}, u32[]{:S(2)}, u32[]{:S(2)}) collective-permute-start(f32[104,128]{1,0:T(8,128)S(1)} %add.30), channel_id=1, source_target_pairs={{0,72},{1,73},{2,74},{3,75},{4,76},{5,77},{6,78},{7,79},{8,64},{9,... | collective-permute-start | bytes 159752 | tf_op jit(solution)/shard_map/ppermute | solution.py:268
where the time goes:
time: 89.7 us; the launch traced here: 88.9 us
  waiting for transfers between devices  29.6 us (33%)
  Pallas kernels  27.1 us (30%)
  starting transfers between devices  21.1 us (24%)
  local copies, waits for them, and re-layouts  6.87 us (8%)
  other arithmetic  3.41 us (4%)
    pallas_call x1, Pallas kernels, run_kernel(): pl.pallas_call(kernel, in_specs=[smem] + [vmem] * 13, out_specs=[vmem] *...  27.1 us
    ppermute x7, waiting for transfers between devices, sum_everywhere(): value = value + lax.ppermute(value, AXES, pairs(move))  21.9 us
    ppermute x7, starting transfers between devices, sum_everywhere(): value = value + lax.ppermute(value, AXES, pairs(move))  11.1 us
    ppermute x1, starting transfers between devices, body(): lax.ppermute(wide[:, :, :4, :], AXES, pairs(lambda i, j: (i, j - 1)))  5.35 us
    ppermute x1, waiting for transfers between devices, body(): x_low = lax.ppermute(velocity, AXES, up)  4.65 us
    unnamed x16, local copies, waits for them, and re-layouts  4 us
    ppermute x1, waiting for transfers between devices, body(): lax.ppermute(wide[:, :, 12:, :], AXES, pairs(lambda i, j: (i, j + 1)))  3.11 us
    ppermute x1, starting transfers between devices, body(): x_high = lax.ppermute(velocity, AXES, down)  2.87 us
  transfers between devices with their start and end apart: 11, of which 9 were waited for; matrix products, arithmetic and copies ran while one was open for 7% of the time, Pallas kernels for 0%

commit v1 on v0

v1 whole, which is shorter than its diff:
```python
import jax
import jax.numpy as jnp
import numpy as np
from jax import lax
from jax.experimental import pallas as pl
from jax.experimental.pallas import tpu as pltpu
from jax.sharding import PartitionSpec as P

f32, bf16 = jnp.float32, jnp.bfloat16
AXES = ("px", "py")
LANES = 640
ROWS = 40
NT = (((1,), (1,)), ((), ()))


def selections():
    pick = np.zeros((512, 216), np.float32)
    pick_target = np.zeros((256, 96), np.float32)
    for y in range(16):
        for c in range(3):
            for ox in range(3):
                for oy in range(3):
                    pick[y * 32 + c * 9 + ox * 3 + oy, (c * 3 + ox) * 24 + y + oy + 3] = 1
        for c in range(6):
            pick_target[y * 16 + c, c * 16 + y] = 1
    order = np.zeros((81, 96), np.float32)
    for oz in range(3):
        for c in range(3):
            for o in range(9):
                order[c * 27 + o * 3 + oz, oz * 32 + c * 9 + o] = 1
    return pick, pick_target, order


def dot(a, b):
    return jnp.dot(a, b, preferred_element_type=f32)


def dot_cells(a, b):
    return lax.dot_general(a, b, NT, preferred_element_type=f32)


def shift_z(value):
    return pltpu.roll(value, LANES - 1, 1) - pltpu.roll(value, 1, 1)


def differences(field, plane, row):
    here = pl.ds(row, 8)
    center = [field[c, plane, here, :] for c in range(3)]
    along_x = [field[c, plane + 1, here, :] - field[c, plane - 1, here, :] for c in range(3)]
    along_y = [field[c, plane, pl.ds(row + 1, 8), :] - field[c, plane, pl.ds(row - 1, 8), :] for c in range(3)]
    along_z = [shift_z(center[c]) for c in range(3)]
    return center, (along_x, along_y, along_z)


def stress_rows(field, plane, tau, tau_plane, row):
    _, d = differences(field, plane, row)
    xy, xz, yz = d[0][1] + d[1][0], d[0][2] + d[2][0], d[1][2] + d[2][1]
    diagonal = d[0][0] * d[0][0] + d[1][1] * d[1][1] + d[2][2] * d[2][2]
    mixed = xy * xy + xz * xz + yz * yz
    nu = 0.05 + 0.04 * jnp.sqrt(0.5 * diagonal + 0.25 * mixed)
    half = -0.5 * nu
    rows = pl.ds(row, 8)
    for c in range(3):
        tau[c, tau_plane, rows, :] = -nu * d[c][c]
    tau[3, tau_plane, rows, :] = half * xy
    tau[4, tau_plane, rows, :] = half * xz
    tau[5, tau_plane, rows, :] = half * yz


def step_rows(field, plane, tau, tau_plane, row):
    center, d = differences(field, plane, row)
    here = pl.ds(row, 8)

    def tau_x(c):
        return tau[c, tau_plane + 1, here, :] - tau[c, tau_plane - 1, here, :]

    def tau_y(c):
        return tau[c, tau_plane, pl.ds(row + 1, 8), :] - tau[c, tau_plane, pl.ds(row - 1, 8), :]

    def tau_z(c):
        return shift_z(tau[c, tau_plane, here, :])

    parts = ((0, 3, 4), (3, 1, 5), (4, 5, 2))
    out = []
    for j in range(3):
        a, b, c = parts[j]
        total = tau_x(a) + tau_y(b) + tau_z(c)
        total += center[0] * d[0][j] + center[1] * d[1][j] + center[2] * d[2][j]
        new = center[j] - 0.05 * total
        out.append(new + 0.005 if j == 0 else new)
    return out


def add_columns(tile, tile_target, starts, weights, totals):
    w1, w2, w2t, w3, w3t = weights
    g1, g2, g3 = totals
    columns, targets = [], []
    for n, first in enumerate(starts):
        start = first + 127
        base_lane = pl.multiple_of(lax.shift_right_logical(start, 7) * 128, 128)
        turn = (512 - (start & 127)) & 511
        window = pltpu.roll(tile[n * 32 : n * 32 + 32, pl.ds(base_lane, 512)], turn, 1)
        columns.append(jnp.concatenate([window[:, 0:256], window[:, 1:257], window[:, 2:258]], 0))
        target = pltpu.roll(tile_target[n * 16 : n * 16 + 16, pl.ds(base_lane, 512)], turn, 1)
        targets.append(target[:, 1:257])
    cols = jnp.concatenate(columns, 1)
    target = jnp.concatenate(targets, 1)
    h1 = dot(w1[...], cols)
    t1 = jnp.tanh(h1)
    q1 = h1 * t1
    a1 = (h1 + q1).astype(bf16)
    s1 = (1.0 + t1) * (1.0 + (h1 - q1))
    h2 = dot(w2[...], a1)
    t2 = jnp.tanh(h2)
    q2 = h2 * t2
    a2 = (h2 + q2).astype(bf16)
    s2 = (1.0 + t2) * (1.0 + (h2 - q2))
    misfit = dot(w3[...], jnp.concatenate([a2, target], 0)).astype(bf16)
    b2 = (dot(w3t[...], misfit) * s2).astype(bf16)
    b1 = (dot(w2t[...], b2) * s1).astype(bf16)
    g3[...] += dot_cells(misfit, a2)
    g2[...] += dot_cells(b2, a1)
    g1[...] += dot_cells(b1, cols)


def input_rows(field, plane):
    rows = [field[c, plane + ox - 1, 8:32, 0:512] for c in range(3) for ox in range(3)]
    return jnp.concatenate(rows, 0).astype(bf16)


def target_rows(tau, plane):
    return jnp.concatenate([tau[c, plane, 12:28, 0:512].astype(bf16) for c in range(6)], 0)


def gather(tile, at, table, rows):
    tile[at : at + table.shape[0], 128:640] = dot(table, rows).astype(bf16)


def clear_edges(*tiles):
    for tile in tiles:
        edge = jnp.zeros((tile.shape[0], 128), bf16)
        tile[:, 0:128] = edge
        tile[:, 640:768] = edge


def clear_rest(field):
    beyond = jnp.zeros((ROWS, 128), f32)
    strip = jnp.zeros((8, LANES), f32)
    for c in range(3):
        for p in range(field.shape[1]):
            field[c, p, :, 512:640] = beyond
            field[c, p, 4:12, :] = strip
            field[c, p, 28:36, :] = strip


def interior_kernel(
    offs, own, first, mid, last, pick, pick_target, order,
    w1, w2, w2t, w3, w3t, g1, g2, g3, field, tau, tile, tile_target,
):
    rows, cols = lax.broadcasted_iota(jnp.int32, (64, 64), 0), lax.broadcasted_iota(jnp.int32, (64, 64), 1)
    half = jnp.where(rows == cols, 0.5, 0.0).astype(bf16)
    w1[...] = (0.5 * dot(first[...], order[...])).astype(bf16)
    w2[...] = (0.5 * mid[...].astype(f32)).astype(bf16)
    w2t[...] = dot_cells(half, mid[...]).astype(bf16)
    rows, cols = lax.broadcasted_iota(jnp.int32, (16, 16), 0), lax.broadcasted_iota(jnp.int32, (16, 16), 1)
    minus = jnp.where(rows == cols, -1.0, 0.0)
    last_rows = jnp.concatenate([last[...].astype(f32), jnp.zeros((10, 64), f32)], 0)
    w3[...] = jnp.concatenate([last_rows, minus], 1).astype(bf16)
    w3t[...] = dot_cells(half, last_rows.astype(bf16)).astype(bf16)
    for total in (g1, g2, g3):
        total[...] = jnp.zeros_like(total)
    clear_edges(tile, tile_target)
    clear_rest(field)
    for c in range(3):
        for p in range(4):
            field[c, p, 12:28, 0:512] = own[c, p]

    def step(n, _):
        x = n + 1
        for row in (12, 20):
            stress_rows(field, x, tau, n, row)
        gather(tile, 0, pick[...], input_rows(field, x))
        gather(tile_target, 0, pick_target[...], target_rows(tau, n))
        starts = [offs[x, y] for y in range(1, 15)]
        add_columns(tile.at[32:480], tile_target.at[16:240], starts, (w1, w2, w2t, w3, w3t), (g1, g2, g3))
        return 0

    lax.fori_loop(0, 2, step, 0)


def rim_kernel(
    offs, own, x_low, x_high, y_low, y_high, w1, w2, w2t, w3, w3t, h1, h2, h3, pick, pick_target,
    g1, g2, g3, field, tau, tile, tile_target,
):
    g1[...] = h1[...]
    g2[...] = h2[...]
    g3[...] = h3[...]
    clear_edges(tile, tile_target)
    clear_rest(field)
    for c in range(3):
        for p in range(6):
            source, q = (x_low, 0) if p == 0 else (x_high, 0) if p == 5 else (own, p - 1)
            field[c, p, 12:28, 0:512] = source[c, q]
            field[c, p, 11:12, 0:512] = y_low[c, p]
            field[c, p, 28:29, 0:512] = y_high[c, p]

    def stress(p, _):
        for row in (12, 20):
            stress_rows(field, p + 1, tau, p, row)
        return 0

    lax.fori_loop(0, 4, stress, 0)

    def step(n, _):
        x, inner = 3 * n, 1 + n
        gather(tile, 0, pick[...], input_rows(field, x + 1))
        gather(tile_target, 0, pick_target[...], target_rows(tau, x))
        rows = input_rows(field, inner + 1)
        gather(tile, 512, pick[0:32, :], rows)
        gather(tile, 544, pick[480:512, :], rows)
        rows = target_rows(tau, inner)
        gather(tile_target, 256, pick_target[0:16, :], rows)
        gather(tile_target, 272, pick_target[240:256, :], rows)
        starts = [offs[x, y] for y in range(16)] + [offs[inner, 0], offs[inner, 15]]
        add_columns(tile, tile_target, starts, (w1, w2, w2t, w3, w3t), (g1, g2, g3))
        return 0

    lax.fori_loop(0, 2, step, 0)


def middle_kernel(
    offs, own, x_low, x_high, y_low, y_high, far_x_low, far_x_high, far_y_low, far_y_high,
    w1, w2, w2t, w3, w3t, h1, h2, h3, pick, pick_target, order,
    middle, packed, field, tau, tile, tile_target, g1, g2, g3,
):
    g1[...] = h1[...]
    g2[...] = h2[...]
    g3[...] = h3[...]
    clear_edges(tile, tile_target)
    clear_rest(field)
    line = jnp.zeros((1, LANES), f32)
    for c in range(6):
        for p in range(10):
            tau[c, p, 7:8, :] = line
            tau[c, p, 32:33, :] = line
    for c in range(3):
        for p in range(12):
            if p < 3:
                center = far_x_low[c, p].astype(f32)
            elif p > 8:
                center = far_x_high[c, p - 8].astype(f32)
            else:
                source, q = (x_low, 0) if p == 3 else (x_high, 0) if p == 8 else (own, p - 4)
                center = source[c, q]
            field[c, p, 12:28, 0:512] = center
            field[c, p, 8:12, 0:512] = far_y_low[c, p].astype(f32)
            field[c, p, 28:32, 0:512] = far_y_high[c, p].astype(f32)
            if 3 <= p <= 8:
                field[c, p, 11:12, 0:512] = y_low[c, p - 3]
                field[c, p, 28:29, 0:512] = y_high[c, p - 3]

    def stress_zero(p, _):
        for row in (8, 16, 24):
            stress_rows(field, p + 1, tau, p, row)
        return 0

    lax.fori_loop(0, 10, stress_zero, 0)
    inside = lax.broadcasted_iota(jnp.int32, (8, LANES), 1) < 512

    def advance_middle(p, _):
        for row in (8, 16, 24):
            new = step_rows(field, p + 2, tau, p + 1, row)
            for c in range(3):
                middle[c, p, pl.ds(row, 8), :] = jnp.where(inside, new[c], 0.0)
        return 0

    lax.fori_loop(0, 8, advance_middle, 0)

    def step(x, _):
        for row in (12, 20):
            stress_rows(middle, x + 2, tau, 0, row)
        gather(tile, 0, pick[...], input_rows(middle, x + 2))
        gather(tile_target, 0, pick_target[...], target_rows(tau, 0))
        starts = [offs[x, y] for y in range(16)]
        add_columns(tile, tile_target, starts, (w1, w2, w2t, w3, w3t), (g1, g2, g3))
        return 0

    lax.fori_loop(0, 4, step, 0)
    scale = 0.5**22
    ordered = lax.dot_general(
        g1[...], order[...].astype(f32), NT, preferred_element_type=f32, precision=lax.Precision.HIGHEST
    )
    mids = g2[...]
    packed[0:64, :] = scale * jnp.concatenate([ordered, jnp.zeros((64, 15), f32), mids[:, 0:32]], 1)
    packed[64:80, :] = scale * jnp.concatenate([mids[16 * k : 16 * k + 16, 32:64] for k in range(4)], 1)
    packed[80:88, :] = scale * jnp.concatenate([g3[0:8, :], jnp.zeros((8, 64), f32)], 1)


def final_kernel(middle, final, tau):
    def stress_one(p, _):
        for row in (8, 16, 24):
            stress_rows(middle, p + 1, tau, p, row)
        return 0

    lax.fori_loop(0, 6, stress_one, 0)

    def advance_final(p, _):
        for row in (12, 20):
            new = step_rows(middle, p + 2, tau, p + 1, row)
            for c in range(3):
                final[c, p, row - 12 : row - 4, :] = new[c][:, 0:512]
        return 0

    lax.fori_loop(0, 4, advance_final, 0)


def last_sum_kernel(a, b, c, d, first, mid, last):
    total = (a[...] + b[...]) + (c[...] + d[...])
    first[...] = total[0:64, 0:81]
    rest = jnp.concatenate([total[64:80, 32 * k : 32 * k + 32] for k in range(4)], 0)
    mid[...] = jnp.concatenate([total[0:64, 96:128], rest], 1)
    last[...] = total[80:86, 0:64]


def shaped(*dims, kind=f32):
    return jax.ShapeDtypeStruct(dims, kind)


WEIGHTS = [shaped(64, 96, kind=bf16), shaped(64, 64, kind=bf16), shaped(64, 64, kind=bf16),
           shaped(16, 80, kind=bf16), shaped(64, 16, kind=bf16)]
TOTALS = [shaped(64, 96), shaped(64, 64), shaped(16, 64)]


def call(kernel, args, out_shape, scratch, smem=0):
    vmem = pl.BlockSpec(memory_space=pltpu.VMEM)
    scalar = pl.BlockSpec(memory_space=pltpu.SMEM)
    return pl.pallas_call(
        kernel,
        in_specs=[scalar] * smem + [vmem] * (len(args) - smem),
        out_specs=[vmem] * len(out_shape),
        out_shape=out_shape,
        scratch_shapes=scratch,
        compiler_params=pltpu.CompilerParams(vmem_limit_bytes=48 * 2**20),
    )(*args)


def columns_scratch(planes, stress_planes, columns):
    return [
        pltpu.VMEM((3, planes, ROWS, LANES), f32),
        pltpu.VMEM((6, stress_planes, ROWS, LANES), f32),
        pltpu.VMEM((32 * columns, 768), bf16),
        pltpu.VMEM((16 * columns, 768), bf16),
    ]


def pairs(move):
    return [(i * 16 + j, (move(i, j)[0] % 8) * 16 + move(i, j)[1] % 16) for i in range(8) for j in range(16)]


ROTATIONS = (lambda k: (k + 1) % 4, lambda k: (k - 1) % 4, lambda k: (k + 2) % 4)


def along_y(turn):
    return lambda i, j: (i & 4 | turn(i & 3), j)


def along_x(turn):
    return lambda i, j: (i, j & 9 | turn(j >> 1 & 3) << 1)


def along_z(turn):
    def move(i, j):
        z = turn((j >> 3) * 2 + (i >> 2))
        return ((z & 1) * 4 + (i & 3), (z >> 1) * 8 + (j & 7))

    return move


def send(value, move):
    return lax.ppermute(value, AXES, pairs(move))


def body(velocity, first_weight, mid_weight, last_weight, offsets):
    pick, pick_target, order = (jnp.asarray(table, bf16) for table in selections())
    up, down = lambda i, j: (i + 1, j), lambda i, j: (i - 1, j)
    right, left = lambda i, j: (i, j + 1), lambda i, j: (i, j - 1)
    x_low = send(velocity[:, 3:4], up)
    x_high = send(velocity[:, 0:1], down)
    coarse = velocity.astype(bf16)
    far_x_low = send(coarse, up)
    far_x_high = send(coarse, down)

    *weights, h1, h2, h3 = call(
        interior_kernel,
        (offsets, velocity, first_weight, mid_weight, last_weight, pick, pick_target, order),
        WEIGHTS + TOTALS, columns_scratch(4, 2, 16), 1,
    )

    near = jnp.concatenate([x_low, velocity, x_high], 1)
    y_low = send(near[:, :, 15:16, :], right)
    y_high = send(near[:, :, 0:1, :], left)
    wide = jnp.concatenate([far_x_low, coarse, far_x_high], 1)
    far_y_low = send(wide[:, :, 12:16, :], right)
    far_y_high = send(wide[:, :, 0:4, :], left)

    totals = call(
        rim_kernel,
        (offsets, velocity, x_low, x_high, y_low, y_high, *weights, h1, h2, h3, pick, pick_target),
        TOTALS, columns_scratch(6, 4, 18), 1,
    )
    middle, packed = call(
        middle_kernel,
        (offsets, velocity, x_low, x_high, y_low, y_high, far_x_low, far_x_high, far_y_low, far_y_high,
         *weights, *totals, pick, pick_target, order),
        [shaped(3, 8, ROWS, LANES), shaped(88, 128)],
        columns_scratch(12, 10, 16) + [pltpu.VMEM(t.shape, f32) for t in TOTALS], 1,
    )
    (final,) = call(final_kernel, (middle,), [shaped(3, 4, 16, 512)], [pltpu.VMEM((6, 6, ROWS, LANES), f32)])

    packed = packed + send(packed, lambda i, j: (i, j ^ 1))
    for along in (along_y, along_x):
        a, b, c = (send(packed, along(turn)) for turn in ROTATIONS)
        packed = (packed + a) + (b + c)
    a, b, c = (send(packed, along_z(turn)) for turn in ROTATIONS)
    grads = call(last_sum_kernel, (packed, a, b, c), [shaped(64, 81), shaped(64, 64), shaped(6, 64)], [])
    return final, *grads


def solution(mesh):
    in_specs = (P(None, "px", "py", None), P(), P(), P(), P("px", "py"))
    out_specs = (P(None, "px", "py", None), P(), P(), P())
    return jax.shard_map(body, mesh=mesh, in_specs=in_specs, out_specs=out_specs, check_vma=False)
```

time: 89.7 us -> 81.3 us (0.906)
  waiting for transfers between devices: 29.6 us -> 23 us
  local copies, waits for them, and re-layouts: 6.87 us -> 1.14 us
  starting transfers between devices: 21.1 us -> 24.5 us
  Pallas kernels: 27.1 us -> 30.3 us
  other arithmetic: 3.41 us -> 1.34 us
    ppermute x11 -> x18, waiting for transfers between devices: 29.6 us -> 23 us  [send(): return lax.ppermute(value, AXES, pairs(move))]
    unnamed x16 -> x17, local copies, waits for them, and re-layouts: 4 us -> 0.05 us
    ppermute x11 -> x18, starting transfers between devices: 21.1 us -> 24.5 us  [send(): return lax.ppermute(value, AXES, pairs(move))]
    pallas_call x1 -> x5, Pallas kernels: 27.1 us -> 30.3 us  [call(): pl.pallas_call(kernel, in_specs=[scalar] * smem + [vmem] * (len(args) - s...]
    mul x3 -> x0, other arithmetic: 1.24 us -> none  [the longest x1 0.62 us: body(): w2t = mid_weight.T * half]
    convert_element_type x0 -> x1, other arithmetic: none -> 1.18 us  [body(): coarse = velocity.astype(bf16)]
    concatenate x2 -> x1, other arithmetic: 1.29 us -> 0.12 us  [body(): wide = jnp.concatenate([far_x_low, coarse, far_x_high], 1)]
  transfers between devices with their start and end apart: 11 -> 18, of which waited for: 9 -> 10; matrix products, arithmetic and copies ran while one was open for 7% -> 2% of each run, Pallas kernels for 0% -> 18%
where the time goes in v1:
time: 81.3 us; the launch traced here: 81.1 us
  Pallas kernels  30.3 us (37%)
  starting transfers between devices  24.5 us (30%)
  waiting for transfers between devices  23 us (28%)
  other arithmetic  1.34 us (2%)
  local copies, waits for them, and re-layouts  1.14 us (1%)
  between operations  0.86 us (1%)
    pallas_call x5, Pallas kernels, call(): pl.pallas_call(kernel, in_specs=[scalar] * smem + [vmem] * (len(args) - s...  30.3 us
    ppermute x18, starting transfers between devices, send(): return lax.ppermute(value, AXES, pairs(move))  24.5 us
    ppermute x18, waiting for transfers between devices, send(): return lax.ppermute(value, AXES, pairs(move))  23 us
  transfers between devices with their start and end apart: 18, of which 10 were waited for; matrix products, arithmetic and copies ran while one was open for 2% of the time, Pallas kernels for 18%

profile of v1, /device:TPU:0, one launch (start us, length us, event | category | flops | bytes accessed | tf_op | source)
XLA Modules:
  0.0 81.1 jit_solution(758571805045059938)
XLA Ops:
  0.7 1.0 %fusion.2 = (f32[3,1,16,512]{3,2,1,0:T(8,128)S(1)}, f32[3,1,16,512]{3,2,1,0:T(8,128)S(1)}) fusion(f32[3,4,16,512]{3,2,1,0:T(8,128)} %own.5), kind=kLoop, calls=%fused_computation.10 | loop fusion | bytes 393216 | tf_op jit(solution)/shard_map/slice | solution.py:388
  1.8 1.7 %collective-permute-start = (f32[3,1,16,512]{3,2,1,0:T(8,128)S(1)}, f32[3,1,16,512]{3,2,1,0:T(8,128)S(1)}, u32[]{:S(2)}, u32[]{:S(2)}) collective-permute-start(f32[3,1,16,512]{3,2,1,0:T(8,128)S(1)} %get-tuple-element.43), channel_id=1, source_target_pairs={{0,16},{1,17},{2,18},{3,19},{4,20},{5,21},{6,22},{7,23},{8,24},{9,... | collective-permute-start | bytes 294920 | tf_op jit(solution)/shard_map/ppermute | solution.py:380
  3.5 2.9 %collective-permute-start.1 = (f32[3,1,16,512]{3,2,1,0:T(8,128)S(1)}, f32[3,1,16,512]{3,2,1,0:T(8,128)S(1)}, u32[]{:S(2)}, u32[]{:S(2)}) collective-permute-start(f32[3,1,16,512]{3,2,1,0:T(8,128)S(1)} %get-tuple-element.42), channel_id=1, source_target_pairs={{0,112},{1,113},{2,114},{3,115},{4,116},{5,117},{6,118},{7,119},{8... | collective-permute-start | bytes 294920 | tf_op jit(solution)/shard_map/ppermute | solution.py:380
  6.4 2.7 %collective-permute-done.x_low = f32[3,1,16,512]{3,2,1,0:T(8,128)S(1)} collective-permute-done((f32[3,1,16,512]{3,2,1,0:T(8,128)S(1)}, f32[3,1,16,512]{3,2,1,0:T(8,128)S(1)}, u32[]{:S(2)}, u32[]{:S(2)}) %collective-permute-start) | collective-permute-done | bytes 98336 | tf_op jit(solution)/shard_map/ppermute | solution.py:380
  9.1 1.2 %fusion.1 = (bf16[3,4,16,512]{3,2,1,0:T(8,128)(2,1)S(1)}, f32[3,6,16,512]{3,2,1,0:T(8,128)S(1)}) fusion(f32[3,4,16,512]{3,2,1,0:T(8,128)} %own.5, f32[3,6,16,512]{3,2,1,0:T(8,128)S(1)} %constant_dynamic-update-slice_fusion.2), kind=kLoop, calls=%fused_computation.9 | loop fusion | flops 98304 | bytes 983040 | tf_op jit(solution)/shard_map/convert_element_type | solution.py:389
  10.3 1.9 %collective-permute-start.5 = (bf16[3,4,16,512]{3,2,1,0:T(8,128)(2,1)S(1)}, bf16[3,4,16,512]{3,2,1,0:T(8,128)(2,1)S(1)}, u32[]{:S(2)}, u32[]{:S(2)}) collective-permute-start(bf16[3,4,16,512]{3,2,1,0:T(8,128)(2,1)S(1)} %get-tuple-element.40), channel_id=1, source_target_pairs={{0,112},{1,113},{2,114},{3,115},{4,116},{5,117},{6,118},{7,119},{8... | collective-permute-start | bytes 589832 | tf_op jit(solution)/shard_map/ppermute | solution.py:380
  12.4 4.0 %collective-permute-done.5.far_x_high = bf16[3,4,16,512]{3,2,1,0:T(8,128)(2,1)S(1)} collective-permute-done((bf16[3,4,16,512]{3,2,1,0:T(8,128)(2,1)S(1)}, bf16[3,4,16,512]{3,2,1,0:T(8,128)(2,1)S(1)}, u32[]{:S(2)}, u32[]{:S(2)}) %collective-permute-start.5) | collective-permute-done | bytes 196640 | tf_op jit(solution)/shard_map/ppermute | solution.py:380
  16.4 3.5 %collective-permute-done.4.far_x_low = bf16[3,4,16,512]{3,2,1,0:T(8,128)(2,1)S(1)} collective-permute-done((bf16[3,4,16,512]{3,2,1,0:T(8,128)(2,1)S(1)}, bf16[3,4,16,512]{3,2,1,0:T(8,128)(2,1)S(1)}, u32[]{:S(2)}, u32[]{:S(2)}) %collective-permute-start.4) | collective-permute-done | bytes 196640 | tf_op jit(solution)/shard_map/ppermute | solution.py:380
  20.1 2.7 %collective-permute-start.7 = (bf16[3,12,4,512]{3,2,1,0:T(4,128)(2,1)S(1)}, bf16[3,12,4,512]{3,2,1,0:T(4,128)(2,1)S(1)}, u32[]{:S(2)}, u32[]{:S(2)}) collective-permute-start(bf16[3,12,4,512]{3,2,1,0:T(4,128)(2,1)S(1)} %get-tuple-element.36), channel_id=1, source_target_pairs={{0,15},{1,0},{2,1},{3,2},{4,3},{5,4},{6,5},{7,6},{8,7},{9,8},{10,9... | collective-permute-start | bytes 442376 | tf_op jit(solution)/shard_map/ppermute | solution.py:380
  22.8 5.4 %collective-permute-start.3 = (f32[3,6,1,512]{3,2,1,0:T(1,128)S(1)}, f32[3,6,1,512]{3,2,1,0:T(1,128)S(1)}, u32[]{:S(2)}, u32[]{:S(2)}) collective-permute-start(f32[3,6,1,512]{3,2,1,0:T(1,128)S(1)} %get-tuple-element.38), channel_id=1, source_target_pairs={{0,15},{1,0},{2,1},{3,2},{4,3},{5,4},{6,5},{7,6},{8,7},{9,8},{10,9... | collective-permute-start | bytes 110600 | tf_op jit(solution)/shard_map/ppermute | solution.py:380
  28.3 4.9 %shard_map.111 = (bf16[64,96]{1,0:T(8,128)(2,1)S(1)}, bf16[64,64]{1,0:T(8,128)(2,1)S(1)}, bf16[64,64]{1,0:T(8,128)(2,1)S(1)}, bf16[16,80]{1,0:T(8,128)(2,1)S(1)}...) custom-call(s32[4,16]{1,0:T(4,128)S(1)} %copy-done.4, ...), custom_call_target="tpu_custom_call" | custom-call | tf_op jit(solution)/shard_map/pallas_call | solution.py:337
  33.3 2.0 %collective-permute-done.2.y_low = f32[3,6,1,512]{3,2,1,0:T(1,128)S(1)} collective-permute-done((f32[3,6,1,512]{3,2,1,0:T(1,128)S(1)}, f32[3,6,1,512]{3,2,1,0:T(1,128)S(1)}, u32[]{:S(2)}, u32[]{:S(2)}) %collective-permute-start.2) | collective-permute-done | bytes 36896 | tf_op jit(solution)/shard_map/ppermute | solution.py:380
  35.3 6.9 %shard_map.112 = (f32[64,96]{1,0:T(8,128)S(1)}, f32[64,64]{1,0:T(8,128)S(1)}, f32[16,64]{1,0:T(8,128)S(1)}) custom-call(s32[4,16]{1,0:T(4,128)S(1)} %copy-done.4, f32[3,4,16,512]{3,2,1,0:T(8,128)S(1)} %copy-done, f32[3,1,16,512]{3,2,1,0:T(8,128)S(1)} %collective-permute-done.x_low, f32[3,1,16,512]{3,2,1,0:T(8,128)S(1)} %collective-permute-done.1.x_high, ...), custom_call_target="tpu_custom_call" | custom-call | tf_op jit(solution)/shard_map/pallas_call | solution.py:337
  42.2 14.8 %shard_map.113 = (f32[3,8,40,640]{3,2,1,0:T(8,128)S(1)}, f32[88,128]{1,0:T(8,128)S(1)}) custom-call(s32[4,16]{1,0:T(4,128)S(1)} %copy-done.4, f32[3,4,16,512]{3,2,1,0:T(8,128)S(1)} %copy-done, f32[3,1,16,512]{3,2,1,0:T(8,128)S(1)} %collective-permute-done.x_low, f32[3,1,16,512]{3,2,1,0:T(8,128)S(1)} %collective-permute-done.1.x_high, ...), custom_call_target="tpu_custom_call" | custom-call | tf_op jit(solution)/shard_map/pallas_call | solution.py:337
  57.1 1.2 %collective-permute-done.8 = f32[88,128]{1,0:T(8,128)S(1)} collective-permute-done((f32[88,128]{1,0:T(8,128)S(1)}, f32[88,128]{1,0:T(8,128)S(1)}, u32[]{:S(2)}, u32[]{:S(2)}) %collective-permute-start.8) | collective-permute-done | bytes 45088 | tf_op jit(solution)/shard_map/ppermute | solution.py:380
  58.6 1.6 %collective-permute-start.10 = (f32[88,128]{1,0:T(8,128)S(1)}, f32[88,128]{1,0:T(8,128)S(1)}, u32[]{:S(2)}, u32[]{:S(2)}) collective-permute-start(f32[88,128]{1,0:T(8,128)S(1)} %add.21), channel_id=1, source_target_pairs={{0,48},{1,49},{2,50},{3,51},{4,52},{5,53},{6,54},{7,55},{8,56},{9,... | collective-permute-start | bytes 135176 | tf_op jit(solution)/shard_map/ppermute | solution.py:380
  60.7 3.5 %collective-permute-done.11 = f32[88,128]{1,0:T(8,128)S(1)} collective-permute-done((f32[88,128]{1,0:T(8,128)S(1)}, f32[88,128]{1,0:T(8,128)S(1)}, u32[]{:S(2)}, u32[]{:S(2)}) %collective-permute-start.11) | collective-permute-done | bytes 45088 | tf_op jit(solution)/shard_map/ppermute | solution.py:380
  64.2 1.2 %collective-permute-done.9 = f32[88,128]{1,0:T(8,128)S(1)} collective-permute-done((f32[88,128]{1,0:T(8,128)S(1)}, f32[88,128]{1,0:T(8,128)S(1)}, u32[]{:S(2)}, u32[]{:S(2)}) %collective-permute-start.9) | collective-permute-done | bytes 45088 | tf_op jit(solution)/shard_map/ppermute | solution.py:380
  65.5 1.1 %collective-permute-start.13 = (f32[88,128]{1,0:T(8,128)S(1)}, f32[88,128]{1,0:T(8,128)S(1)}, u32[]{:S(2)}, u32[]{:S(2)}) collective-permute-start(f32[88,128]{1,0:T(8,128)S(1)} %add_add_fusion.1), channel_id=1, source_target_pairs={{0,6},{1,7},{2,0},{3,1},{4,2},{5,3},{6,4},{7,5},{8,14},{9,15},{10,... | collective-permute-start | bytes 135176 | tf_op jit(solution)/shard_map/ppermute | solution.py:380
  66.6 1.0 %collective-permute-start.12 = (f32[88,128]{1,0:T(8,128)S(1)}, f32[88,128]{1,0:T(8,128)S(1)}, u32[]{:S(2)}, u32[]{:S(2)}) collective-permute-start(f32[88,128]{1,0:T(8,128)S(1)} %add_add_fusion.1), channel_id=1, source_target_pairs={{0,2},{1,3},{2,4},{3,5},{4,6},{5,7},{6,0},{7,1},{8,10},{9,11},{10,... | collective-permute-start | bytes 135176 | tf_op jit(solution)/shard_map/ppermute | solution.py:380
  67.6 3.5 %collective-permute-done.14 = f32[88,128]{1,0:T(8,128)S(1)} collective-permute-done((f32[88,128]{1,0:T(8,128)S(1)}, f32[88,128]{1,0:T(8,128)S(1)}, u32[]{:S(2)}, u32[]{:S(2)}) %collective-permute-start.14) | collective-permute-done | bytes 45088 | tf_op jit(solution)/shard_map/ppermute | solution.py:380
  71.9 3.0 %collective-permute-start.17 = (f32[88,128]{1,0:T(8,128)S(1)}, f32[88,128]{1,0:T(8,128)S(1)}, u32[]{:S(2)}, u32[]{:S(2)}) collective-permute-start(f32[88,128]{1,0:T(8,128)S(1)} %add_add_fusion.a), channel_id=1, source_target_pairs={{0,8},{1,9},{2,10},{3,11},{4,12},{5,13},{6,14},{7,15},{8,0},{9,1},... | collective-permute-start | bytes 135176 | tf_op jit(solution)/shard_map/ppermute | solution.py:380
  75.1 1.8 %collective-permute-start.15 = (f32[88,128]{1,0:T(8,128)S(1)}, f32[88,128]{1,0:T(8,128)S(1)}, u32[]{:S(2)}, u32[]{:S(2)}) collective-permute-start(f32[88,128]{1,0:T(8,128)S(1)} %add_add_fusion.a), channel_id=1, source_target_pairs={{0,64},{1,65},{2,66},{3,67},{4,68},{5,69},{6,70},{7,71},{8,72},{9,... | collective-permute-start | bytes 135176 | tf_op jit(solution)/shard_map/ppermute | solution.py:380
  76.9 2.9 %shard_map.114 = f32[3,4,16,512]{3,2,1,0:T(8,128)} custom-call(f32[3,8,40,640]{3,2,1,0:T(8,128)S(1)} %get-tuple-element.31.middle), custom_call_target="tpu_custom_call" | custom-call | tf_op jit(solution)/shard_map/pallas_call | solution.py:337
  (42 shorter events, 3.6 us)
Async XLA Ops:
  0.6 27.6 %copy-start.2 = (bf16[256,96]{1,0:T(8,128)(2,1)S(1)}, bf16[256,96]{1,0:T(8,128)(2,1)}, u32[]{:S(2)}) copy-start(bf16[256,96]{1,0:T(8,128)(2,1)} %constant.7.clone.pick_target) | copy-start | bytes 147460
  0.6 27.6 %copy-start.1 = (bf16[512,216]{1,0:T(8,128)(2,1)S(1)}, bf16[512,216]{1,0:T(8,128)(2,1)}, u32[]{:S(2)}) copy-start(bf16[512,216]{1,0:T(8,128)(2,1)} %constant.6.clone.pick) | copy-start | bytes 663556
  0.7 27.6 %copy-start.3 = (bf16[81,96]{1,0:T(8,128)(2,1)S(1)}, bf16[81,96]{1,0:T(8,128)(2,1)}, u32[]{:S(2)}) copy-start(bf16[81,96]{1,0:T(8,128)(2,1)} %constant.8.clone.order) | copy-start | bytes 46660
  0.7 27.6 %copy-start = (f32[3,4,16,512]{3,2,1,0:T(8,128)S(1)}, f32[3,4,16,512]{3,2,1,0:T(8,128)}, u32[]{:S(2)}) copy-start(f32[3,4,16,512]{3,2,1,0:T(8,128)} %own.5) | copy-start | bytes 1179652
  0.7 27.6 %copy-start.4 = (s32[4,16]{1,0:T(4,128)S(1)}, s32[4,16]{1,0:T(4,128)}, u32[]{:S(2)}) copy-start(s32[4,16]{1,0:T(4,128)} %offs.5) | copy-start | bytes 772
  0.7 27.6 %copy-start.7 = (bf16[6,64]{1,0:T(8,128)(2,1)S(1)}, bf16[6,64]{1,0:T(8,128)(2,1)}, u32[]{:S(2)}) copy-start(bf16[6,64]{1,0:T(8,128)(2,1)} %last.1) | copy-start | bytes 2308
  1.8 7.3 %collective-permute-start = (f32[3,1,16,512]{3,2,1,0:T(8,128)S(1)}, f32[3,1,16,512]{3,2,1,0:T(8,128)S(1)}, u32[]{:S(2)}, u32[]{:S(2)}) collective-permute-start(f32[3,1,16,512]{3,2,1,0:T(8,128)S(1)} %get-tuple-element.43), channel_id=1, source_target_pairs={{0,16},{1,17},{2,18},{3,19},{4,20},{5,21},{6,22},{7,23},{8,24},{9,... | collective-permute-start | bytes 294920 | tf_op jit(solution)/shard_map/ppermute | solution.py:380
  3.5 8.9 %collective-permute-start.1 = (f32[3,1,16,512]{3,2,1,0:T(8,128)S(1)}, f32[3,1,16,512]{3,2,1,0:T(8,128)S(1)}, u32[]{:S(2)}, u32[]{:S(2)}) collective-permute-start(f32[3,1,16,512]{3,2,1,0:T(8,128)S(1)} %get-tuple-element.42), channel_id=1, source_target_pairs={{0,112},{1,113},{2,114},{3,115},{4,116},{5,117},{6,118},{7,119},{8... | collective-permute-start | bytes 294920 | tf_op jit(solution)/shard_map/ppermute | solution.py:380
  10.3 6.2 %collective-permute-start.5 = (bf16[3,4,16,512]{3,2,1,0:T(8,128)(2,1)S(1)}, bf16[3,4,16,512]{3,2,1,0:T(8,128)(2,1)S(1)}, u32[]{:S(2)}, u32[]{:S(2)}) collective-permute-start(bf16[3,4,16,512]{3,2,1,0:T(8,128)(2,1)S(1)} %get-tuple-element.40), channel_id=1, source_target_pairs={{0,112},{1,113},{2,114},{3,115},{4,116},{5,117},{6,118},{7,119},{8... | collective-permute-start | bytes 589832 | tf_op jit(solution)/shard_map/ppermute | solution.py:380
  12.2 7.8 %collective-permute-start.4 = (bf16[3,4,16,512]{3,2,1,0:T(8,128)(2,1)S(1)}, bf16[3,4,16,512]{3,2,1,0:T(8,128)(2,1)S(1)}, u32[]{:S(2)}, u32[]{:S(2)}) collective-permute-start(bf16[3,4,16,512]{3,2,1,0:T(8,128)(2,1)S(1)} %get-tuple-element.40), channel_id=1, source_target_pairs={{0,16},{1,17},{2,18},{3,19},{4,20},{5,21},{6,22},{7,23},{8,24},{9,... | collective-permute-start | bytes 589832 | tf_op jit(solution)/shard_map/ppermute | solution.py:380
  20.1 22.1 %collective-permute-start.7 = (bf16[3,12,4,512]{3,2,1,0:T(4,128)(2,1)S(1)}, bf16[3,12,4,512]{3,2,1,0:T(4,128)(2,1)S(1)}, u32[]{:S(2)}, u32[]{:S(2)}) collective-permute-start(bf16[3,12,4,512]{3,2,1,0:T(4,128)(2,1)S(1)} %get-tuple-element.36), channel_id=1, source_target_pairs={{0,15},{1,0},{2,1},{3,2},{4,3},{5,4},{6,5},{7,6},{8,7},{9,8},{10,9... | collective-permute-start | bytes 442376 | tf_op jit(solution)/shard_map/ppermute | solution.py:380
  22.8 19.4 %collective-permute-start.6 = (bf16[3,12,4,512]{3,2,1,0:T(4,128)(2,1)S(1)}, bf16[3,12,4,512]{3,2,1,0:T(4,128)(2,1)S(1)}, u32[]{:S(2)}, u32[]{:S(2)}) collective-permute-start(bf16[3,12,4,512]{3,2,1,0:T(4,128)(2,1)S(1)} %get-tuple-element.37), channel_id=1, source_target_pairs={{0,1},{1,2},{2,3},{3,4},{4,5},{5,6},{6,7},{7,8},{8,9},{9,10},{10,1... | collective-permute-start | bytes 442376 | tf_op jit(solution)/shard_map/ppermute | solution.py:380
  22.8 10.4 %collective-permute-start.3 = (f32[3,6,1,512]{3,2,1,0:T(1,128)S(1)}, f32[3,6,1,512]{3,2,1,0:T(1,128)S(1)}, u32[]{:S(2)}, u32[]{:S(2)}) collective-permute-start(f32[3,6,1,512]{3,2,1,0:T(1,128)S(1)} %get-tuple-element.38), channel_id=1, source_target_pairs={{0,15},{1,0},{2,1},{3,2},{4,3},{5,4},{6,5},{7,6},{8,7},{9,8},{10,9... | collective-permute-start | bytes 110600 | tf_op jit(solution)/shard_map/ppermute | solution.py:380
  28.3 7.0 %collective-permute-start.2 = (f32[3,6,1,512]{3,2,1,0:T(1,128)S(1)}, f32[3,6,1,512]{3,2,1,0:T(1,128)S(1)}, u32[]{:S(2)}, u32[]{:S(2)}) collective-permute-start(f32[3,6,1,512]{3,2,1,0:T(1,128)S(1)} %get-tuple-element.39), channel_id=1, source_target_pairs={{0,1},{1,2},{2,3},{3,4},{4,5},{5,6},{6,7},{7,8},{8,9},{9,10},{10,1... | collective-permute-start | bytes 110600 | tf_op jit(solution)/shard_map/ppermute | solution.py:380
  57.0 1.3 %collective-permute-start.8 = (f32[88,128]{1,0:T(8,128)S(1)}, f32[88,128]{1,0:T(8,128)S(1)}, u32[]{:S(2)}, u32[]{:S(2)}) collective-permute-start(f32[88,128]{1,0:T(8,128)S(1)} %get-tuple-element.32), channel_id=1, source_target_pairs={{0,1},{1,0},{2,3},{3,2},{4,5},{5,4},{6,7},{7,6},{8,9},{9,8},{10,11... | collective-permute-start | bytes 135176 | tf_op jit(solution)/shard_map/ppermute | solution.py:380
  58.3 5.9 %collective-permute-start.11 = (f32[88,128]{1,0:T(8,128)S(1)}, f32[88,128]{1,0:T(8,128)S(1)}, u32[]{:S(2)}, u32[]{:S(2)}) collective-permute-start(f32[88,128]{1,0:T(8,128)S(1)} %add.21), channel_id=1, source_target_pairs={{0,32},{1,33},{2,34},{3,35},{4,36},{5,37},{6,38},{7,39},{8,40},{9,... | collective-permute-start | bytes 135176 | tf_op jit(solution)/shard_map/ppermute | solution.py:380
  58.6 5.6 %collective-permute-start.10 = (f32[88,128]{1,0:T(8,128)S(1)}, f32[88,128]{1,0:T(8,128)S(1)}, u32[]{:S(2)}, u32[]{:S(2)}) collective-permute-start(f32[88,128]{1,0:T(8,128)S(1)} %add.21), channel_id=1, source_target_pairs={{0,48},{1,49},{2,50},{3,51},{4,52},{5,53},{6,54},{7,55},{8,56},{9,... | collective-permute-start | bytes 135176 | tf_op jit(solution)/shard_map/ppermute | solution.py:380
  60.2 5.3 %collective-permute-start.9 = (f32[88,128]{1,0:T(8,128)S(1)}, f32[88,128]{1,0:T(8,128)S(1)}, u32[]{:S(2)}, u32[]{:S(2)}) collective-permute-start(f32[88,128]{1,0:T(8,128)S(1)} %add.21), channel_id=1, source_target_pairs={{0,16},{1,17},{2,18},{3,19},{4,20},{5,21},{6,22},{7,23},{8,24},{9,... | collective-permute-start | bytes 135176 | tf_op jit(solution)/shard_map/ppermute | solution.py:380
  65.4 5.7 %collective-permute-start.14 = (f32[88,128]{1,0:T(8,128)S(1)}, f32[88,128]{1,0:T(8,128)S(1)}, u32[]{:S(2)}, u32[]{:S(2)}) collective-permute-start(f32[88,128]{1,0:T(8,128)S(1)} %add_add_fusion.1), channel_id=1, source_target_pairs={{0,4},{1,5},{2,6},{3,7},{4,0},{5,1},{6,2},{7,3},{8,12},{9,13},{10,... | collective-permute-start | bytes 135176 | tf_op jit(solution)/shard_map/ppermute | solution.py:380
  65.5 5.6 %collective-permute-start.13 = (f32[88,128]{1,0:T(8,128)S(1)}, f32[88,128]{1,0:T(8,128)S(1)}, u32[]{:S(2)}, u32[]{:S(2)}) collective-permute-start(f32[88,128]{1,0:T(8,128)S(1)} %add_add_fusion.1), channel_id=1, source_target_pairs={{0,6},{1,7},{2,0},{3,1},{4,2},{5,3},{6,4},{7,5},{8,14},{9,15},{10,... | collective-permute-start | bytes 135176 | tf_op jit(solution)/shard_map/ppermute | solution.py:380
  66.6 5.3 %collective-permute-start.12 = (f32[88,128]{1,0:T(8,128)S(1)}, f32[88,128]{1,0:T(8,128)S(1)}, u32[]{:S(2)}, u32[]{:S(2)}) collective-permute-start(f32[88,128]{1,0:T(8,128)S(1)} %add_add_fusion.1), channel_id=1, source_target_pairs={{0,2},{1,3},{2,4},{3,5},{4,6},{5,7},{6,0},{7,1},{8,10},{9,11},{10,... | collective-permute-start | bytes 135176 | tf_op jit(solution)/shard_map/ppermute | solution.py:380
  71.9 8.0 %collective-permute-start.17 = (f32[88,128]{1,0:T(8,128)S(1)}, f32[88,128]{1,0:T(8,128)S(1)}, u32[]{:S(2)}, u32[]{:S(2)}) collective-permute-start(f32[88,128]{1,0:T(8,128)S(1)} %add_add_fusion.a), channel_id=1, source_target_pairs={{0,8},{1,9},{2,10},{3,11},{4,12},{5,13},{6,14},{7,15},{8,0},{9,1},... | collective-permute-start | bytes 135176 | tf_op jit(solution)/shard_map/ppermute | solution.py:380
  74.9 5.0 %collective-permute-start.16 = (f32[88,128]{1,0:T(8,128)S(1)}, f32[88,128]{1,0:T(8,128)S(1)}, u32[]{:S(2)}, u32[]{:S(2)}) collective-permute-start(f32[88,128]{1,0:T(8,128)S(1)} %add_add_fusion.a), channel_id=1, source_target_pairs={{0,72},{1,73},{2,74},{3,75},{4,76},{5,77},{6,78},{7,79},{8,64},{9,... | collective-permute-start | bytes 135176 | tf_op jit(solution)/shard_map/ppermute | solution.py:380
  75.1 5.3 %collective-permute-start.15 = (f32[88,128]{1,0:T(8,128)S(1)}, f32[88,128]{1,0:T(8,128)S(1)}, u32[]{:S(2)}, u32[]{:S(2)}) collective-permute-start(f32[88,128]{1,0:T(8,128)S(1)} %add_add_fusion.a), channel_id=1, source_target_pairs={{0,64},{1,65},{2,66},{3,67},{4,68},{5,69},{6,70},{7,71},{8,72},{9,... | collective-permute-start | bytes 135176 | tf_op jit(solution)/shard_map/ppermute | solution.py:380
  (2 other events, 55.2 us)

commit v2 on v1

--- a/solution.py
+++ b/solution.py
@@ -188,8 +188,8 @@
     lax.fori_loop(0, 2, step, 0)
 
 
-def rim_kernel(
-    offs, own, x_low, x_high, y_low, y_high, w1, w2, w2t, w3, w3t, h1, h2, h3, pick, pick_target,
+def side_kernel(
+    offs, own, x_low, x_high, w1, w2, w2t, w3, w3t, h1, h2, h3, pick, pick_target,
     g1, g2, g3, field, tau, tile, tile_target,
 ):
     g1[...] = h1[...]
@@ -199,37 +199,24 @@
     clear_rest(field)
     for c in range(3):
         for p in range(6):
-            source, q = (x_low, 0) if p == 0 else (x_high, 0) if p == 5 else (own, p - 1)
+            source, q = (x_low, 3) if p == 0 else (x_high, 0) if p == 5 else (own, p - 1)
             field[c, p, 12:28, 0:512] = source[c, q]
-            field[c, p, 11:12, 0:512] = y_low[c, p]
-            field[c, p, 28:29, 0:512] = y_high[c, p]
-
-    def stress(p, _):
+
+    def step(n, _):
+        x = 3 * n
         for row in (12, 20):
-            stress_rows(field, p + 1, tau, p, row)
-        return 0
-
-    lax.fori_loop(0, 4, stress, 0)
-
-    def step(n, _):
-        x, inner = 3 * n, 1 + n
+            stress_rows(field, x + 1, tau, 0, row)
         gather(tile, 0, pick[...], input_rows(field, x + 1))
-        gather(tile_target, 0, pick_target[...], target_rows(tau, x))
-        rows = input_rows(field, inner + 1)
-        gather(tile, 512, pick[0:32, :], rows)
-        gather(tile, 544, pick[480:512, :], rows)
-        rows = target_rows(tau, inner)
-        gather(tile_target, 256, pick_target[0:16, :], rows)
-        gather(tile_target, 272, pick_target[240:256, :], rows)
-        starts = [offs[x, y] for y in range(16)] + [offs[inner, 0], offs[inner, 15]]
-        add_columns(tile, tile_target, starts, (w1, w2, w2t, w3, w3t), (g1, g2, g3))
+        gather(tile_target, 0, pick_target[...], target_rows(tau, 0))
+        starts = [offs[x, y] for y in range(1, 15)]
+        add_columns(tile.at[32:480], tile_target.at[16:240], starts, (w1, w2, w2t, w3, w3t), (g1, g2, g3))
         return 0
 
     lax.fori_loop(0, 2, step, 0)
 
 
 def middle_kernel(
-    offs, own, x_low, x_high, y_low, y_high, far_x_low, far_x_high, far_y_low, far_y_high,
+    offs, own, x_low, x_high, y_low, y_high,
     w1, w2, w2t, w3, w3t, h1, h2, h3, pick, pick_target, order,
     middle, packed, field, tau, tile, tile_target, g1, g2, g3,
 ):
@@ -245,19 +232,10 @@
             tau[c, p, 32:33, :] = line
     for c in range(3):
         for p in range(12):
-            if p < 3:
-                center = far_x_low[c, p].astype(f32)
-            elif p > 8:
-                center = far_x_high[c, p - 8].astype(f32)
-            else:
-                source, q = (x_low, 0) if p == 3 else (x_high, 0) if p == 8 else (own, p - 4)
-                center = source[c, q]
-            field[c, p, 12:28, 0:512] = center
-            field[c, p, 8:12, 0:512] = far_y_low[c, p].astype(f32)
-            field[c, p, 28:32, 0:512] = far_y_high[c, p].astype(f32)
-            if 3 <= p <= 8:
-                field[c, p, 11:12, 0:512] = y_low[c, p - 3]
-                field[c, p, 28:29, 0:512] = y_high[c, p - 3]
+            source, q = ((x_low, p), (own, p - 4), (x_high, p - 8))[p // 4]
+            field[c, p, 12:28, 0:512] = source[c, q]
+            field[c, p, 8:12, 0:512] = y_low[c, p]
+            field[c, p, 28:32, 0:512] = y_high[c, p]
 
     def stress_zero(p, _):
         for row in (8, 16, 24):
@@ -277,11 +255,17 @@
     lax.fori_loop(0, 8, advance_middle, 0)
 
     def step(x, _):
+        rows = input_rows(field, x + 4)
+        gather(tile, 512, pick[0:32, :], rows)
+        gather(tile, 544, pick[480:512, :], rows)
+        rows = target_rows(tau, x + 3)
+        gather(tile_target, 256, pick_target[0:16, :], rows)
+        gather(tile_target, 272, pick_target[240:256, :], rows)
         for row in (12, 20):
             stress_rows(middle, x + 2, tau, 0, row)
         gather(tile, 0, pick[...], input_rows(middle, x + 2))
         gather(tile_target, 0, pick_target[...], target_rows(tau, 0))
-        starts = [offs[x, y] for y in range(16)]
+        starts = [offs[x, y] for y in range(16)] + [offs[x, 0], offs[x, 15]]
         add_columns(tile, tile_target, starts, (w1, w2, w2t, w3, w3t), (g1, g2, g3))
         return 0
 
@@ -331,7 +315,7 @@
 TOTALS = [shaped(64, 96), shaped(64, 64), shaped(16, 64)]
 
 
-def call(kernel, args, out_shape, scratch, smem=0):
+def call(kernel, args, out_shape, scratch, smem=0, us=1, mib=48):
     vmem = pl.BlockSpec(memory_space=pltpu.VMEM)
     scalar = pl.BlockSpec(memory_space=pltpu.SMEM)
     return pl.pallas_call(
@@ -340,7 +324,8 @@
         out_specs=[vmem] * len(out_shape),
         out_shape=out_shape,
         scratch_shapes=scratch,
-        compiler_params=pltpu.CompilerParams(vmem_limit_bytes=48 * 2**20),
+        compiler_params=pltpu.CompilerParams(vmem_limit_bytes=mib * 2**20),
+        cost_estimate=pl.CostEstimate(flops=int(us * 1.15e9), bytes_accessed=int(us * 3.69e6), transcendentals=0),
     )(*args)
 
 
@@ -357,7 +342,7 @@
     return [(i * 16 + j, (move(i, j)[0] % 8) * 16 + move(i, j)[1] % 16) for i in range(8) for j in range(16)]
 
 
-ROTATIONS = (lambda k: (k + 1) % 4, lambda k: (k - 1) % 4, lambda k: (k + 2) % 4)
+EXCHANGES = (lambda k: k ^ 1, lambda k: k ^ 3, lambda k: k ^ 2)
 
 
 def along_y(turn):
@@ -384,44 +369,33 @@
     pick, pick_target, order = (jnp.asarray(table, bf16) for table in selections())
     up, down = lambda i, j: (i + 1, j), lambda i, j: (i - 1, j)
     right, left = lambda i, j: (i, j + 1), lambda i, j: (i, j - 1)
-    x_low = send(velocity[:, 3:4], up)
-    x_high = send(velocity[:, 0:1], down)
-    coarse = velocity.astype(bf16)
-    far_x_low = send(coarse, up)
-    far_x_high = send(coarse, down)
-
+    x_low, x_high = send(velocity, up), send(velocity, down)
     *weights, h1, h2, h3 = call(
         interior_kernel,
         (offsets, velocity, first_weight, mid_weight, last_weight, pick, pick_target, order),
-        WEIGHTS + TOTALS, columns_scratch(4, 2, 16), 1,
+        WEIGHTS + TOTALS, columns_scratch(4, 2, 16), 1, 6, 62,
     )
-
-    near = jnp.concatenate([x_low, velocity, x_high], 1)
-    y_low = send(near[:, :, 15:16, :], right)
-    y_high = send(near[:, :, 0:1, :], left)
-    wide = jnp.concatenate([far_x_low, coarse, far_x_high], 1)
-    far_y_low = send(wide[:, :, 12:16, :], right)
-    far_y_high = send(wide[:, :, 0:4, :], left)
-
+    x_low, x_high, h1 = lax.optimization_barrier((x_low, x_high, h1))
+    wide = jnp.concatenate([x_low, velocity, x_high], 1)
+    y_low, y_high = send(wide[:, :, 12:16, :], right), send(wide[:, :, 0:4, :], left)
     totals = call(
-        rim_kernel,
-        (offsets, velocity, x_low, x_high, y_low, y_high, *weights, h1, h2, h3, pick, pick_target),
-        TOTALS, columns_scratch(6, 4, 18), 1,
+        side_kernel,
+        (offsets, velocity, x_low, x_high, *weights, h1, h2, h3, pick, pick_target),
+        TOTALS, columns_scratch(6, 1, 16), 1, 6,
     )
     middle, packed = call(
         middle_kernel,
-        (offsets, velocity, x_low, x_high, y_low, y_high, far_x_low, far_x_high, far_y_low, far_y_high,
-         *weights, *totals, pick, pick_target, order),
+        (offsets, velocity, x_low, x_high, y_low, y_high, *weights, *totals, pick, pick_target, order),
         [shaped(3, 8, ROWS, LANES), shaped(88, 128)],
-        columns_scratch(12, 10, 16) + [pltpu.VMEM(t.shape, f32) for t in TOTALS], 1,
+        columns_scratch(12, 10, 18) + [pltpu.VMEM(t.shape, f32) for t in TOTALS], 1, 16,
     )
-    (final,) = call(final_kernel, (middle,), [shaped(3, 4, 16, 512)], [pltpu.VMEM((6, 6, ROWS, LANES), f32)])
+    (final,) = call(final_kernel, (middle,), [shaped(3, 4, 16, 512)], [pltpu.VMEM((6, 6, ROWS, LANES), f32)], 0, 3)
 
     packed = packed + send(packed, lambda i, j: (i, j ^ 1))
     for along in (along_y, along_x):
-        a, b, c = (send(packed, along(turn)) for turn in ROTATIONS)
+        a, b, c = (send(packed, along(turn)) for turn in EXCHANGES)
         packed = (packed + a) + (b + c)
-    a, b, c = (send(packed, along_z(turn)) for turn in ROTATIONS)
+    a, b, c = (send(packed, along_z(turn)) for turn in EXCHANGES)
     grads = call(last_sum_kernel, (packed, a, b, c), [shaped(64, 81), shaped(64, 64), shaped(6, 64)], [])
     return final, *grads
 

time: 81.3 us -> 69.3 us (0.85)
  waiting for transfers between devices: 23 us -> 17.4 us
  starting transfers between devices: 24.5 us -> 19.4 us
  other arithmetic: 1.34 us -> 0.03 us
  local copies, waits for them, and re-layouts: 1.14 us -> 0.29 us
    ppermute x18 -> x14, waiting for transfers between devices: 23 us -> 17.4 us  [send(): return lax.ppermute(value, AXES, pairs(move))]
    ppermute x18 -> x14, starting transfers between devices: 24.5 us -> 19.4 us  [send(): return lax.ppermute(value, AXES, pairs(move))]
    convert_element_type x1 -> x0, other arithmetic: 1.18 us -> none  [body(): coarse = velocity.astype(bf16)]
    slice x2 -> x1, local copies, waits for them, and re-layouts: 1.08 us -> 0.13 us  [body(): wide[:, :, 0:4, :]]
  transfers between devices with their start and end apart: 18 -> 14, of which waited for: 10 -> 8; matrix products, arithmetic and copies ran while one was open for 2% -> 0% of each run, Pallas kernels for 18% -> 20%
where the time goes in v2:
time: 69.3 us; the launch traced here: 69.1 us
  Pallas kernels  31 us (45%)
  starting transfers between devices  19.4 us (28%)
  waiting for transfers between devices  17.4 us (25%)
  between operations  0.93 us (1%)
    pallas_call x5, Pallas kernels, call(): pl.pallas_call(kernel, in_specs=[scalar] * smem + [vmem] * (len(args) - s...  31 us
    ppermute x14, starting transfers between devices, send(): return lax.ppermute(value, AXES, pairs(move))  19.4 us
    ppermute x14, waiting for transfers between devices, send(): return lax.ppermute(value, AXES, pairs(move))  17.4 us
  transfers between devices with their start and end apart: 14, of which 8 were waited for; matrix products, arithmetic and copies ran while one was open for 0% of the time, Pallas kernels for 20%

profile of v2, /device:TPU:0, one launch (start us, length us, event | category | flops | bytes accessed | tf_op | source)
XLA Modules:
  0.0 69.1 jit_solution(6464940640476417708)
XLA Ops:
  0.6 4.5 %collective-permute-start.1 = (f32[3,4,16,512]{3,2,1,0:T(8,128)}, f32[3,4,16,512]{3,2,1,0:T(8,128)S(1)}, u32[]{:S(2)}, u32[]{:S(2)}) collective-permute-start(f32[3,4,16,512]{3,2,1,0:T(8,128)} %own.5), channel_id=1, source_target_pairs={{0,112},{1,113},{2,114},{3,115},{4,116},{5,117},{6,118},{7,119},{8... | collective-permute-start | bytes 1179656 | tf_op jit(solution)/shard_map/ppermute | solution.py:365
  5.2 6.2 %shard_map.111 = (bf16[64,96]{1,0:T(8,128)(2,1)}, bf16[64,64]{1,0:T(8,128)(2,1)}, bf16[64,64]{1,0:T(8,128)(2,1)}, bf16[16,80]{1,0:T(8,128)(2,1)}, bf16[64,16]{1,...) custom-call(s32[4,16]{1,0:T(4,128)} %offs.5, f32[3,4,16,512]{3,2,1,0:T(8,128)} %own.5, ...), custom_call_target="tpu_custom_call" | custom-call | flops 6899999744 | bytes 22140000 | tf_op jit(solution)/shard_map/pallas_call | solution.py:321
  11.3 2.5 %collective-permute-done.1.x_high = f32[3,4,16,512]{3,2,1,0:T(8,128)S(1)} collective-permute-done((f32[3,4,16,512]{3,2,1,0:T(8,128)}, f32[3,4,16,512]{3,2,1,0:T(8,128)S(1)}, u32[]{:S(2)}, u32[]{:S(2)}) %collective-permute-start.1) | collective-permute-done | bytes 393248 | tf_op jit(solution)/shard_map/ppermute | solution.py:365
  13.9 4.2 %collective-permute-done.x_low = f32[3,4,16,512]{3,2,1,0:T(8,128)S(1)} collective-permute-done((f32[3,4,16,512]{3,2,1,0:T(8,128)}, f32[3,4,16,512]{3,2,1,0:T(8,128)S(1)}, u32[]{:S(2)}, u32[]{:S(2)}) %collective-permute-start) | collective-permute-done | bytes 393248 | tf_op jit(solution)/shard_map/ppermute | solution.py:365
  18.3 0.1 fusion
  18.4 4.1 %collective-permute-start.3 = (f32[3,12,4,512]{3,2,1,0:T(4,128)S(1)}, f32[3,12,4,512]{3,2,1,0:T(4,128)S(1)}, u32[]{:S(2)}, u32[]{:S(2)}) collective-permute-start(f32[3,12,4,512]{3,2,1,0:T(4,128)S(1)} %get-tuple-element.42), channel_id=1, source_target_pairs={{0,15},{1,0},{2,1},{3,2},{4,3},{5,4},{6,5},{7,6},{8,7},{9,8},{10,9... | collective-permute-start | bytes 884744 | tf_op jit(solution)/shard_map/ppermute | solution.py:365
  22.6 5.0 %shard_map.112 = (f32[64,96]{1,0:T(8,128)S(1)}, f32[64,64]{1,0:T(8,128)S(1)}, f32[16,64]{1,0:T(8,128)S(1)}) custom-call(s32[4,16]{1,0:T(4,128)S(1)} %copy-done.1, f32[3,4,16,512]{3,2,1,0:T(8,128)S(1)} %copy-done, f32[3,4,16,512]{3,2,1,0:T(8,128)S(1)} %collective-permute-done.x_low, f32[3,4,16,512]{3,2,1,0:T(8,128)S(1)} %collective-permute-done.1.x_high, ...), custom_call_target="tpu_custom_call" | custom-call | flops 6899999744 | bytes 22140000 | tf_op jit(solution)/shard_map/pallas_call | solution.py:321
  27.7 4.6 %collective-permute-done.2.y_low = f32[3,12,4,512]{3,2,1,0:T(4,128)S(1)} collective-permute-done((f32[3,12,4,512]{3,2,1,0:T(4,128)S(1)}, f32[3,12,4,512]{3,2,1,0:T(4,128)S(1)}, u32[]{:S(2)}, u32[]{:S(2)}) %collective-permute-start.2) | collective-permute-done | bytes 294944 | tf_op jit(solution)/shard_map/ppermute | solution.py:365
  32.3 16.1 %shard_map.113 = (f32[3,8,40,640]{3,2,1,0:T(8,128)S(1)}, f32[88,128]{1,0:T(8,128)S(1)}) custom-call(s32[4,16]{1,0:T(4,128)S(1)} %copy-done.1, f32[3,4,16,512]{3,2,1,0:T(8,128)S(1)} %copy-done, f32[3,4,16,512]{3,2,1,0:T(8,128)S(1)} %collective-permute-done.x_low, f32[3,4,16,512]{3,2,1,0:T(8,128)S(1)} %collective-permute-done.1.x_high, ...), custom_call_target="tpu_custom_call" | custom-call | flops 18400000000 | bytes 59040000 | tf_op jit(solution)/shard_map/pallas_call | solution.py:321
  48.4 0.1 collective-permute-start.4
  48.5 1.2 %collective-permute-done.4 = f32[88,128]{1,0:T(8,128)S(1)} collective-permute-done((f32[88,128]{1,0:T(8,128)S(1)}, f32[88,128]{1,0:T(8,128)S(1)}, u32[]{:S(2)}, u32[]{:S(2)}) %collective-permute-start.4) | collective-permute-done | bytes 45088 | tf_op jit(solution)/shard_map/ppermute | solution.py:365
  49.8 1.2 %collective-permute-start.6 = (f32[88,128]{1,0:T(8,128)S(1)}, f32[88,128]{1,0:T(8,128)S(1)}, u32[]{:S(2)}, u32[]{:S(2)}) collective-permute-start(f32[88,128]{1,0:T(8,128)S(1)} %add.21), channel_id=1, source_target_pairs={{0,48},{1,49},{2,50},{3,51},{4,52},{5,53},{6,54},{7,55},{8,56},{9,... | collective-permute-start | bytes 135176 | tf_op jit(solution)/shard_map/ppermute | solution.py:365
  51.0 2.3 %collective-permute-start.5 = (f32[88,128]{1,0:T(8,128)S(1)}, f32[88,128]{1,0:T(8,128)S(1)}, u32[]{:S(2)}, u32[]{:S(2)}) collective-permute-start(f32[88,128]{1,0:T(8,128)S(1)} %add.21), channel_id=1, source_target_pairs={{0,16},{1,17},{2,18},{3,19},{4,20},{5,21},{6,22},{7,23},{8,24},{9,... | collective-permute-start | bytes 135176 | tf_op jit(solution)/shard_map/ppermute | solution.py:365
  53.3 2.4 %collective-permute-done.7 = f32[88,128]{1,0:T(8,128)S(1)} collective-permute-done((f32[88,128]{1,0:T(8,128)S(1)}, f32[88,128]{1,0:T(8,128)S(1)}, u32[]{:S(2)}, u32[]{:S(2)}) %collective-permute-start.7) | collective-permute-done | bytes 45088 | tf_op jit(solution)/shard_map/ppermute | solution.py:365
  55.8 0.1 collective-permute-start.10
  55.9 3.4 %collective-permute-start.8 = (f32[88,128]{1,0:T(8,128)S(1)}, f32[88,128]{1,0:T(8,128)S(1)}, u32[]{:S(2)}, u32[]{:S(2)}) collective-permute-start(f32[88,128]{1,0:T(8,128)S(1)} %add_add_fusion.1), channel_id=1, source_target_pairs={{0,2},{1,3},{2,0},{3,1},{4,6},{5,7},{6,4},{7,5},{8,10},{9,11},{10,... | collective-permute-start | bytes 135176 | tf_op jit(solution)/shard_map/ppermute | solution.py:365
  59.3 2.2 %collective-permute-done.10 = f32[88,128]{1,0:T(8,128)S(1)} collective-permute-done((f32[88,128]{1,0:T(8,128)S(1)}, f32[88,128]{1,0:T(8,128)S(1)}, u32[]{:S(2)}, u32[]{:S(2)}) %collective-permute-start.10) | collective-permute-done | bytes 45088 | tf_op jit(solution)/shard_map/ppermute | solution.py:365
  61.5 0.2 collective-permute-done.9
  61.7 0.1 collective-permute-start.13
  61.8 2.5 %collective-permute-start.12 = (f32[88,128]{1,0:T(8,128)S(1)}, f32[88,128]{1,0:T(8,128)S(1)}, u32[]{:S(2)}, u32[]{:S(2)}) collective-permute-start(f32[88,128]{1,0:T(8,128)S(1)} %add_add_fusion.a), channel_id=1, source_target_pairs={{0,72},{1,73},{2,74},{3,75},{4,76},{5,77},{6,78},{7,79},{8,64},{9,... | collective-permute-start | bytes 135176 | tf_op jit(solution)/shard_map/ppermute | solution.py:365
  64.2 1.0 %collective-permute-start.11 = (f32[88,128]{1,0:T(8,128)S(1)}, f32[88,128]{1,0:T(8,128)S(1)}, u32[]{:S(2)}, u32[]{:S(2)}) collective-permute-start(f32[88,128]{1,0:T(8,128)S(1)} %add_add_fusion.a), channel_id=1, source_target_pairs={{0,64},{1,65},{2,66},{3,67},{4,68},{5,69},{6,70},{7,71},{8,72},{9,... | collective-permute-start | bytes 135176 | tf_op jit(solution)/shard_map/ppermute | solution.py:365
  65.3 2.9 %shard_map.114 = f32[3,4,16,512]{3,2,1,0:T(8,128)} custom-call(f32[3,8,40,640]{3,2,1,0:T(8,128)S(1)} %get-tuple-element.37.middle), custom_call_target="tpu_custom_call" | custom-call | flops 3449999872 | bytes 11070000 | tf_op jit(solution)/shard_map/pallas_call | solution.py:321
  68.2 0.1 collective-permute-done.11.b
  68.3 0.8 %shard_map.115 = (f32[64,81]{1,0:T(8,128)}, f32[64,64]{1,0:T(8,128)}, f32[6,64]{1,0:T(8,128)}) custom-call(f32[88,128]{1,0:T(8,128)S(1)} %add_add_fusion.a, f32[88,128]{1,0:T(8,128)S(1)} %collective-permute-done.11.b, f32[88,128]{1,0:T(8,128)S(1)} %collective-permute-done.12.c, f32[88,128]{1,0:T(8,128)S(1)} %collective-permute-done.13.d), custom_call_target="tpu_custom_call" | custom-call | flops 1150000000 | bytes 3690000 | tf_op jit(solution)/shard_map/pallas_call | solution.py:321
  (42 shorter events, 0.4 us)
Async XLA Ops:
  0.6 17.5 %copy-start = (f32[3,4,16,512]{3,2,1,0:T(8,128)S(1)}, f32[3,4,16,512]{3,2,1,0:T(8,128)}, u32[]{:S(2)}) copy-start(f32[3,4,16,512]{3,2,1,0:T(8,128)} %own.5) | copy-start | bytes 1179652
  0.6 13.2 %collective-permute-start.1 = (f32[3,4,16,512]{3,2,1,0:T(8,128)}, f32[3,4,16,512]{3,2,1,0:T(8,128)S(1)}, u32[]{:S(2)}, u32[]{:S(2)}) collective-permute-start(f32[3,4,16,512]{3,2,1,0:T(8,128)} %own.5), channel_id=1, source_target_pairs={{0,112},{1,113},{2,114},{3,115},{4,116},{5,117},{6,118},{7,119},{8... | collective-permute-start | bytes 1179656 | tf_op jit(solution)/shard_map/ppermute | solution.py:365
  5.2 12.9 %collective-permute-start = (f32[3,4,16,512]{3,2,1,0:T(8,128)}, f32[3,4,16,512]{3,2,1,0:T(8,128)S(1)}, u32[]{:S(2)}, u32[]{:S(2)}) collective-permute-start(f32[3,4,16,512]{3,2,1,0:T(8,128)} %own.5), channel_id=1, source_target_pairs={{0,16},{1,17},{2,18},{3,19},{4,20},{5,21},{6,22},{7,23},{8,24},{9,... | collective-permute-start | bytes 1179656 | tf_op jit(solution)/shard_map/ppermute | solution.py:365
  18.1 4.4 %copy-start.1 = (s32[4,16]{1,0:T(4,128)S(1)}, s32[4,16]{1,0:T(4,128)}, u32[]{:S(2)}) copy-start(s32[4,16]{1,0:T(4,128)} %offs.5) | copy-start | bytes 772
  18.1 4.4 %copy-start.2 = (bf16[512,216]{1,0:T(8,128)(2,1)S(1)}, bf16[512,216]{1,0:T(8,128)(2,1)}, u32[]{:S(2)}) copy-start(bf16[512,216]{1,0:T(8,128)(2,1)} %constant.6.clone.pick) | copy-start | bytes 663556
  18.2 4.4 %copy-start.3 = (bf16[256,96]{1,0:T(8,128)(2,1)S(1)}, bf16[256,96]{1,0:T(8,128)(2,1)}, u32[]{:S(2)}) copy-start(bf16[256,96]{1,0:T(8,128)(2,1)} %constant.7.clone.pick_target) | copy-start | bytes 147460
  18.2 4.4 %copy-start.5 = (f32[64,96]{1,0:T(8,128)S(1)}, f32[64,96]{1,0:T(8,128)}, u32[]{:S(2)}) copy-start(f32[64,96]{1,0:T(8,128)} %get-tuple-element.31.h1) | copy-start | bytes 73732
  18.2 4.4 %copy-start.6 = (f32[64,64]{1,0:T(8,128)S(1)}, f32[64,64]{1,0:T(8,128)}, u32[]{:S(2)}) copy-start(f32[64,64]{1,0:T(8,128)} %get-tuple-element.32.h2) | copy-start | bytes 49156
  18.2 4.4 %copy-start.7 = (bf16[64,96]{1,0:T(8,128)(2,1)S(1)}, bf16[64,96]{1,0:T(8,128)(2,1)}, u32[]{:S(2)}) copy-start(bf16[64,96]{1,0:T(8,128)(2,1)} %get-tuple-element.26.w1) | copy-start | bytes 36868
  18.2 4.4 %copy-start.8 = (bf16[64,64]{1,0:T(8,128)(2,1)S(1)}, bf16[64,64]{1,0:T(8,128)(2,1)}, u32[]{:S(2)}) copy-start(bf16[64,64]{1,0:T(8,128)(2,1)} %get-tuple-element.27.w2) | copy-start | bytes 24580
  18.2 4.4 %copy-start.9 = (bf16[64,64]{1,0:T(8,128)(2,1)S(1)}, bf16[64,64]{1,0:T(8,128)(2,1)}, u32[]{:S(2)}) copy-start(bf16[64,64]{1,0:T(8,128)(2,1)} %get-tuple-element.28.w2t) | copy-start | bytes 24580
  18.4 9.2 %collective-permute-start.3 = (f32[3,12,4,512]{3,2,1,0:T(4,128)S(1)}, f32[3,12,4,512]{3,2,1,0:T(4,128)S(1)}, u32[]{:S(2)}, u32[]{:S(2)}) collective-permute-start(f32[3,12,4,512]{3,2,1,0:T(4,128)S(1)} %get-tuple-element.42), channel_id=1, source_target_pairs={{0,15},{1,0},{2,1},{3,2},{4,3},{5,4},{6,5},{7,6},{8,7},{9,8},{10,9... | collective-permute-start | bytes 884744 | tf_op jit(solution)/shard_map/ppermute | solution.py:365
  22.5 9.8 %collective-permute-start.2 = (f32[3,12,4,512]{3,2,1,0:T(4,128)S(1)}, f32[3,12,4,512]{3,2,1,0:T(4,128)S(1)}, u32[]{:S(2)}, u32[]{:S(2)}) collective-permute-start(f32[3,12,4,512]{3,2,1,0:T(4,128)S(1)} %get-tuple-element.43), channel_id=1, source_target_pairs={{0,1},{1,2},{2,3},{3,4},{4,5},{5,6},{6,7},{7,8},{8,9},{9,10},{10,1... | collective-permute-start | bytes 884744 | tf_op jit(solution)/shard_map/ppermute | solution.py:365
  22.6 9.7 %copy-start.4 = (bf16[81,96]{1,0:T(8,128)(2,1)S(1)}, bf16[81,96]{1,0:T(8,128)(2,1)}, u32[]{:S(2)}) copy-start(bf16[81,96]{1,0:T(8,128)(2,1)} %constant.8.clone.order) | copy-start | bytes 46660
  48.4 1.3 %collective-permute-start.4 = (f32[88,128]{1,0:T(8,128)S(1)}, f32[88,128]{1,0:T(8,128)S(1)}, u32[]{:S(2)}, u32[]{:S(2)}) collective-permute-start(f32[88,128]{1,0:T(8,128)S(1)} %get-tuple-element.38), channel_id=1, source_target_pairs={{0,1},{1,0},{2,3},{3,2},{4,5},{5,4},{6,7},{7,6},{8,9},{9,8},{10,11... | collective-permute-start | bytes 135176 | tf_op jit(solution)/shard_map/ppermute | solution.py:365
  49.7 6.0 %collective-permute-start.7 = (f32[88,128]{1,0:T(8,128)S(1)}, f32[88,128]{1,0:T(8,128)S(1)}, u32[]{:S(2)}, u32[]{:S(2)}) collective-permute-start(f32[88,128]{1,0:T(8,128)S(1)} %add.21), channel_id=1, source_target_pairs={{0,32},{1,33},{2,34},{3,35},{4,36},{5,37},{6,38},{7,39},{8,40},{9,... | collective-permute-start | bytes 135176 | tf_op jit(solution)/shard_map/ppermute | solution.py:365
  49.8 5.9 %collective-permute-start.6 = (f32[88,128]{1,0:T(8,128)S(1)}, f32[88,128]{1,0:T(8,128)S(1)}, u32[]{:S(2)}, u32[]{:S(2)}) collective-permute-start(f32[88,128]{1,0:T(8,128)S(1)} %add.21), channel_id=1, source_target_pairs={{0,48},{1,49},{2,50},{3,51},{4,52},{5,53},{6,54},{7,55},{8,56},{9,... | collective-permute-start | bytes 135176 | tf_op jit(solution)/shard_map/ppermute | solution.py:365
  51.0 4.7 %collective-permute-start.5 = (f32[88,128]{1,0:T(8,128)S(1)}, f32[88,128]{1,0:T(8,128)S(1)}, u32[]{:S(2)}, u32[]{:S(2)}) collective-permute-start(f32[88,128]{1,0:T(8,128)S(1)} %add.21), channel_id=1, source_target_pairs={{0,16},{1,17},{2,18},{3,19},{4,20},{5,21},{6,22},{7,23},{8,24},{9,... | collective-permute-start | bytes 135176 | tf_op jit(solution)/shard_map/ppermute | solution.py:365
  55.8 5.7 %collective-permute-start.10 = (f32[88,128]{1,0:T(8,128)S(1)}, f32[88,128]{1,0:T(8,128)S(1)}, u32[]{:S(2)}, u32[]{:S(2)}) collective-permute-start(f32[88,128]{1,0:T(8,128)S(1)} %add_add_fusion.1), channel_id=1, source_target_pairs={{0,4},{1,5},{2,6},{3,7},{4,0},{5,1},{6,2},{7,3},{8,12},{9,13},{10,... | collective-permute-start | bytes 135176 | tf_op jit(solution)/shard_map/ppermute | solution.py:365
  55.9 5.8 %collective-permute-start.9 = (f32[88,128]{1,0:T(8,128)S(1)}, f32[88,128]{1,0:T(8,128)S(1)}, u32[]{:S(2)}, u32[]{:S(2)}) collective-permute-start(f32[88,128]{1,0:T(8,128)S(1)} %add_add_fusion.1), channel_id=1, source_target_pairs={{0,6},{1,7},{2,4},{3,5},{4,2},{5,3},{6,0},{7,1},{8,14},{9,15},{10,... | collective-permute-start | bytes 135176 | tf_op jit(solution)/shard_map/ppermute | solution.py:365
  55.9 5.7 %collective-permute-start.8 = (f32[88,128]{1,0:T(8,128)S(1)}, f32[88,128]{1,0:T(8,128)S(1)}, u32[]{:S(2)}, u32[]{:S(2)}) collective-permute-start(f32[88,128]{1,0:T(8,128)S(1)} %add_add_fusion.1), channel_id=1, source_target_pairs={{0,2},{1,3},{2,0},{3,1},{4,6},{5,7},{6,4},{7,5},{8,10},{9,11},{10,... | collective-permute-start | bytes 135176 | tf_op jit(solution)/shard_map/ppermute | solution.py:365
  61.7 6.5 %collective-permute-start.13 = (f32[88,128]{1,0:T(8,128)S(1)}, f32[88,128]{1,0:T(8,128)S(1)}, u32[]{:S(2)}, u32[]{:S(2)}) collective-permute-start(f32[88,128]{1,0:T(8,128)S(1)} %add_add_fusion.a), channel_id=1, source_target_pairs={{0,8},{1,9},{2,10},{3,11},{4,12},{5,13},{6,14},{7,15},{8,0},{9,1},... | collective-permute-start | bytes 135176 | tf_op jit(solution)/shard_map/ppermute | solution.py:365
  61.8 6.4 %collective-permute-start.12 = (f32[88,128]{1,0:T(8,128)S(1)}, f32[88,128]{1,0:T(8,128)S(1)}, u32[]{:S(2)}, u32[]{:S(2)}) collective-permute-start(f32[88,128]{1,0:T(8,128)S(1)} %add_add_fusion.a), channel_id=1, source_target_pairs={{0,72},{1,73},{2,74},{3,75},{4,76},{5,77},{6,78},{7,79},{8,64},{9,... | collective-permute-start | bytes 135176 | tf_op jit(solution)/shard_map/ppermute | solution.py:365
  64.2 4.0 %collective-permute-start.11 = (f32[88,128]{1,0:T(8,128)S(1)}, f32[88,128]{1,0:T(8,128)S(1)}, u32[]{:S(2)}, u32[]{:S(2)}) collective-permute-start(f32[88,128]{1,0:T(8,128)S(1)} %add_add_fusion.a), channel_id=1, source_target_pairs={{0,64},{1,65},{2,66},{3,67},{4,68},{5,69},{6,70},{7,71},{8,72},{9,... | collective-permute-start | bytes 135176 | tf_op jit(solution)/shard_map/ppermute | solution.py:365
  (3 other events, 13.1 us)

commit v3 on v2

--- a/solution.py
+++ b/solution.py
@@ -14,21 +14,46 @@
 
 
 def selections():
-    pick = np.zeros((512, 216), np.float32)
-    pick_target = np.zeros((256, 96), np.float32)
+    table = np.zeros((864, 216), np.float32)
     for y in range(16):
         for c in range(3):
             for ox in range(3):
                 for oy in range(3):
-                    pick[y * 32 + c * 9 + ox * 3 + oy, (c * 3 + ox) * 24 + y + oy + 3] = 1
+                    table[y * 32 + c * 9 + ox * 3 + oy, (c * 3 + ox) * 24 + y + oy + 3] = 1
         for c in range(6):
-            pick_target[y * 16 + c, c * 16 + y] = 1
-    order = np.zeros((81, 96), np.float32)
+            table[512 + y * 16 + c, c * 16 + y] = 1
     for oz in range(3):
         for c in range(3):
             for o in range(9):
-                order[c * 27 + o * 3 + oz, oz * 32 + c * 9 + o] = 1
-    return pick, pick_target, order
+                table[768 + c * 27 + o * 3 + oz, oz * 32 + c * 9 + o] = 1
+    return table
+
+
+class Part:
+    def __init__(self, ref, first, last, lanes):
+        self.ref, self.first, self.last, self.lanes = ref, first, last, lanes
+
+    def rows(self, first, last):
+        return self.ref[self.first + first : self.first + last, 0 : self.lanes]
+
+    def __getitem__(self, _):
+        return self.ref[self.first : self.last, 0 : self.lanes]
+
+    def __setitem__(self, _, value):
+        self.ref[self.first : self.last, 0 : self.lanes] = value
+
+
+def table_parts(table):
+    return Part(table, 0, 512, 216), Part(table, 512, 768, 96), Part(table, 768, 849, 96)
+
+
+def weight_parts(packed):
+    return (Part(packed, 0, 64, 96), Part(packed, 64, 128, 64), Part(packed, 128, 192, 64),
+            Part(packed, 192, 208, 80), Part(packed, 208, 272, 16))
+
+
+def total_parts(packed):
+    return Part(packed, 0, 64, 96), Part(packed, 64, 128, 64), Part(packed, 128, 144, 64)
 
 
 def dot(a, b):
@@ -154,9 +179,24 @@
 
 
 def interior_kernel(
-    offs, own, first, mid, last, pick, pick_target, order,
-    w1, w2, w2t, w3, w3t, g1, g2, g3, field, tau, tile, tile_target,
+    offs, own, first, mid, last, table, packed_weights, packed_totals, field, tau, tile, tile_target,
+    local_table, local_first, local_mid, local_last, sems,
 ):
+    pairs_in = ((first, local_first), (mid, local_mid), (last, local_last), (table, local_table))
+    copies = [pltpu.make_async_copy(a, b, sems.at[k]) for k, (a, b) in enumerate(pairs_in)]
+    for copy in copies:
+        copy.start()
+    clear_edges(tile, tile_target)
+    clear_rest(field)
+    for c in range(3):
+        for p in range(4):
+            field[c, p, 12:28, 0:512] = own[c, p]
+    for copy in copies:
+        copy.wait()
+    first, mid, last = local_first, local_mid, local_last
+    pick, pick_target, order = table_parts(local_table)
+    weights, totals = weight_parts(packed_weights), total_parts(packed_totals)
+    w1, w2, w2t, w3, w3t = weights
     rows, cols = lax.broadcasted_iota(jnp.int32, (64, 64), 0), lax.broadcasted_iota(jnp.int32, (64, 64), 1)
     half = jnp.where(rows == cols, 0.5, 0.0).astype(bf16)
     w1[...] = (0.5 * dot(first[...], order[...])).astype(bf16)
@@ -167,13 +207,7 @@
     last_rows = jnp.concatenate([last[...].astype(f32), jnp.zeros((10, 64), f32)], 0)
     w3[...] = jnp.concatenate([last_rows, minus], 1).astype(bf16)
     w3t[...] = dot_cells(half, last_rows.astype(bf16)).astype(bf16)
-    for total in (g1, g2, g3):
-        total[...] = jnp.zeros_like(total)
-    clear_edges(tile, tile_target)
-    clear_rest(field)
-    for c in range(3):
-        for p in range(4):
-            field[c, p, 12:28, 0:512] = own[c, p]
+    packed_totals[...] = jnp.zeros_like(packed_totals)
 
     def step(n, _):
         x = n + 1
@@ -182,25 +216,78 @@
         gather(tile, 0, pick[...], input_rows(field, x))
         gather(tile_target, 0, pick_target[...], target_rows(tau, n))
         starts = [offs[x, y] for y in range(1, 15)]
-        add_columns(tile.at[32:480], tile_target.at[16:240], starts, (w1, w2, w2t, w3, w3t), (g1, g2, g3))
+        add_columns(tile.at[32:480], tile_target.at[16:240], starts, weights, totals)
         return 0
 
     lax.fori_loop(0, 2, step, 0)
 
 
+def split_bf16(value):
+    high = value.astype(bf16)
+    return high, (value - high.astype(f32)).astype(bf16)
+
+
+def pack_x_kernel(own, up, down):
+    for c in range(3):
+        for x in range(4):
+            high, rest = split_bf16(own[c, x])
+            up[c, x] = high
+            down[c, x + 1] = high
+            if x == 3:
+                up[c, 4] = rest
+            if x == 0:
+                down[c, 0] = rest
+
+
+def pack_y_kernel(own, x_low, x_high, right, left):
+    for c in range(3):
+        for out, first, near in ((right, 12, 15), (left, 0, 0)):
+            rests = []
+            for p in range(12):
+                if p < 4:
+                    high = x_low[c, p].astype(f32)
+                elif p < 8:
+                    high, rest = split_bf16(own[c, p - 4])
+                    high, rest = high.astype(f32), rest.astype(f32)
+                else:
+                    high = x_high[c, p - 7].astype(f32)
+                if p == 3:
+                    rest = x_low[c, 4].astype(f32)
+                if p == 8:
+                    rest = x_high[c, 0].astype(f32)
+                out[c, p] = high[first : first + 4, :].astype(bf16)
+                if 3 <= p <= 8:
+                    rests.append(rest[near : near + 1, :])
+            rests = jnp.concatenate(rests + [jnp.zeros((2, 512), f32)], 0)
+            out[c, 12] = rests[0:4].astype(bf16)
+            out[c, 13] = rests[4:8].astype(bf16)
+
+
+def x_plane(x_low, own, x_high, c, p):
+    if p < 4:
+        plane = x_low[c, p].astype(f32)
+        return plane + x_low[c, 4].astype(f32) if p == 3 else plane
+    if p < 8:
+        return own[c, p - 4]
+    plane = x_high[c, p - 7].astype(f32)
+    return plane + x_high[c, 0].astype(f32) if p == 8 else plane
+
+
 def side_kernel(
-    offs, own, x_low, x_high, w1, w2, w2t, w3, w3t, h1, h2, h3, pick, pick_target,
-    g1, g2, g3, field, tau, tile, tile_target,
+    offs, own, x_low, x_high, packed_weights, before, table, packed_totals, field, tau, tile, tile_target,
+    local_table, sems,
 ):
-    g1[...] = h1[...]
-    g2[...] = h2[...]
-    g3[...] = h3[...]
+    copy = pltpu.make_async_copy(table, local_table, sems.at[0])
+    copy.start()
+    pick, pick_target, _ = table_parts(local_table)
+    weights, totals = weight_parts(packed_weights), total_parts(packed_totals)
+    packed_totals[...] = before[...]
     clear_edges(tile, tile_target)
     clear_rest(field)
     for c in range(3):
         for p in range(6):
-            source, q = (x_low, 3) if p == 0 else (x_high, 0) if p == 5 else (own, p - 1)
-            field[c, p, 12:28, 0:512] = source[c, q]
+            field[c, p, 12:28, 0:512] = x_plane(x_low, own, x_high, c, p + 3)
+    copy.wait()
 
     def step(n, _):
         x = 3 * n
@@ -209,7 +296,7 @@
         gather(tile, 0, pick[...], input_rows(field, x + 1))
         gather(tile_target, 0, pick_target[...], target_rows(tau, 0))
         starts = [offs[x, y] for y in range(1, 15)]
-        add_columns(tile.at[32:480], tile_target.at[16:240], starts, (w1, w2, w2t, w3, w3t), (g1, g2, g3))
+        add_columns(tile.at[32:480], tile_target.at[16:240], starts, weights, totals)
         return 0
 
     lax.fori_loop(0, 2, step, 0)
@@ -217,12 +304,15 @@
 
 def middle_kernel(
     offs, own, x_low, x_high, y_low, y_high,
-    w1, w2, w2t, w3, w3t, h1, h2, h3, pick, pick_target, order,
-    middle, packed, field, tau, tile, tile_target, g1, g2, g3,
+    packed_weights, before, table, middle, packed, field, tau, tile, tile_target,
+    local_table, sems, packed_totals,
 ):
-    g1[...] = h1[...]
-    g2[...] = h2[...]
-    g3[...] = h3[...]
+    copy = pltpu.make_async_copy(table, local_table, sems.at[0])
+    copy.start()
+    pick, pick_target, order = table_parts(local_table)
+    weights, totals = weight_parts(packed_weights), total_parts(packed_totals)
+    packed_totals[...] = before[...]
+    g1, g2, g3 = totals
     clear_edges(tile, tile_target)
     clear_rest(field)
     line = jnp.zeros((1, LANES), f32)
@@ -232,10 +322,14 @@
             tau[c, p, 32:33, :] = line
     for c in range(3):
         for p in range(12):
-            source, q = ((x_low, p), (own, p - 4), (x_high, p - 8))[p // 4]
-            field[c, p, 12:28, 0:512] = source[c, q]
-            field[c, p, 8:12, 0:512] = y_low[c, p]
-            field[c, p, 28:32, 0:512] = y_high[c, p]
+            field[c, p, 12:28, 0:512] = x_plane(x_low, own, x_high, c, p)
+            low, high = y_low[c, p].astype(f32), y_high[c, p].astype(f32)
+            field[c, p, 8:12, 0:512] = low
+            field[c, p, 28:32, 0:512] = high
+            if 3 <= p <= 8:
+                k, r = 12 + (p - 3) // 4, (p - 3) % 4
+                field[c, p, 11:12, 0:512] = low[3:4] + y_low[c, k].astype(f32)[r : r + 1]
+                field[c, p, 28:29, 0:512] = high[0:1] + y_high[c, k].astype(f32)[r : r + 1]
 
     def stress_zero(p, _):
         for row in (8, 16, 24):
@@ -253,20 +347,21 @@
         return 0
 
     lax.fori_loop(0, 8, advance_middle, 0)
+    copy.wait()
 
     def step(x, _):
         rows = input_rows(field, x + 4)
-        gather(tile, 512, pick[0:32, :], rows)
-        gather(tile, 544, pick[480:512, :], rows)
+        gather(tile, 512, pick.rows(0, 32), rows)
+        gather(tile, 544, pick.rows(480, 512), rows)
         rows = target_rows(tau, x + 3)
-        gather(tile_target, 256, pick_target[0:16, :], rows)
-        gather(tile_target, 272, pick_target[240:256, :], rows)
+        gather(tile_target, 256, pick_target.rows(0, 16), rows)
+        gather(tile_target, 272, pick_target.rows(240, 256), rows)
         for row in (12, 20):
             stress_rows(middle, x + 2, tau, 0, row)
         gather(tile, 0, pick[...], input_rows(middle, x + 2))
         gather(tile_target, 0, pick_target[...], target_rows(tau, 0))
         starts = [offs[x, y] for y in range(16)] + [offs[x, 0], offs[x, 15]]
-        add_columns(tile, tile_target, starts, (w1, w2, w2t, w3, w3t), (g1, g2, g3))
+        add_columns(tile, tile_target, starts, weights, totals)
         return 0
 
     lax.fori_loop(0, 4, step, 0)
@@ -277,7 +372,7 @@
     mids = g2[...]
     packed[0:64, :] = scale * jnp.concatenate([ordered, jnp.zeros((64, 15), f32), mids[:, 0:32]], 1)
     packed[64:80, :] = scale * jnp.concatenate([mids[16 * k : 16 * k + 16, 32:64] for k in range(4)], 1)
-    packed[80:88, :] = scale * jnp.concatenate([g3[0:8, :], jnp.zeros((8, 64), f32)], 1)
+    packed[80:88, :] = scale * jnp.concatenate([g3[...][0:8], jnp.zeros((8, 64), f32)], 1)
 
 
 def final_kernel(middle, final, tau):
@@ -310,17 +405,16 @@
     return jax.ShapeDtypeStruct(dims, kind)
 
 
-WEIGHTS = [shaped(64, 96, kind=bf16), shaped(64, 64, kind=bf16), shaped(64, 64, kind=bf16),
-           shaped(16, 80, kind=bf16), shaped(64, 16, kind=bf16)]
-TOTALS = [shaped(64, 96), shaped(64, 64), shaped(16, 64)]
-
-
-def call(kernel, args, out_shape, scratch, smem=0, us=1, mib=48):
+WEIGHTS, TOTALS = shaped(272, 128, kind=bf16), shaped(144, 128)
+
+
+def call(kernel, args, out_shape, scratch, smem=0, us=1, mib=16, hbm=0):
     vmem = pl.BlockSpec(memory_space=pltpu.VMEM)
     scalar = pl.BlockSpec(memory_space=pltpu.SMEM)
+    far = pl.BlockSpec(memory_space=pltpu.HBM)
     return pl.pallas_call(
         kernel,
-        in_specs=[scalar] * smem + [vmem] * (len(args) - smem),
+        in_specs=[scalar] * smem + [vmem] * (len(args) - smem - hbm) + [far] * hbm,
         out_specs=[vmem] * len(out_shape),
         out_shape=out_shape,
         scratch_shapes=scratch,
@@ -335,6 +429,7 @@
         pltpu.VMEM((6, stress_planes, ROWS, LANES), f32),
         pltpu.VMEM((32 * columns, 768), bf16),
         pltpu.VMEM((16 * columns, 768), bf16),
+        pltpu.VMEM((864, 216), bf16),
     ]
 
 
@@ -366,28 +461,33 @@
 
 
 def body(velocity, first_weight, mid_weight, last_weight, offsets):
-    pick, pick_target, order = (jnp.asarray(table, bf16) for table in selections())
+    table = jnp.asarray(selections(), bf16)
     up, down = lambda i, j: (i + 1, j), lambda i, j: (i - 1, j)
     right, left = lambda i, j: (i, j + 1), lambda i, j: (i, j - 1)
-    x_low, x_high = send(velocity, up), send(velocity, down)
-    *weights, h1, h2, h3 = call(
+    to_up, to_down = call(pack_x_kernel, (velocity,), [shaped(3, 5, 16, 512, kind=bf16)] * 2, [])
+    x_low, x_high = send(to_up, up), send(to_down, down)
+    weights, totals = call(
         interior_kernel,
-        (offsets, velocity, first_weight, mid_weight, last_weight, pick, pick_target, order),
-        WEIGHTS + TOTALS, columns_scratch(4, 2, 16), 1, 6, 62,
+        (offsets, velocity, first_weight, mid_weight, last_weight, table),
+        [WEIGHTS, TOTALS], columns_scratch(4, 2, 16)
+        + [pltpu.VMEM(n, bf16) for n in ((64, 81), (64, 64), (6, 64))] + [pltpu.SemaphoreType.DMA((4,))],
+        1, 6, 16, 4,
     )
-    x_low, x_high, h1 = lax.optimization_barrier((x_low, x_high, h1))
-    wide = jnp.concatenate([x_low, velocity, x_high], 1)
-    y_low, y_high = send(wide[:, :, 12:16, :], right), send(wide[:, :, 0:4, :], left)
-    totals = call(
+    x_low, x_high, totals = lax.optimization_barrier((x_low, x_high, totals))
+    to_right, to_left = call(
+        pack_y_kernel, (velocity, x_low, x_high), [shaped(3, 14, 4, 512, kind=bf16)] * 2, []
+    )
+    y_low, y_high = send(to_right, right), send(to_left, left)
+    (totals,) = call(
         side_kernel,
-        (offsets, velocity, x_low, x_high, *weights, h1, h2, h3, pick, pick_target),
-        TOTALS, columns_scratch(6, 1, 16), 1, 6,
+        (offsets, velocity, x_low, x_high, weights, totals, table),
+        [TOTALS], columns_scratch(6, 1, 16) + [pltpu.SemaphoreType.DMA((1,))], 1, 6, 16, 1,
     )
     middle, packed = call(
         middle_kernel,
-        (offsets, velocity, x_low, x_high, y_low, y_high, *weights, *totals, pick, pick_target, order),
+        (offsets, velocity, x_low, x_high, y_low, y_high, weights, totals, table),
         [shaped(3, 8, ROWS, LANES), shaped(88, 128)],
-        columns_scratch(12, 10, 18) + [pltpu.VMEM(t.shape, f32) for t in TOTALS], 1, 16,
+        columns_scratch(12, 10, 18) + [pltpu.SemaphoreType.DMA((1,)), pltpu.VMEM(TOTALS.shape, f32)], 1, 16, 32, 1,
     )
     (final,) = call(final_kernel, (middle,), [shaped(3, 4, 16, 512)], [pltpu.VMEM((6, 6, ROWS, LANES), f32)], 0, 3)
 

time: 69.3 us -> 64.8 us (0.935)
  waiting for transfers between devices: 17.4 us -> 8.83 us
  starting transfers between devices: 19.4 us -> 23.1 us
  local copies, waits for them, and re-layouts: 0.29 us -> 1.02 us
    ppermute x14, waiting for transfers between devices: 17.4 us -> 8.83 us  [send(): return lax.ppermute(value, AXES, pairs(move))]
    ppermute x14, starting transfers between devices: 19.4 us -> 23.1 us  [send(): return lax.ppermute(value, AXES, pairs(move))]
    unnamed x28 -> x14, local copies, waits for them, and re-layouts: 0.13 us -> 1.02 us
    pallas_call x5 -> x7, Pallas kernels: 31 us -> 30.9 us  [call(): pl.pallas_call(kernel, in_specs=[scalar] * smem + [vmem] * (len(args) - s...]
  transfers between devices with their start and end apart: 14 -> 14, of which waited for: 8 -> 10; matrix products, arithmetic and copies ran while one was open for 0% -> 0% of each run, Pallas kernels for 20% -> 21%
where the time goes in v3:
time: 64.8 us; the launch traced here: 64.6 us
  Pallas kernels  30.9 us (48%)
  starting transfers between devices  23.1 us (36%)
  waiting for transfers between devices  8.83 us (14%)
  local copies, waits for them, and re-layouts  1.02 us (2%)
  between operations  0.76 us (1%)
    pallas_call x7, Pallas kernels, call(): pl.pallas_call(kernel, in_specs=[scalar] * smem + [vmem] * (len(args) - s...  30.9 us
    ppermute x14, starting transfers between devices, send(): return lax.ppermute(value, AXES, pairs(move))  23.1 us
    ppermute x14, waiting for transfers between devices, send(): return lax.ppermute(value, AXES, pairs(move))  8.83 us
  transfers between devices with their start and end apart: 14, of which 10 were waited for; matrix products, arithmetic and copies ran while one was open for 0% of the time, Pallas kernels for 21%

profile of v3, /device:TPU:0, one launch (start us, length us, event | category | flops | bytes accessed | tf_op | source)
XLA Modules:
  0.0 64.6 jit_solution(1134012629652858244)
XLA Ops:
  0.6 1.0 %copy-done = f32[3,4,16,512]{3,2,1,0:T(8,128)S(1)} copy-done((f32[3,4,16,512]{3,2,1,0:T(8,128)S(1)}, f32[3,4,16,512]{3,2,1,0:T(8,128)}, u32[]{:S(2)}) %copy-start) | copy-done | bytes 393240
  1.7 1.7 %collective-permute-start = (bf16[3,5,16,512]{3,2,1,0:T(8,128)(2,1)S(1)}, bf16[3,5,16,512]{3,2,1,0:T(8,128)(2,1)S(1)}, u32[]{:S(2)}, u32[]{:S(2)}) collective-permute-start(bf16[3,5,16,512]{3,2,1,0:T(8,128)(2,1)S(1)} %get-tuple-element.18), channel_id=1, source_target_pairs={{0,16},{1,17},{2,18},{3,19},{4,20},{5,21},{6,22},{7,23},{8,24},{9,... | collective-permute-start | bytes 737288 | tf_op jit(solution)/shard_map/ppermute | solution.py:460
  3.4 2.9 %collective-permute-start.1 = (bf16[3,5,16,512]{3,2,1,0:T(8,128)(2,1)S(1)}, bf16[3,5,16,512]{3,2,1,0:T(8,128)(2,1)S(1)}, u32[]{:S(2)}, u32[]{:S(2)}) collective-permute-start(bf16[3,5,16,512]{3,2,1,0:T(8,128)(2,1)S(1)} %get-tuple-element.19), channel_id=1, source_target_pairs={{0,112},{1,113},{2,114},{3,115},{4,116},{5,117},{6,118},{7,119},{8... | collective-permute-start | bytes 737288 | tf_op jit(solution)/shard_map/ppermute | solution.py:460
  6.3 5.4 %shard_map.94 = (bf16[272,128]{1,0:T(8,128)(2,1)S(1)}, f32[144,128]{1,0:T(8,128)S(1)}) custom-call(s32[4,16]{1,0:T(4,128)S(1)} %copy-done.5, f32[3,4,16,512]{3,2,1,0:T(8,128)S(1)} %copy-done, bf16[64,81]{1,0:T(8,128)(2,1)S(1)} %copy-done.2, bf16[64,64]{1,0:T(8,128)(2,1)S(1)} %copy-done.3, bf16[6,64]{1,0:T(8,128)(2,1)S(1)} %copy-done.4, ...), custom_call_target="tpu_custom_call" | custom-call | flops 6899999744 | bytes 22140000 | tf_op jit(solution)/shard_map/pallas_call | solution.py:415
  12.4 5.3 %collective-permute-start.3 = (bf16[3,14,4,512]{3,2,1,0:T(4,128)(2,1)S(1)}, bf16[3,14,4,512]{3,2,1,0:T(4,128)(2,1)S(1)}, u32[]{:S(2)}, u32[]{:S(2)}) collective-permute-start(bf16[3,14,4,512]{3,2,1,0:T(4,128)(2,1)S(1)} %get-tuple-element.24), channel_id=1, source_target_pairs={{0,15},{1,0},{2,1},{3,2},{4,3},{5,4},{6,5},{7,6},{8,7},{9,8},{10,9... | collective-permute-start | bytes 516104 | tf_op jit(solution)/shard_map/ppermute | solution.py:460
  17.7 5.3 %shard_map.96.before = f32[144,128]{1,0:T(8,128)S(1)} custom-call(s32[4,16]{1,0:T(4,128)S(1)} %copy-done.5, f32[3,4,16,512]{3,2,1,0:T(8,128)S(1)} %copy-done, bf16[3,5,16,512]{3,2,1,0:T(8,128)(2,1)S(1)} %collective-permute-done.x_low, bf16[3,5,16,512]{3,2,1,0:T(8,128)(2,1)S(1)} %collective-permute-done.1.x_high, ...), custom_call_target="tpu_custom_call" | custom-call | flops 6899999744 | bytes 22140000 | tf_op jit(solution)/shard_map/pallas_call | solution.py:415
  23.0 16.4 %shard_map.97 = (f32[3,8,40,640]{3,2,1,0:T(8,128)S(1)}, f32[88,128]{1,0:T(8,128)S(1)}) custom-call(s32[4,16]{1,0:T(4,128)S(1)} %copy-done.5, f32[3,4,16,512]{3,2,1,0:T(8,128)S(1)} %copy-done.1, bf16[3,5,16,512]{3,2,1,0:T(8,128)(2,1)S(1)} %collective-permute-done.x_low, bf16[3,5,16,512]{3,2,1,0:T(8,128)(2,1)S(1)} %collective-permute-done.1.x_high, ...), custom_call_target="tpu_custom_call" | custom-call | flops 18400000000 | bytes 59040000 | tf_op jit(solution)/shard_map/pallas_call | solution.py:415
  39.5 1.2 %collective-permute-done.4 = f32[88,128]{1,0:T(8,128)S(1)} collective-permute-done((f32[88,128]{1,0:T(8,128)S(1)}, f32[88,128]{1,0:T(8,128)S(1)}, u32[]{:S(2)}, u32[]{:S(2)}) %collective-permute-start.4) | collective-permute-done | bytes 45088 | tf_op jit(solution)/shard_map/ppermute | solution.py:460
  40.7 1.6 %collective-permute-start.7 = (f32[88,128]{1,0:T(8,128)S(1)}, f32[88,128]{1,0:T(8,128)S(1)}, u32[]{:S(2)}, u32[]{:S(2)}) collective-permute-start(f32[88,128]{1,0:T(8,128)S(1)} %add.21), channel_id=1, source_target_pairs={{0,32},{1,33},{2,34},{3,35},{4,36},{5,37},{6,38},{7,39},{8,40},{9,... | collective-permute-start | bytes 135176 | tf_op jit(solution)/shard_map/ppermute | solution.py:460
  42.4 2.3 %collective-permute-start.6 = (f32[88,128]{1,0:T(8,128)S(1)}, f32[88,128]{1,0:T(8,128)S(1)}, u32[]{:S(2)}, u32[]{:S(2)}) collective-permute-start(f32[88,128]{1,0:T(8,128)S(1)} %add.21), channel_id=1, source_target_pairs={{0,48},{1,49},{2,50},{3,51},{4,52},{5,53},{6,54},{7,55},{8,56},{9,... | collective-permute-start | bytes 135176 | tf_op jit(solution)/shard_map/ppermute | solution.py:460
  44.7 0.8 %collective-permute-start.5 = (f32[88,128]{1,0:T(8,128)S(1)}, f32[88,128]{1,0:T(8,128)S(1)}, u32[]{:S(2)}, u32[]{:S(2)}) collective-permute-start(f32[88,128]{1,0:T(8,128)S(1)} %add.21), channel_id=1, source_target_pairs={{0,16},{1,17},{2,18},{3,19},{4,20},{5,21},{6,22},{7,23},{8,24},{9,... | collective-permute-start | bytes 135176 | tf_op jit(solution)/shard_map/ppermute | solution.py:460
  45.5 0.9 %collective-permute-done.7 = f32[88,128]{1,0:T(8,128)S(1)} collective-permute-done((f32[88,128]{1,0:T(8,128)S(1)}, f32[88,128]{1,0:T(8,128)S(1)}, u32[]{:S(2)}, u32[]{:S(2)}) %collective-permute-start.7) | collective-permute-done | bytes 45088 | tf_op jit(solution)/shard_map/ppermute | solution.py:460
  46.4 1.2 %collective-permute-done.6 = f32[88,128]{1,0:T(8,128)S(1)} collective-permute-done((f32[88,128]{1,0:T(8,128)S(1)}, f32[88,128]{1,0:T(8,128)S(1)}, u32[]{:S(2)}, u32[]{:S(2)}) %collective-permute-start.6) | collective-permute-done | bytes 45088 | tf_op jit(solution)/shard_map/ppermute | solution.py:460
  47.6 1.1 %collective-permute-done.5 = f32[88,128]{1,0:T(8,128)S(1)} collective-permute-done((f32[88,128]{1,0:T(8,128)S(1)}, f32[88,128]{1,0:T(8,128)S(1)}, u32[]{:S(2)}, u32[]{:S(2)}) %collective-permute-start.5) | collective-permute-done | bytes 45088 | tf_op jit(solution)/shard_map/ppermute | solution.py:460
  48.9 3.8 %collective-permute-start.9 = (f32[88,128]{1,0:T(8,128)S(1)}, f32[88,128]{1,0:T(8,128)S(1)}, u32[]{:S(2)}, u32[]{:S(2)}) collective-permute-start(f32[88,128]{1,0:T(8,128)S(1)} %add_add_fusion.1), channel_id=1, source_target_pairs={{0,6},{1,7},{2,4},{3,5},{4,2},{5,3},{6,0},{7,1},{8,14},{9,15},{10,... | collective-permute-start | bytes 135176 | tf_op jit(solution)/shard_map/ppermute | solution.py:460
  52.7 0.8 %collective-permute-start.8 = (f32[88,128]{1,0:T(8,128)S(1)}, f32[88,128]{1,0:T(8,128)S(1)}, u32[]{:S(2)}, u32[]{:S(2)}) collective-permute-start(f32[88,128]{1,0:T(8,128)S(1)} %add_add_fusion.1), channel_id=1, source_target_pairs={{0,2},{1,3},{2,0},{3,1},{4,6},{5,7},{6,4},{7,5},{8,10},{9,11},{10,... | collective-permute-start | bytes 135176 | tf_op jit(solution)/shard_map/ppermute | solution.py:460
  53.5 1.0 %collective-permute-done.10 = f32[88,128]{1,0:T(8,128)S(1)} collective-permute-done((f32[88,128]{1,0:T(8,128)S(1)}, f32[88,128]{1,0:T(8,128)S(1)}, u32[]{:S(2)}, u32[]{:S(2)}) %collective-permute-start.10) | collective-permute-done | bytes 45088 | tf_op jit(solution)/shard_map/ppermute | solution.py:460
  54.4 0.5 collective-permute-done.9
  54.9 1.8 %collective-permute-done.8 = f32[88,128]{1,0:T(8,128)S(1)} collective-permute-done((f32[88,128]{1,0:T(8,128)S(1)}, f32[88,128]{1,0:T(8,128)S(1)}, u32[]{:S(2)}, u32[]{:S(2)}) %collective-permute-start.8) | collective-permute-done | bytes 45088 | tf_op jit(solution)/shard_map/ppermute | solution.py:460
  56.7 1.6 %collective-permute-start.13 = (f32[88,128]{1,0:T(8,128)S(1)}, f32[88,128]{1,0:T(8,128)S(1)}, u32[]{:S(2)}, u32[]{:S(2)}) collective-permute-start(f32[88,128]{1,0:T(8,128)S(1)} %add_add_fusion.a), channel_id=1, source_target_pairs={{0,8},{1,9},{2,10},{3,11},{4,12},{5,13},{6,14},{7,15},{8,0},{9,1},... | collective-permute-start | bytes 135176 | tf_op jit(solution)/shard_map/ppermute | solution.py:460
  58.4 1.5 %collective-permute-start.12 = (f32[88,128]{1,0:T(8,128)S(1)}, f32[88,128]{1,0:T(8,128)S(1)}, u32[]{:S(2)}, u32[]{:S(2)}) collective-permute-start(f32[88,128]{1,0:T(8,128)S(1)} %add_add_fusion.a), channel_id=1, source_target_pairs={{0,72},{1,73},{2,74},{3,75},{4,76},{5,77},{6,78},{7,79},{8,64},{9,... | collective-permute-start | bytes 135176 | tf_op jit(solution)/shard_map/ppermute | solution.py:460
  59.8 0.5 collective-permute-start.11
  60.3 2.9 %shard_map.98 = f32[3,4,16,512]{3,2,1,0:T(8,128)} custom-call(f32[3,8,40,640]{3,2,1,0:T(8,128)S(1)} %get-tuple-element.27.middle), custom_call_target="tpu_custom_call" | custom-call | flops 3449999872 | bytes 11070000 | tf_op jit(solution)/shard_map/pallas_call | solution.py:415
  63.9 0.8 %shard_map.99 = (f32[64,81]{1,0:T(8,128)}, f32[64,64]{1,0:T(8,128)}, f32[6,64]{1,0:T(8,128)}) custom-call(f32[88,128]{1,0:T(8,128)S(1)} %add_add_fusion.a, f32[88,128]{1,0:T(8,128)S(1)} %collective-permute-done.11.b, f32[88,128]{1,0:T(8,128)S(1)} %collective-permute-done.12.c, f32[88,128]{1,0:T(8,128)S(1)} %collective-permute-done.13.d), custom_call_target="tpu_custom_call" | custom-call | flops 1150000000 | bytes 3690000 | tf_op jit(solution)/shard_map/pallas_call | solution.py:415
  (28 shorter events, 1.5 us)
Async XLA Ops:
  0.6 1.0 %copy-start = (f32[3,4,16,512]{3,2,1,0:T(8,128)S(1)}, f32[3,4,16,512]{3,2,1,0:T(8,128)}, u32[]{:S(2)}) copy-start(f32[3,4,16,512]{3,2,1,0:T(8,128)} %own.9) | copy-start | bytes 1179652
  1.6 4.7 %copy-start.2 = (bf16[64,81]{1,0:T(8,128)(2,1)S(1)}, bf16[64,81]{1,0:T(8,128)(2,1)}, u32[]{:S(2)}) copy-start(bf16[64,81]{1,0:T(8,128)(2,1)} %first.1) | copy-start | bytes 31108
  1.6 4.7 %copy-start.3 = (bf16[64,64]{1,0:T(8,128)(2,1)S(1)}, bf16[64,64]{1,0:T(8,128)(2,1)}, u32[]{:S(2)}) copy-start(bf16[64,64]{1,0:T(8,128)(2,1)} %mid.1) | copy-start | bytes 24580
  1.6 4.7 %copy-start.4 = (bf16[6,64]{1,0:T(8,128)(2,1)S(1)}, bf16[6,64]{1,0:T(8,128)(2,1)}, u32[]{:S(2)}) copy-start(bf16[6,64]{1,0:T(8,128)(2,1)} %last.1) | copy-start | bytes 2308
  1.6 4.7 %copy-start.5 = (s32[4,16]{1,0:T(4,128)S(1)}, s32[4,16]{1,0:T(4,128)}, u32[]{:S(2)}) copy-start(s32[4,16]{1,0:T(4,128)} %offs.5) | copy-start | bytes 772
  1.6 4.7 %copy-start.6 = (bf16[864,216]{1,0:T(8,128)(2,1)S(1)}, bf16[864,216]{1,0:T(8,128)(2,1)}, u32[]{:S(2)}) copy-start(bf16[864,216]{1,0:T(8,128)(2,1)} %constant.2.clone.table) | copy-start | bytes 1119748
  1.7 10.5 %collective-permute-start = (bf16[3,5,16,512]{3,2,1,0:T(8,128)(2,1)S(1)}, bf16[3,5,16,512]{3,2,1,0:T(8,128)(2,1)S(1)}, u32[]{:S(2)}, u32[]{:S(2)}) collective-permute-start(bf16[3,5,16,512]{3,2,1,0:T(8,128)(2,1)S(1)} %get-tuple-element.18), channel_id=1, source_target_pairs={{0,16},{1,17},{2,18},{3,19},{4,20},{5,21},{6,22},{7,23},{8,24},{9,... | collective-permute-start | bytes 737288 | tf_op jit(solution)/shard_map/ppermute | solution.py:460
  3.4 8.7 %collective-permute-start.1 = (bf16[3,5,16,512]{3,2,1,0:T(8,128)(2,1)S(1)}, bf16[3,5,16,512]{3,2,1,0:T(8,128)(2,1)S(1)}, u32[]{:S(2)}, u32[]{:S(2)}) collective-permute-start(bf16[3,5,16,512]{3,2,1,0:T(8,128)(2,1)S(1)} %get-tuple-element.19), channel_id=1, source_target_pairs={{0,112},{1,113},{2,114},{3,115},{4,116},{5,117},{6,118},{7,119},{8... | collective-permute-start | bytes 737288 | tf_op jit(solution)/shard_map/ppermute | solution.py:460
  12.3 10.7 %collective-permute-start.2 = (bf16[3,14,4,512]{3,2,1,0:T(4,128)(2,1)S(1)}, bf16[3,14,4,512]{3,2,1,0:T(4,128)(2,1)S(1)}, u32[]{:S(2)}, u32[]{:S(2)}) collective-permute-start(bf16[3,14,4,512]{3,2,1,0:T(4,128)(2,1)S(1)} %get-tuple-element.23), channel_id=1, source_target_pairs={{0,1},{1,2},{2,3},{3,4},{4,5},{5,6},{6,7},{7,8},{8,9},{9,10},{10,1... | collective-permute-start | bytes 516104 | tf_op jit(solution)/shard_map/ppermute | solution.py:460
  12.4 10.6 %collective-permute-start.3 = (bf16[3,14,4,512]{3,2,1,0:T(4,128)(2,1)S(1)}, bf16[3,14,4,512]{3,2,1,0:T(4,128)(2,1)S(1)}, u32[]{:S(2)}, u32[]{:S(2)}) collective-permute-start(bf16[3,14,4,512]{3,2,1,0:T(4,128)(2,1)S(1)} %get-tuple-element.24), channel_id=1, source_target_pairs={{0,15},{1,0},{2,1},{3,2},{4,3},{5,4},{6,5},{7,6},{8,7},{9,8},{10,9... | collective-permute-start | bytes 516104 | tf_op jit(solution)/shard_map/ppermute | solution.py:460
  17.7 5.3 %copy-start.1 = (f32[3,4,16,512]{3,2,1,0:T(8,128)S(1)}, f32[3,4,16,512]{3,2,1,0:T(8,128)}, u32[]{:S(2)}) copy-start(f32[3,4,16,512]{3,2,1,0:T(8,128)} %own.9) | copy-start | bytes 1179652
  39.4 1.3 %collective-permute-start.4 = (f32[88,128]{1,0:T(8,128)S(1)}, f32[88,128]{1,0:T(8,128)S(1)}, u32[]{:S(2)}, u32[]{:S(2)}) collective-permute-start(f32[88,128]{1,0:T(8,128)S(1)} %get-tuple-element.28), channel_id=1, source_target_pairs={{0,1},{1,0},{2,3},{3,2},{4,5},{5,4},{6,7},{7,6},{8,9},{9,8},{10,11... | collective-permute-start | bytes 135176 | tf_op jit(solution)/shard_map/ppermute | solution.py:460
  40.7 5.7 %collective-permute-start.7 = (f32[88,128]{1,0:T(8,128)S(1)}, f32[88,128]{1,0:T(8,128)S(1)}, u32[]{:S(2)}, u32[]{:S(2)}) collective-permute-start(f32[88,128]{1,0:T(8,128)S(1)} %add.21), channel_id=1, source_target_pairs={{0,32},{1,33},{2,34},{3,35},{4,36},{5,37},{6,38},{7,39},{8,40},{9,... | collective-permute-start | bytes 135176 | tf_op jit(solution)/shard_map/ppermute | solution.py:460
  42.4 5.3 %collective-permute-start.6 = (f32[88,128]{1,0:T(8,128)S(1)}, f32[88,128]{1,0:T(8,128)S(1)}, u32[]{:S(2)}, u32[]{:S(2)}) collective-permute-start(f32[88,128]{1,0:T(8,128)S(1)} %add.21), channel_id=1, source_target_pairs={{0,48},{1,49},{2,50},{3,51},{4,52},{5,53},{6,54},{7,55},{8,56},{9,... | collective-permute-start | bytes 135176 | tf_op jit(solution)/shard_map/ppermute | solution.py:460
  44.7 4.0 %collective-permute-start.5 = (f32[88,128]{1,0:T(8,128)S(1)}, f32[88,128]{1,0:T(8,128)S(1)}, u32[]{:S(2)}, u32[]{:S(2)}) collective-permute-start(f32[88,128]{1,0:T(8,128)S(1)} %add.21), channel_id=1, source_target_pairs={{0,16},{1,17},{2,18},{3,19},{4,20},{5,21},{6,22},{7,23},{8,24},{9,... | collective-permute-start | bytes 135176 | tf_op jit(solution)/shard_map/ppermute | solution.py:460
  48.8 5.6 %collective-permute-start.10 = (f32[88,128]{1,0:T(8,128)S(1)}, f32[88,128]{1,0:T(8,128)S(1)}, u32[]{:S(2)}, u32[]{:S(2)}) collective-permute-start(f32[88,128]{1,0:T(8,128)S(1)} %add_add_fusion.1), channel_id=1, source_target_pairs={{0,4},{1,5},{2,6},{3,7},{4,0},{5,1},{6,2},{7,3},{8,12},{9,13},{10,... | collective-permute-start | bytes 135176 | tf_op jit(solution)/shard_map/ppermute | solution.py:460
  48.9 6.0 %collective-permute-start.9 = (f32[88,128]{1,0:T(8,128)S(1)}, f32[88,128]{1,0:T(8,128)S(1)}, u32[]{:S(2)}, u32[]{:S(2)}) collective-permute-start(f32[88,128]{1,0:T(8,128)S(1)} %add_add_fusion.1), channel_id=1, source_target_pairs={{0,6},{1,7},{2,4},{3,5},{4,2},{5,3},{6,0},{7,1},{8,14},{9,15},{10,... | collective-permute-start | bytes 135176 | tf_op jit(solution)/shard_map/ppermute | solution.py:460
  52.7 4.0 %collective-permute-start.8 = (f32[88,128]{1,0:T(8,128)S(1)}, f32[88,128]{1,0:T(8,128)S(1)}, u32[]{:S(2)}, u32[]{:S(2)}) collective-permute-start(f32[88,128]{1,0:T(8,128)S(1)} %add_add_fusion.1), channel_id=1, source_target_pairs={{0,2},{1,3},{2,0},{3,1},{4,6},{5,7},{6,4},{7,5},{8,10},{9,11},{10,... | collective-permute-start | bytes 135176 | tf_op jit(solution)/shard_map/ppermute | solution.py:460
  56.7 6.5 %collective-permute-start.13 = (f32[88,128]{1,0:T(8,128)S(1)}, f32[88,128]{1,0:T(8,128)S(1)}, u32[]{:S(2)}, u32[]{:S(2)}) collective-permute-start(f32[88,128]{1,0:T(8,128)S(1)} %add_add_fusion.a), channel_id=1, source_target_pairs={{0,8},{1,9},{2,10},{3,11},{4,12},{5,13},{6,14},{7,15},{8,0},{9,1},... | collective-permute-start | bytes 135176 | tf_op jit(solution)/shard_map/ppermute | solution.py:460
  58.4 5.3 %collective-permute-start.12 = (f32[88,128]{1,0:T(8,128)S(1)}, f32[88,128]{1,0:T(8,128)S(1)}, u32[]{:S(2)}, u32[]{:S(2)}) collective-permute-start(f32[88,128]{1,0:T(8,128)S(1)} %add_add_fusion.a), channel_id=1, source_target_pairs={{0,72},{1,73},{2,74},{3,75},{4,76},{5,77},{6,78},{7,79},{8,64},{9,... | collective-permute-start | bytes 135176 | tf_op jit(solution)/shard_map/ppermute | solution.py:460
  59.8 4.0 %collective-permute-start.11 = (f32[88,128]{1,0:T(8,128)S(1)}, f32[88,128]{1,0:T(8,128)S(1)}, u32[]{:S(2)}, u32[]{:S(2)}) collective-permute-start(f32[88,128]{1,0:T(8,128)S(1)} %add_add_fusion.a), channel_id=1, source_target_pairs={{0,64},{1,65},{2,66},{3,67},{4,68},{5,69},{6,70},{7,71},{8,72},{9,... | collective-permute-start | bytes 135176 | tf_op jit(solution)/shard_map/ppermute | solution.py:460

commit v4 on v3

--- a/solution.py
+++ b/solution.py
@@ -8,13 +8,13 @@
 
 f32, bf16 = jnp.float32, jnp.bfloat16
 AXES = ("px", "py")
-LANES = 640
+LANES = 512
 ROWS = 40
 NT = (((1,), (1,)), ((), ()))
 
 
 def selections():
-    table = np.zeros((864, 216), np.float32)
+    table = np.zeros((960, 216), np.float32)
     for y in range(16):
         for c in range(3):
             for ox in range(3):
@@ -26,6 +26,8 @@
         for c in range(3):
             for o in range(9):
                 table[768 + c * 27 + o * 3 + oz, oz * 32 + c * 9 + o] = 1
+    table[864:928] = table[np.r_[0:32, 480:512]]
+    table[928:960] = table[np.r_[512:528, 752:768]]
     return table
 
 
@@ -33,9 +35,6 @@
     def __init__(self, ref, first, last, lanes):
         self.ref, self.first, self.last, self.lanes = ref, first, last, lanes
 
-    def rows(self, first, last):
-        return self.ref[self.first + first : self.first + last, 0 : self.lanes]
-
     def __getitem__(self, _):
         return self.ref[self.first : self.last, 0 : self.lanes]
 
@@ -47,9 +46,13 @@
     return Part(table, 0, 512, 216), Part(table, 512, 768, 96), Part(table, 768, 849, 96)
 
 
+def edge_parts(table):
+    return Part(table, 864, 928, 216), Part(table, 928, 960, 96)
+
+
 def weight_parts(packed):
-    return (Part(packed, 0, 64, 96), Part(packed, 64, 128, 64), Part(packed, 128, 192, 64),
-            Part(packed, 192, 208, 80), Part(packed, 208, 272, 16))
+    return (Part(packed, 0, 64, 96), Part(packed, 64, 192, 128), Part(packed, 192, 320, 128),
+            Part(packed, 320, 352, 128), Part(packed, 352, 480, 32))
 
 
 def total_parts(packed):
@@ -64,8 +67,18 @@
     return lax.dot_general(a, b, NT, preferred_element_type=f32)
 
 
-def shift_z(value):
-    return pltpu.roll(value, LANES - 1, 1) - pltpu.roll(value, 1, 1)
+def shift_z(value, below=0.0, above=0.0):
+    up, down = pltpu.roll(value, LANES - 1, 1), pltpu.roll(value, 1, 1)
+    lane = lax.broadcasted_iota(jnp.int32, (8, 128), 1)
+    first = up[:, :128] - jnp.where(lane == 0, below, down[:, :128])
+    last = jnp.where(lane == 127, above, up[:, 384:]) - down[:, 384:]
+    return jnp.concatenate([first, up[:, 128:384] - down[:, 128:384], last], 1)
+
+
+def wall_stress(velocity):
+    x, y, z = velocity
+    nu = 0.05 + 0.04 * jnp.sqrt(0.5 * z * z + 0.25 * (x * x + y * y))
+    return {4: -0.5 * nu * x, 5: -0.5 * nu * y, 2: -nu * z}
 
 
 def differences(field, plane, row):
@@ -102,8 +115,11 @@
     def tau_y(c):
         return tau[c, tau_plane, pl.ds(row + 1, 8), :] - tau[c, tau_plane, pl.ds(row - 1, 8), :]
 
+    below = wall_stress([value[:, :128] for value in center])
+    above = wall_stress([-value[:, 384:] for value in center])
+
     def tau_z(c):
-        return shift_z(tau[c, tau_plane, here, :])
+        return shift_z(tau[c, tau_plane, here, :], below[c], above[c])
 
     parts = ((0, 3, 4), (3, 1, 5), (4, 5, 2))
     out = []
@@ -128,9 +144,10 @@
         columns.append(jnp.concatenate([window[:, 0:256], window[:, 1:257], window[:, 2:258]], 0))
         target = pltpu.roll(tile_target[n * 16 : n * 16 + 16, pl.ds(base_lane, 512)], turn, 1)
         targets.append(target[:, 1:257])
-    cols = jnp.concatenate(columns, 1)
-    target = jnp.concatenate(targets, 1)
-    h1 = dot(w1[...], cols)
+    half = len(starts) // 2
+    cols = [jnp.concatenate(columns[:half], 1), jnp.concatenate(columns[half:], 1)]
+    target = jnp.concatenate([jnp.concatenate(targets[:half], 1), jnp.concatenate(targets[half:], 1)], 0)
+    h1 = jnp.concatenate([dot(w1[...], cols[0]), dot(w1[...], cols[1])], 0)
     t1 = jnp.tanh(h1)
     q1 = h1 * t1
     a1 = (h1 + q1).astype(bf16)
@@ -140,12 +157,18 @@
     q2 = h2 * t2
     a2 = (h2 + q2).astype(bf16)
     s2 = (1.0 + t2) * (1.0 + (h2 - q2))
-    misfit = dot(w3[...], jnp.concatenate([a2, target], 0)).astype(bf16)
+    misfit = (dot(w3[...], a2) - target.astype(f32)).astype(bf16)
     b2 = (dot(w3t[...], misfit) * s2).astype(bf16)
     b1 = (dot(w2t[...], b2) * s1).astype(bf16)
-    g3[...] += dot_cells(misfit, a2)
-    g2[...] += dot_cells(b2, a1)
-    g1[...] += dot_cells(b1, cols)
+    g3[...] += dot_cells(side_by_side(misfit), side_by_side(a2))
+    both = dot_cells(b2, a1)
+    g2[...] += both[0:64, 0:64] + both[64:128, 64:128]
+    g1[...] += dot_cells(side_by_side(b1), jnp.concatenate(cols, 1))
+
+
+def side_by_side(value):
+    half = value.shape[0] // 2
+    return jnp.concatenate([value[:half], value[half:]], 1)
 
 
 def input_rows(field, plane):
@@ -169,13 +192,16 @@
 
 
 def clear_rest(field):
-    beyond = jnp.zeros((ROWS, 128), f32)
     strip = jnp.zeros((8, LANES), f32)
     for c in range(3):
         for p in range(field.shape[1]):
-            field[c, p, :, 512:640] = beyond
             field[c, p, 4:12, :] = strip
             field[c, p, 28:36, :] = strip
+
+
+def twice(block):
+    zero = jnp.zeros_like(block)
+    return jnp.concatenate([jnp.concatenate([block, zero], 1), jnp.concatenate([zero, block], 1)], 0)
 
 
 def interior_kernel(
@@ -200,13 +226,11 @@
     rows, cols = lax.broadcasted_iota(jnp.int32, (64, 64), 0), lax.broadcasted_iota(jnp.int32, (64, 64), 1)
     half = jnp.where(rows == cols, 0.5, 0.0).astype(bf16)
     w1[...] = (0.5 * dot(first[...], order[...])).astype(bf16)
-    w2[...] = (0.5 * mid[...].astype(f32)).astype(bf16)
-    w2t[...] = dot_cells(half, mid[...]).astype(bf16)
-    rows, cols = lax.broadcasted_iota(jnp.int32, (16, 16), 0), lax.broadcasted_iota(jnp.int32, (16, 16), 1)
-    minus = jnp.where(rows == cols, -1.0, 0.0)
+    w2[...] = twice(0.5 * mid[...].astype(f32)).astype(bf16)
+    w2t[...] = twice(dot_cells(half, mid[...])).astype(bf16)
     last_rows = jnp.concatenate([last[...].astype(f32), jnp.zeros((10, 64), f32)], 0)
-    w3[...] = jnp.concatenate([last_rows, minus], 1).astype(bf16)
-    w3t[...] = dot_cells(half, last_rows.astype(bf16)).astype(bf16)
+    w3[...] = twice(last_rows).astype(bf16)
+    w3t[...] = twice(dot_cells(half, last_rows.astype(bf16))).astype(bf16)
     packed_totals[...] = jnp.zeros_like(packed_totals)
 
     def step(n, _):
@@ -227,40 +251,61 @@
     return high, (value - high.astype(f32)).astype(bf16)
 
 
-def pack_x_kernel(own, up, down):
-    for c in range(3):
-        for x in range(4):
-            high, rest = split_bf16(own[c, x])
-            up[c, x] = high
-            down[c, x + 1] = high
-            if x == 3:
-                up[c, 4] = rest
-            if x == 0:
-                down[c, 0] = rest
-
-
-def pack_y_kernel(own, x_low, x_high, right, left):
-    for c in range(3):
-        for out, first, near in ((right, 12, 15), (left, 0, 0)):
-            rests = []
-            for p in range(12):
-                if p < 4:
-                    high = x_low[c, p].astype(f32)
-                elif p < 8:
-                    high, rest = split_bf16(own[c, p - 4])
-                    high, rest = high.astype(f32), rest.astype(f32)
-                else:
-                    high = x_high[c, p - 7].astype(f32)
-                if p == 3:
-                    rest = x_low[c, 4].astype(f32)
-                if p == 8:
-                    rest = x_high[c, 0].astype(f32)
-                out[c, p] = high[first : first + 4, :].astype(bf16)
-                if 3 <= p <= 8:
-                    rests.append(rest[near : near + 1, :])
-            rests = jnp.concatenate(rests + [jnp.zeros((2, 512), f32)], 0)
-            out[c, 12] = rests[0:4].astype(bf16)
-            out[c, 13] = rests[4:8].astype(bf16)
+def in_order(axis, step, first, second):
+    odd = lax.axis_index(axis) % 2
+
+    @pl.when(odd == 1)
+    def _():
+        step(first, second)
+
+    @pl.when(odd == 0)
+    def _():
+        step(second, first)
+
+
+def pack_x_kernel(own, first, second):
+    def pack(down, up):
+        for c in range(3):
+            for x in range(4):
+                high, rest = split_bf16(own[c, x])
+                up[c, x] = high
+                down[c, x + 1] = high
+                if x == 3:
+                    up[c, 4] = rest
+                if x == 0:
+                    down[c, 0] = rest
+
+    in_order("px", pack, first, second)
+
+
+def pack_y_kernel(own, x_first, x_second, first, second):
+    def pack(x_low, x_high, left, right):
+        for c in range(3):
+            for out, start, near in ((right, 12, 15), (left, 0, 0)):
+                rests = []
+                for p in range(12):
+                    if p < 4:
+                        high = x_low[c, p].astype(f32)
+                    elif p < 8:
+                        high, rest = split_bf16(own[c, p - 4])
+                        high, rest = high.astype(f32), rest.astype(f32)
+                    else:
+                        high = x_high[c, p - 7].astype(f32)
+                    if p == 3:
+                        rest = x_low[c, 4].astype(f32)
+                    if p == 8:
+                        rest = x_high[c, 0].astype(f32)
+                    out[c, p] = high[start : start + 4, :].astype(bf16)
+                    if 3 <= p <= 8:
+                        rests.append(rest[near : near + 1, :])
+                rests = jnp.concatenate(rests + [jnp.zeros((2, 512), f32)], 0)
+                out[c, 12] = rests[0:4].astype(bf16)
+                out[c, 13] = rests[4:8].astype(bf16)
+
+    def with_x(x_low, x_high):
+        in_order("py", lambda left, right: pack(x_low, x_high, left, right), first, second)
+
+    in_order("px", with_x, x_first, x_second)
 
 
 def x_plane(x_low, own, x_high, c, p):
@@ -274,7 +319,7 @@
 
 
 def side_kernel(
-    offs, own, x_low, x_high, packed_weights, before, table, packed_totals, field, tau, tile, tile_target,
+    offs, own, x_first, x_second, packed_weights, before, table, packed_totals, field, tau, tile, tile_target,
     local_table, sems,
 ):
     copy = pltpu.make_async_copy(table, local_table, sems.at[0])
@@ -284,9 +329,13 @@
     packed_totals[...] = before[...]
     clear_edges(tile, tile_target)
     clear_rest(field)
-    for c in range(3):
-        for p in range(6):
-            field[c, p, 12:28, 0:512] = x_plane(x_low, own, x_high, c, p + 3)
+
+    def place(x_low, x_high):
+        for c in range(3):
+            for p in range(6):
+                field[c, p, 12:28, 0:512] = x_plane(x_low, own, x_high, c, p + 3)
+
+    in_order("px", place, x_first, x_second)
     copy.wait()
 
     def step(n, _):
@@ -303,7 +352,7 @@
 
 
 def middle_kernel(
-    offs, own, x_low, x_high, y_low, y_high,
+    offs, own, x_first, x_second, y_first, y_second,
     packed_weights, before, table, middle, packed, field, tau, tile, tile_target,
     local_table, sems, packed_totals,
 ):
@@ -312,6 +361,7 @@
     pick, pick_target, order = table_parts(local_table)
     weights, totals = weight_parts(packed_weights), total_parts(packed_totals)
     packed_totals[...] = before[...]
+    edges, edges_target = edge_parts(local_table)
     g1, g2, g3 = totals
     clear_edges(tile, tile_target)
     clear_rest(field)
@@ -320,42 +370,45 @@
         for p in range(10):
             tau[c, p, 7:8, :] = line
             tau[c, p, 32:33, :] = line
-    for c in range(3):
-        for p in range(12):
-            field[c, p, 12:28, 0:512] = x_plane(x_low, own, x_high, c, p)
-            low, high = y_low[c, p].astype(f32), y_high[c, p].astype(f32)
-            field[c, p, 8:12, 0:512] = low
-            field[c, p, 28:32, 0:512] = high
-            if 3 <= p <= 8:
-                k, r = 12 + (p - 3) // 4, (p - 3) % 4
-                field[c, p, 11:12, 0:512] = low[3:4] + y_low[c, k].astype(f32)[r : r + 1]
-                field[c, p, 28:29, 0:512] = high[0:1] + y_high[c, k].astype(f32)[r : r + 1]
+    def place_x(x_low, x_high):
+        for c in range(3):
+            for p in range(12):
+                field[c, p, 12:28, 0:512] = x_plane(x_low, own, x_high, c, p)
+
+    def place_y(y_low, y_high):
+        for c in range(3):
+            for p in range(12):
+                low, high = y_low[c, p].astype(f32), y_high[c, p].astype(f32)
+                field[c, p, 8:12, 0:512] = low
+                field[c, p, 28:32, 0:512] = high
+                if 3 <= p <= 8:
+                    k, r = 12 + (p - 3) // 4, (p - 3) % 4
+                    field[c, p, 11:12, 0:512] = low[3:4] + y_low[c, k].astype(f32)[r : r + 1]
+                    field[c, p, 28:29, 0:512] = high[0:1] + y_high[c, k].astype(f32)[r : r + 1]
+
+    in_order("px", place_x, x_first, x_second)
+    in_order("py", place_y, y_first, y_second)
 
     def stress_zero(p, _):
         for row in (8, 16, 24):
             stress_rows(field, p + 1, tau, p, row)
         return 0
 
-    lax.fori_loop(0, 10, stress_zero, 0)
-    inside = lax.broadcasted_iota(jnp.int32, (8, LANES), 1) < 512
+    lax.fori_loop(0, 10, stress_zero, 0, unroll=5)
 
     def advance_middle(p, _):
         for row in (8, 16, 24):
             new = step_rows(field, p + 2, tau, p + 1, row)
             for c in range(3):
-                middle[c, p, pl.ds(row, 8), :] = jnp.where(inside, new[c], 0.0)
-        return 0
-
-    lax.fori_loop(0, 8, advance_middle, 0)
+                middle[c, p, pl.ds(row, 8), :] = new[c]
+        return 0
+
+    lax.fori_loop(0, 8, advance_middle, 0, unroll=4)
     copy.wait()
 
     def step(x, _):
-        rows = input_rows(field, x + 4)
-        gather(tile, 512, pick.rows(0, 32), rows)
-        gather(tile, 544, pick.rows(480, 512), rows)
-        rows = target_rows(tau, x + 3)
-        gather(tile_target, 256, pick_target.rows(0, 16), rows)
-        gather(tile_target, 272, pick_target.rows(240, 256), rows)
+        gather(tile, 512, edges[...], input_rows(field, x + 4))
+        gather(tile_target, 256, edges_target[...], target_rows(tau, x + 3))
         for row in (12, 20):
             stress_rows(middle, x + 2, tau, 0, row)
         gather(tile, 0, pick[...], input_rows(middle, x + 2))
@@ -381,16 +434,16 @@
             stress_rows(middle, p + 1, tau, p, row)
         return 0
 
-    lax.fori_loop(0, 6, stress_one, 0)
+    lax.fori_loop(0, 6, stress_one, 0, unroll=3)
 
     def advance_final(p, _):
         for row in (12, 20):
             new = step_rows(middle, p + 2, tau, p + 1, row)
             for c in range(3):
-                final[c, p, row - 12 : row - 4, :] = new[c][:, 0:512]
-        return 0
-
-    lax.fori_loop(0, 4, advance_final, 0)
+                final[c, p, row - 12 : row - 4, :] = new[c]
+        return 0
+
+    lax.fori_loop(0, 4, advance_final, 0, unroll=2)
 
 
 def last_sum_kernel(a, b, c, d, first, mid, last):
@@ -405,7 +458,7 @@
     return jax.ShapeDtypeStruct(dims, kind)
 
 
-WEIGHTS, TOTALS = shaped(272, 128, kind=bf16), shaped(144, 128)
+WEIGHTS, TOTALS = shaped(480, 128, kind=bf16), shaped(144, 128)
 
 
 def call(kernel, args, out_shape, scratch, smem=0, us=1, mib=16, hbm=0):
@@ -429,7 +482,7 @@
         pltpu.VMEM((6, stress_planes, ROWS, LANES), f32),
         pltpu.VMEM((32 * columns, 768), bf16),
         pltpu.VMEM((16 * columns, 768), bf16),
-        pltpu.VMEM((864, 216), bf16),
+        pltpu.VMEM((960, 216), bf16),
     ]
 
 
@@ -462,10 +515,10 @@
 
 def body(velocity, first_weight, mid_weight, last_weight, offsets):
     table = jnp.asarray(selections(), bf16)
-    up, down = lambda i, j: (i + 1, j), lambda i, j: (i - 1, j)
-    right, left = lambda i, j: (i, j + 1), lambda i, j: (i, j - 1)
-    to_up, to_down = call(pack_x_kernel, (velocity,), [shaped(3, 5, 16, 512, kind=bf16)] * 2, [])
-    x_low, x_high = send(to_up, up), send(to_down, down)
+    near_x, far_x = lambda i, j: (i ^ 1, j), lambda i, j: (i + 2 * (i % 2) - 1, j)
+    near_y, far_y = lambda i, j: (i, j ^ 1), lambda i, j: (i, j + 2 * (j % 2) - 1)
+    to_near, to_far = call(pack_x_kernel, (velocity,), [shaped(3, 5, 16, 512, kind=bf16)] * 2, [])
+    x_first, x_second = send(to_near, near_x), send(to_far, far_x)
     weights, totals = call(
         interior_kernel,
         (offsets, velocity, first_weight, mid_weight, last_weight, table),
@@ -473,25 +526,25 @@
         + [pltpu.VMEM(n, bf16) for n in ((64, 81), (64, 64), (6, 64))] + [pltpu.SemaphoreType.DMA((4,))],
         1, 6, 16, 4,
     )
-    x_low, x_high, totals = lax.optimization_barrier((x_low, x_high, totals))
-    to_right, to_left = call(
-        pack_y_kernel, (velocity, x_low, x_high), [shaped(3, 14, 4, 512, kind=bf16)] * 2, []
+    x_first, x_second, totals = lax.optimization_barrier((x_first, x_second, totals))
+    to_near, to_far = call(
+        pack_y_kernel, (velocity, x_first, x_second), [shaped(3, 14, 4, 512, kind=bf16)] * 2, []
     )
-    y_low, y_high = send(to_right, right), send(to_left, left)
+    y_first, y_second = send(to_near, near_y), send(to_far, far_y)
     (totals,) = call(
         side_kernel,
-        (offsets, velocity, x_low, x_high, weights, totals, table),
+        (offsets, velocity, x_first, x_second, weights, totals, table),
         [TOTALS], columns_scratch(6, 1, 16) + [pltpu.SemaphoreType.DMA((1,))], 1, 6, 16, 1,
     )
     middle, packed = call(
         middle_kernel,
-        (offsets, velocity, x_low, x_high, y_low, y_high, weights, totals, table),
+        (offsets, velocity, x_first, x_second, y_first, y_second, weights, totals, table),
         [shaped(3, 8, ROWS, LANES), shaped(88, 128)],
         columns_scratch(12, 10, 18) + [pltpu.SemaphoreType.DMA((1,)), pltpu.VMEM(TOTALS.shape, f32)], 1, 16, 32, 1,
     )
     (final,) = call(final_kernel, (middle,), [shaped(3, 4, 16, 512)], [pltpu.VMEM((6, 6, ROWS, LANES), f32)], 0, 3)
 
-    packed = packed + send(packed, lambda i, j: (i, j ^ 1))
+    packed = packed + send(packed, near_y)
     for along in (along_y, along_x):
         a, b, c = (send(packed, along(turn)) for turn in EXCHANGES)
         packed = (packed + a) + (b + c)

time: 64.8 us -> 61.6 us (0.951)
  Pallas kernels: 30.9 us -> 28.4 us
    pallas_call x7, Pallas kernels: 30.9 us -> 28.4 us  [call(): pl.pallas_call(kernel, in_specs=[scalar] * smem + [vmem] * (len(args) - s...]
  transfers between devices with their start and end apart: 14 -> 14, of which waited for: 10 -> 9; matrix products, arithmetic and copies ran while one was open for 0% -> 0% of each run, Pallas kernels for 21% -> 21%
where the time goes in v4:
time: 61.6 us; the launch traced here: 61.4 us
  Pallas kernels  28.4 us (46%)
  starting transfers between devices  22.7 us (37%)
  waiting for transfers between devices  8.41 us (14%)
  local copies, waits for them, and re-layouts  1.02 us (2%)
  between operations  0.77 us (1%)
    pallas_call x7, Pallas kernels, call(): pl.pallas_call(kernel, in_specs=[scalar] * smem + [vmem] * (len(args) - s...  28.4 us
    ppermute x14, starting transfers between devices, send(): return lax.ppermute(value, AXES, pairs(move))  22.7 us
    ppermute x14, waiting for transfers between devices, send(): return lax.ppermute(value, AXES, pairs(move))  8.41 us
  transfers between devices with their start and end apart: 14, of which 9 were waited for; matrix products, arithmetic and copies ran while one was open for 0% of the time, Pallas kernels for 21%

profile of v4, /device:TPU:0, one launch (start us, length us, event | category | flops | bytes accessed | tf_op | source)
XLA Modules:
  0.0 61.4 jit_solution(15427858980831092045)
XLA Ops:
  0.6 1.0 %copy-done = f32[3,4,16,512]{3,2,1,0:T(8,128)S(1)} copy-done((f32[3,4,16,512]{3,2,1,0:T(8,128)S(1)}, f32[3,4,16,512]{3,2,1,0:T(8,128)}, u32[]{:S(2)}) %copy-start) | copy-done | bytes 393240
  1.7 1.7 %collective-permute-start = (bf16[3,5,16,512]{3,2,1,0:T(8,128)(2,1)S(1)}, bf16[3,5,16,512]{3,2,1,0:T(8,128)(2,1)S(1)}, u32[]{:S(2)}, u32[]{:S(2)}) collective-permute-start(bf16[3,5,16,512]{3,2,1,0:T(8,128)(2,1)S(1)} %get-tuple-element.18), channel_id=1, source_target_pairs={{0,16},{1,17},{2,18},{3,19},{4,20},{5,21},{6,22},{7,23},{8,24},{9,... | collective-permute-start | bytes 737288 | tf_op jit(solution)/shard_map/ppermute | solution.py:513
  3.5 3.5 %collective-permute-start.1 = (bf16[3,5,16,512]{3,2,1,0:T(8,128)(2,1)S(1)}, bf16[3,5,16,512]{3,2,1,0:T(8,128)(2,1)S(1)}, u32[]{:S(2)}, u32[]{:S(2)}) collective-permute-start(bf16[3,5,16,512]{3,2,1,0:T(8,128)(2,1)S(1)} %get-tuple-element.19), channel_id=1, source_target_pairs={{0,112},{1,113},{2,114},{3,115},{4,116},{5,117},{6,118},{7,119},{8... | collective-permute-start | bytes 737288 | tf_op jit(solution)/shard_map/ppermute | solution.py:513
  7.0 5.4 %shard_map.94 = (bf16[480,128]{1,0:T(8,128)(2,1)S(1)}, f32[144,128]{1,0:T(8,128)S(1)}) custom-call(s32[4,16]{1,0:T(4,128)S(1)} %copy-done.5, f32[3,4,16,512]{3,2,1,0:T(8,128)S(1)} %copy-done, bf16[64,81]{1,0:T(8,128)(2,1)S(1)} %copy-done.2, bf16[64,64]{1,0:T(8,128)(2,1)S(1)} %copy-done.3, bf16[6,64]{1,0:T(8,128)(2,1)S(1)} %copy-done.4, ...), custom_call_target="tpu_custom_call" | custom-call | flops 6899999744 | bytes 22140000 | tf_op jit(solution)/shard_map/pallas_call | solution.py:468
  12.5 0.5 collective-permute-done.1.x_second
  13.2 6.2 %collective-permute-start.3 = (bf16[3,14,4,512]{3,2,1,0:T(4,128)(2,1)S(1)}, bf16[3,14,4,512]{3,2,1,0:T(4,128)(2,1)S(1)}, u32[]{:S(2)}, u32[]{:S(2)}) collective-permute-start(bf16[3,14,4,512]{3,2,1,0:T(4,128)(2,1)S(1)} %get-tuple-element.24), channel_id=1, source_target_pairs={{0,15},{1,2},{2,1},{3,4},{4,3},{5,6},{6,5},{7,8},{8,7},{9,10},{10,... | collective-permute-start | bytes 516104 | tf_op jit(solution)/shard_map/ppermute | solution.py:513
  19.4 5.2 %shard_map.96.before = f32[144,128]{1,0:T(8,128)S(1)} custom-call(s32[4,16]{1,0:T(4,128)S(1)} %copy-done.5, f32[3,4,16,512]{3,2,1,0:T(8,128)S(1)} %copy-done, bf16[3,5,16,512]{3,2,1,0:T(8,128)(2,1)S(1)} %collective-permute-done.x_first, bf16[3,5,16,512]{3,2,1,0:T(8,128)(2,1)S(1)} %collective-permute-done.1.x_second, ...), custom_call_target="tpu_custom_call" | custom-call | flops 6899999744 | bytes 22140000 | tf_op jit(solution)/shard_map/pallas_call | solution.py:468
  24.6 14.3 %shard_map.97 = (f32[3,8,40,512]{3,2,1,0:T(8,128)S(1)}, f32[88,128]{1,0:T(8,128)S(1)}) custom-call(s32[4,16]{1,0:T(4,128)S(1)} %copy-done.5, f32[3,4,16,512]{3,2,1,0:T(8,128)S(1)} %copy-done.1, bf16[3,5,16,512]{3,2,1,0:T(8,128)(2,1)S(1)} %collective-permute-done.x_first, bf16[3,5,16,512]{3,2,1,0:T(8,128)(2,1)S(1)} %collective-permute-done.1.x_second, ...), custom_call_target="tpu_custom_call" | custom-call | flops 18400000000 | bytes 59040000 | tf_op jit(solution)/shard_map/pallas_call | solution.py:468
  39.0 1.2 %collective-permute-done.4 = f32[88,128]{1,0:T(8,128)S(1)} collective-permute-done((f32[88,128]{1,0:T(8,128)S(1)}, f32[88,128]{1,0:T(8,128)S(1)}, u32[]{:S(2)}, u32[]{:S(2)}) %collective-permute-start.4) | collective-permute-done | bytes 45088 | tf_op jit(solution)/shard_map/ppermute | solution.py:513
  40.3 0.9 %collective-permute-start.7 = (f32[88,128]{1,0:T(8,128)S(1)}, f32[88,128]{1,0:T(8,128)S(1)}, u32[]{:S(2)}, u32[]{:S(2)}) collective-permute-start(f32[88,128]{1,0:T(8,128)S(1)} %add.21), channel_id=1, source_target_pairs={{0,32},{1,33},{2,34},{3,35},{4,36},{5,37},{6,38},{7,39},{8,40},{9,... | collective-permute-start | bytes 135176 | tf_op jit(solution)/shard_map/ppermute | solution.py:513
  41.1 1.5 %collective-permute-start.6 = (f32[88,128]{1,0:T(8,128)S(1)}, f32[88,128]{1,0:T(8,128)S(1)}, u32[]{:S(2)}, u32[]{:S(2)}) collective-permute-start(f32[88,128]{1,0:T(8,128)S(1)} %add.21), channel_id=1, source_target_pairs={{0,48},{1,49},{2,50},{3,51},{4,52},{5,53},{6,54},{7,55},{8,56},{9,... | collective-permute-start | bytes 135176 | tf_op jit(solution)/shard_map/ppermute | solution.py:513
  42.6 1.2 %collective-permute-start.5 = (f32[88,128]{1,0:T(8,128)S(1)}, f32[88,128]{1,0:T(8,128)S(1)}, u32[]{:S(2)}, u32[]{:S(2)}) collective-permute-start(f32[88,128]{1,0:T(8,128)S(1)} %add.21), channel_id=1, source_target_pairs={{0,16},{1,17},{2,18},{3,19},{4,20},{5,21},{6,22},{7,23},{8,24},{9,... | collective-permute-start | bytes 135176 | tf_op jit(solution)/shard_map/ppermute | solution.py:513
  43.8 2.1 %collective-permute-done.7 = f32[88,128]{1,0:T(8,128)S(1)} collective-permute-done((f32[88,128]{1,0:T(8,128)S(1)}, f32[88,128]{1,0:T(8,128)S(1)}, u32[]{:S(2)}, u32[]{:S(2)}) %collective-permute-start.7) | collective-permute-done | bytes 45088 | tf_op jit(solution)/shard_map/ppermute | solution.py:513
  45.9 0.5 collective-permute-done.6
  46.7 0.3 collective-permute-start.10
  46.9 0.4 collective-permute-start.9
  47.3 3.1 %collective-permute-start.8 = (f32[88,128]{1,0:T(8,128)S(1)}, f32[88,128]{1,0:T(8,128)S(1)}, u32[]{:S(2)}, u32[]{:S(2)}) collective-permute-start(f32[88,128]{1,0:T(8,128)S(1)} %add_add_fusion.1), channel_id=1, source_target_pairs={{0,2},{1,3},{2,0},{3,1},{4,6},{5,7},{6,4},{7,5},{8,10},{9,11},{10,... | collective-permute-start | bytes 135176 | tf_op jit(solution)/shard_map/ppermute | solution.py:513
  50.4 2.1 %collective-permute-done.10 = f32[88,128]{1,0:T(8,128)S(1)} collective-permute-done((f32[88,128]{1,0:T(8,128)S(1)}, f32[88,128]{1,0:T(8,128)S(1)}, u32[]{:S(2)}, u32[]{:S(2)}) %collective-permute-start.10) | collective-permute-done | bytes 45088 | tf_op jit(solution)/shard_map/ppermute | solution.py:513
  52.8 2.3 %collective-permute-start.13 = (f32[88,128]{1,0:T(8,128)S(1)}, f32[88,128]{1,0:T(8,128)S(1)}, u32[]{:S(2)}, u32[]{:S(2)}) collective-permute-start(f32[88,128]{1,0:T(8,128)S(1)} %add_add_fusion.a), channel_id=1, source_target_pairs={{0,8},{1,9},{2,10},{3,11},{4,12},{5,13},{6,14},{7,15},{8,0},{9,1},... | collective-permute-start | bytes 135176 | tf_op jit(solution)/shard_map/ppermute | solution.py:513
  55.0 1.5 %collective-permute-start.12 = (f32[88,128]{1,0:T(8,128)S(1)}, f32[88,128]{1,0:T(8,128)S(1)}, u32[]{:S(2)}, u32[]{:S(2)}) collective-permute-start(f32[88,128]{1,0:T(8,128)S(1)} %add_add_fusion.a), channel_id=1, source_target_pairs={{0,72},{1,73},{2,74},{3,75},{4,76},{5,77},{6,78},{7,79},{8,64},{9,... | collective-permute-start | bytes 135176 | tf_op jit(solution)/shard_map/ppermute | solution.py:513
  56.6 2.5 %shard_map.98 = f32[3,4,16,512]{3,2,1,0:T(8,128)} custom-call(f32[3,8,40,512]{3,2,1,0:T(8,128)S(1)} %get-tuple-element.27.middle), custom_call_target="tpu_custom_call" | custom-call | flops 3449999872 | bytes 11070000 | tf_op jit(solution)/shard_map/pallas_call | solution.py:468
  59.1 1.2 %collective-permute-done.12.c = f32[88,128]{1,0:T(8,128)S(1)} collective-permute-done((f32[88,128]{1,0:T(8,128)S(1)}, f32[88,128]{1,0:T(8,128)S(1)}, u32[]{:S(2)}, u32[]{:S(2)}) %collective-permute-start.12) | collective-permute-done | bytes 45088 | tf_op jit(solution)/shard_map/ppermute | solution.py:513
  60.3 0.3 collective-permute-done.11.b
  60.6 0.8 %shard_map.99 = (f32[64,81]{1,0:T(8,128)}, f32[64,64]{1,0:T(8,128)}, f32[6,64]{1,0:T(8,128)}) custom-call(f32[88,128]{1,0:T(8,128)S(1)} %add_add_fusion.a, f32[88,128]{1,0:T(8,128)S(1)} %collective-permute-done.11.b, f32[88,128]{1,0:T(8,128)S(1)} %collective-permute-done.12.c, f32[88,128]{1,0:T(8,128)S(1)} %collective-permute-done.13.d), custom_call_target="tpu_custom_call" | custom-call | flops 1150000000 | bytes 3690000 | tf_op jit(solution)/shard_map/pallas_call | solution.py:468
  (28 shorter events, 0.9 us)
Async XLA Ops:
  0.6 1.0 %copy-start = (f32[3,4,16,512]{3,2,1,0:T(8,128)S(1)}, f32[3,4,16,512]{3,2,1,0:T(8,128)}, u32[]{:S(2)}) copy-start(f32[3,4,16,512]{3,2,1,0:T(8,128)} %own.9) | copy-start | bytes 1179652
  1.6 5.4 %copy-start.2 = (bf16[64,81]{1,0:T(8,128)(2,1)S(1)}, bf16[64,81]{1,0:T(8,128)(2,1)}, u32[]{:S(2)}) copy-start(bf16[64,81]{1,0:T(8,128)(2,1)} %first.1) | copy-start | bytes 31108
  1.6 5.4 %copy-start.3 = (bf16[64,64]{1,0:T(8,128)(2,1)S(1)}, bf16[64,64]{1,0:T(8,128)(2,1)}, u32[]{:S(2)}) copy-start(bf16[64,64]{1,0:T(8,128)(2,1)} %mid.1) | copy-start | bytes 24580
  1.6 5.4 %copy-start.4 = (bf16[6,64]{1,0:T(8,128)(2,1)S(1)}, bf16[6,64]{1,0:T(8,128)(2,1)}, u32[]{:S(2)}) copy-start(bf16[6,64]{1,0:T(8,128)(2,1)} %last.1) | copy-start | bytes 2308
  1.6 5.4 %copy-start.5 = (s32[4,16]{1,0:T(4,128)S(1)}, s32[4,16]{1,0:T(4,128)}, u32[]{:S(2)}) copy-start(s32[4,16]{1,0:T(4,128)} %offs.5) | copy-start | bytes 772
  1.6 5.4 %copy-start.6 = (bf16[960,216]{1,0:T(8,128)(2,1)S(1)}, bf16[960,216]{1,0:T(8,128)(2,1)}, u32[]{:S(2)}) copy-start(bf16[960,216]{1,0:T(8,128)(2,1)} %constant.2.clone.table) | copy-start | bytes 1244164
  1.7 10.7 %collective-permute-start = (bf16[3,5,16,512]{3,2,1,0:T(8,128)(2,1)S(1)}, bf16[3,5,16,512]{3,2,1,0:T(8,128)(2,1)S(1)}, u32[]{:S(2)}, u32[]{:S(2)}) collective-permute-start(bf16[3,5,16,512]{3,2,1,0:T(8,128)(2,1)S(1)} %get-tuple-element.18), channel_id=1, source_target_pairs={{0,16},{1,17},{2,18},{3,19},{4,20},{5,21},{6,22},{7,23},{8,24},{9,... | collective-permute-start | bytes 737288 | tf_op jit(solution)/shard_map/ppermute | solution.py:513
  3.5 9.5 %collective-permute-start.1 = (bf16[3,5,16,512]{3,2,1,0:T(8,128)(2,1)S(1)}, bf16[3,5,16,512]{3,2,1,0:T(8,128)(2,1)S(1)}, u32[]{:S(2)}, u32[]{:S(2)}) collective-permute-start(bf16[3,5,16,512]{3,2,1,0:T(8,128)(2,1)S(1)} %get-tuple-element.19), channel_id=1, source_target_pairs={{0,112},{1,113},{2,114},{3,115},{4,116},{5,117},{6,118},{7,119},{8... | collective-permute-start | bytes 737288 | tf_op jit(solution)/shard_map/ppermute | solution.py:513
  13.1 11.5 %collective-permute-start.2 = (bf16[3,14,4,512]{3,2,1,0:T(4,128)(2,1)S(1)}, bf16[3,14,4,512]{3,2,1,0:T(4,128)(2,1)S(1)}, u32[]{:S(2)}, u32[]{:S(2)}) collective-permute-start(bf16[3,14,4,512]{3,2,1,0:T(4,128)(2,1)S(1)} %get-tuple-element.23), channel_id=1, source_target_pairs={{0,1},{1,0},{2,3},{3,2},{4,5},{5,4},{6,7},{7,6},{8,9},{9,8},{10,11... | collective-permute-start | bytes 516104 | tf_op jit(solution)/shard_map/ppermute | solution.py:513
  13.2 11.4 %collective-permute-start.3 = (bf16[3,14,4,512]{3,2,1,0:T(4,128)(2,1)S(1)}, bf16[3,14,4,512]{3,2,1,0:T(4,128)(2,1)S(1)}, u32[]{:S(2)}, u32[]{:S(2)}) collective-permute-start(bf16[3,14,4,512]{3,2,1,0:T(4,128)(2,1)S(1)} %get-tuple-element.24), channel_id=1, source_target_pairs={{0,15},{1,2},{2,1},{3,4},{4,3},{5,6},{6,5},{7,8},{8,7},{9,10},{10,... | collective-permute-start | bytes 516104 | tf_op jit(solution)/shard_map/ppermute | solution.py:513
  19.4 5.2 %copy-start.1 = (f32[3,4,16,512]{3,2,1,0:T(8,128)S(1)}, f32[3,4,16,512]{3,2,1,0:T(8,128)}, u32[]{:S(2)}) copy-start(f32[3,4,16,512]{3,2,1,0:T(8,128)} %own.9) | copy-start | bytes 1179652
  38.9 1.3 %collective-permute-start.4 = (f32[88,128]{1,0:T(8,128)S(1)}, f32[88,128]{1,0:T(8,128)S(1)}, u32[]{:S(2)}, u32[]{:S(2)}) collective-permute-start(f32[88,128]{1,0:T(8,128)S(1)} %get-tuple-element.28), channel_id=1, source_target_pairs={{0,1},{1,0},{2,3},{3,2},{4,5},{5,4},{6,7},{7,6},{8,9},{9,8},{10,11... | collective-permute-start | bytes 135176 | tf_op jit(solution)/shard_map/ppermute | solution.py:513
  40.3 5.7 %collective-permute-start.7 = (f32[88,128]{1,0:T(8,128)S(1)}, f32[88,128]{1,0:T(8,128)S(1)}, u32[]{:S(2)}, u32[]{:S(2)}) collective-permute-start(f32[88,128]{1,0:T(8,128)S(1)} %add.21), channel_id=1, source_target_pairs={{0,32},{1,33},{2,34},{3,35},{4,36},{5,37},{6,38},{7,39},{8,40},{9,... | collective-permute-start | bytes 135176 | tf_op jit(solution)/shard_map/ppermute | solution.py:513
  41.1 5.3 %collective-permute-start.6 = (f32[88,128]{1,0:T(8,128)S(1)}, f32[88,128]{1,0:T(8,128)S(1)}, u32[]{:S(2)}, u32[]{:S(2)}) collective-permute-start(f32[88,128]{1,0:T(8,128)S(1)} %add.21), channel_id=1, source_target_pairs={{0,48},{1,49},{2,50},{3,51},{4,52},{5,53},{6,54},{7,55},{8,56},{9,... | collective-permute-start | bytes 135176 | tf_op jit(solution)/shard_map/ppermute | solution.py:513
  42.6 4.0 %collective-permute-start.5 = (f32[88,128]{1,0:T(8,128)S(1)}, f32[88,128]{1,0:T(8,128)S(1)}, u32[]{:S(2)}, u32[]{:S(2)}) collective-permute-start(f32[88,128]{1,0:T(8,128)S(1)} %add.21), channel_id=1, source_target_pairs={{0,16},{1,17},{2,18},{3,19},{4,20},{5,21},{6,22},{7,23},{8,24},{9,... | collective-permute-start | bytes 135176 | tf_op jit(solution)/shard_map/ppermute | solution.py:513
  46.7 5.9 %collective-permute-start.10 = (f32[88,128]{1,0:T(8,128)S(1)}, f32[88,128]{1,0:T(8,128)S(1)}, u32[]{:S(2)}, u32[]{:S(2)}) collective-permute-start(f32[88,128]{1,0:T(8,128)S(1)} %add_add_fusion.1), channel_id=1, source_target_pairs={{0,4},{1,5},{2,6},{3,7},{4,0},{5,1},{6,2},{7,3},{8,12},{9,13},{10,... | collective-permute-start | bytes 135176 | tf_op jit(solution)/shard_map/ppermute | solution.py:513
  46.9 5.8 %collective-permute-start.9 = (f32[88,128]{1,0:T(8,128)S(1)}, f32[88,128]{1,0:T(8,128)S(1)}, u32[]{:S(2)}, u32[]{:S(2)}) collective-permute-start(f32[88,128]{1,0:T(8,128)S(1)} %add_add_fusion.1), channel_id=1, source_target_pairs={{0,6},{1,7},{2,4},{3,5},{4,2},{5,3},{6,0},{7,1},{8,14},{9,15},{10,... | collective-permute-start | bytes 135176 | tf_op jit(solution)/shard_map/ppermute | solution.py:513
  47.3 5.4 %collective-permute-start.8 = (f32[88,128]{1,0:T(8,128)S(1)}, f32[88,128]{1,0:T(8,128)S(1)}, u32[]{:S(2)}, u32[]{:S(2)}) collective-permute-start(f32[88,128]{1,0:T(8,128)S(1)} %add_add_fusion.1), channel_id=1, source_target_pairs={{0,2},{1,3},{2,0},{3,1},{4,6},{5,7},{6,4},{7,5},{8,10},{9,11},{10,... | collective-permute-start | bytes 135176 | tf_op jit(solution)/shard_map/ppermute | solution.py:513
  52.8 6.3 %collective-permute-start.13 = (f32[88,128]{1,0:T(8,128)S(1)}, f32[88,128]{1,0:T(8,128)S(1)}, u32[]{:S(2)}, u32[]{:S(2)}) collective-permute-start(f32[88,128]{1,0:T(8,128)S(1)} %add_add_fusion.a), channel_id=1, source_target_pairs={{0,8},{1,9},{2,10},{3,11},{4,12},{5,13},{6,14},{7,15},{8,0},{9,1},... | collective-permute-start | bytes 135176 | tf_op jit(solution)/shard_map/ppermute | solution.py:513
  55.0 5.3 %collective-permute-start.12 = (f32[88,128]{1,0:T(8,128)S(1)}, f32[88,128]{1,0:T(8,128)S(1)}, u32[]{:S(2)}, u32[]{:S(2)}) collective-permute-start(f32[88,128]{1,0:T(8,128)S(1)} %add_add_fusion.a), channel_id=1, source_target_pairs={{0,72},{1,73},{2,74},{3,75},{4,76},{5,77},{6,78},{7,79},{8,64},{9,... | collective-permute-start | bytes 135176 | tf_op jit(solution)/shard_map/ppermute | solution.py:513
  56.6 4.0 %collective-permute-start.11 = (f32[88,128]{1,0:T(8,128)S(1)}, f32[88,128]{1,0:T(8,128)S(1)}, u32[]{:S(2)}, u32[]{:S(2)}) collective-permute-start(f32[88,128]{1,0:T(8,128)S(1)} %add_add_fusion.a), channel_id=1, source_target_pairs={{0,64},{1,65},{2,66},{3,67},{4,68},{5,69},{6,70},{7,71},{8,72},{9,... | collective-permute-start | bytes 135176 | tf_op jit(solution)/shard_map/ppermute | solution.py:513

commit v5 on v4

--- a/solution.py
+++ b/solution.py
@@ -142,8 +142,8 @@
         turn = (512 - (start & 127)) & 511
         window = pltpu.roll(tile[n * 32 : n * 32 + 32, pl.ds(base_lane, 512)], turn, 1)
         columns.append(jnp.concatenate([window[:, 0:256], window[:, 1:257], window[:, 2:258]], 0))
-        target = pltpu.roll(tile_target[n * 16 : n * 16 + 16, pl.ds(base_lane, 512)], turn, 1)
-        targets.append(target[:, 1:257])
+        target = pltpu.roll(tile_target[n * 16 : n * 16 + 16, pl.ds(base_lane, 512)], (turn - 1) & 511, 1)
+        targets.append(target[:, 0:256])
     half = len(starts) // 2
     cols = [jnp.concatenate(columns[:half], 1), jnp.concatenate(columns[half:], 1)]
     target = jnp.concatenate([jnp.concatenate(targets[:half], 1), jnp.concatenate(targets[half:], 1)], 0)
@@ -233,17 +233,15 @@
     w3t[...] = twice(dot_cells(half, last_rows.astype(bf16))).astype(bf16)
     packed_totals[...] = jnp.zeros_like(packed_totals)
 
-    def step(n, _):
+    starts = []
+    for n in range(2):
         x = n + 1
         for row in (12, 20):
             stress_rows(field, x, tau, n, row)
-        gather(tile, 0, pick[...], input_rows(field, x))
-        gather(tile_target, 0, pick_target[...], target_rows(tau, n))
-        starts = [offs[x, y] for y in range(1, 15)]
-        add_columns(tile.at[32:480], tile_target.at[16:240], starts, weights, totals)
-        return 0
-
-    lax.fori_loop(0, 2, step, 0)
+        gather(tile, 448 * n, pick.ref[32:480, :], input_rows(field, x))
+        gather(tile_target, 224 * n, pick_target.ref[528:752, 0:96], target_rows(tau, n))
+        starts += [offs[x, y] for y in range(1, 15)]
+    add_columns(tile, tile_target, starts, weights, totals)
 
 
 def split_bf16(value):
@@ -254,11 +252,11 @@
 def in_order(axis, step, first, second):
     odd = lax.axis_index(axis) % 2
 
-    @pl.when(odd == 1)
+    @pl.when(odd == 0)
     def _():
         step(first, second)
 
-    @pl.when(odd == 0)
+    @pl.when(odd == 1)
     def _():
         step(second, first)
 
@@ -281,26 +279,24 @@
 def pack_y_kernel(own, x_first, x_second, first, second):
     def pack(x_low, x_high, left, right):
         for c in range(3):
-            for out, start, near in ((right, 12, 15), (left, 0, 0)):
-                rests = []
-                for p in range(12):
-                    if p < 4:
-                        high = x_low[c, p].astype(f32)
-                    elif p < 8:
-                        high, rest = split_bf16(own[c, p - 4])
-                        high, rest = high.astype(f32), rest.astype(f32)
+            for out, at_top in ((right, True), (left, False)):
+
+                def rows(p, count):
+                    plane = x_low[c, p] if p < 4 else own[c, p - 4] if p < 8 else x_high[c, p - 7]
+                    return plane.astype(f32)[16 - count :] if at_top else plane.astype(f32)[:count]
+
+                def rest(p):
+                    if p == 3 or p == 8:
+                        plane = (x_low[c, 4] if p == 3 else x_high[c, 0]).astype(f32)
                     else:
-                        high = x_high[c, p - 7].astype(f32)
-                    if p == 3:
-                        rest = x_low[c, 4].astype(f32)
-                    if p == 8:
-                        rest = x_high[c, 0].astype(f32)
-                    out[c, p] = high[start : start + 4, :].astype(bf16)
-                    if 3 <= p <= 8:
-                        rests.append(rest[near : near + 1, :])
-                rests = jnp.concatenate(rests + [jnp.zeros((2, 512), f32)], 0)
-                out[c, 12] = rests[0:4].astype(bf16)
-                out[c, 13] = rests[4:8].astype(bf16)
+                        plane = split_bf16(own[c, p - 4])[1].astype(f32)
+                    return plane[15:] if at_top else plane[:1]
+
+                blocks = [[rows(p, 4)] for p in range(4, 8)]
+                blocks += [[rows(3, 3), rows(1, 1)], [rows(8, 3), rows(10, 1)], [rows(2, 2), rows(9, 2)]]
+                blocks += [[rest(p) for p in range(3, 7)], [rest(7), rest(8), jnp.zeros((2, 512), f32)]]
+                for k, block in enumerate(blocks):
+                    out[c, k] = jnp.concatenate(block, 0).astype(bf16)
 
     def with_x(x_low, x_high):
         in_order("py", lambda left, right: pack(x_low, x_high, left, right), first, second)
@@ -338,17 +334,15 @@
     in_order("px", place, x_first, x_second)
     copy.wait()
 
-    def step(n, _):
+    starts = []
+    for n in range(2):
         x = 3 * n
         for row in (12, 20):
-            stress_rows(field, x + 1, tau, 0, row)
-        gather(tile, 0, pick[...], input_rows(field, x + 1))
-        gather(tile_target, 0, pick_target[...], target_rows(tau, 0))
-        starts = [offs[x, y] for y in range(1, 15)]
-        add_columns(tile.at[32:480], tile_target.at[16:240], starts, weights, totals)
-        return 0
-
-    lax.fori_loop(0, 2, step, 0)
+            stress_rows(field, x + 1, tau, n, row)
+        gather(tile, 448 * n, pick.ref[32:480, :], input_rows(field, x + 1))
+        gather(tile_target, 224 * n, pick_target.ref[528:752, 0:96], target_rows(tau, n))
+        starts += [offs[x, y] for y in range(1, 15)]
+    add_columns(tile, tile_target, starts, weights, totals)
 
 
 def middle_kernel(
@@ -376,15 +370,18 @@
                 field[c, p, 12:28, 0:512] = x_plane(x_low, own, x_high, c, p)
 
     def place_y(y_low, y_high):
-        for c in range(3):
-            for p in range(12):
-                low, high = y_low[c, p].astype(f32), y_high[c, p].astype(f32)
-                field[c, p, 8:12, 0:512] = low
-                field[c, p, 28:32, 0:512] = high
+        parts = [(p, 4, p - 4, 0) for p in range(4, 8)]
+        parts += [(3, 3, 4, 0), (1, 1, 4, 3), (8, 3, 5, 0), (10, 1, 5, 3), (2, 2, 6, 0), (9, 2, 6, 2)]
+        for c in range(3):
+            for p, count, k, at in parts:
+                low = y_low[c, k].astype(f32)[at : at + count]
+                high = y_high[c, k].astype(f32)[at : at + count]
+                field[c, p, 12 - count : 12, 0:512] = low
+                field[c, p, 28 : 28 + count, 0:512] = high
                 if 3 <= p <= 8:
-                    k, r = 12 + (p - 3) // 4, (p - 3) % 4
-                    field[c, p, 11:12, 0:512] = low[3:4] + y_low[c, k].astype(f32)[r : r + 1]
-                    field[c, p, 28:29, 0:512] = high[0:1] + y_high[c, k].astype(f32)[r : r + 1]
+                    k, at = 7 + (p - 3) // 4, (p - 3) % 4
+                    field[c, p, 11:12, 0:512] = low[count - 1 :] + y_low[c, k].astype(f32)[at : at + 1]
+                    field[c, p, 28:29, 0:512] = high[:1] + y_high[c, k].astype(f32)[at : at + 1]
 
     in_order("px", place_x, x_first, x_second)
     in_order("py", place_y, y_first, y_second)
@@ -517,24 +514,24 @@
     table = jnp.asarray(selections(), bf16)
     near_x, far_x = lambda i, j: (i ^ 1, j), lambda i, j: (i + 2 * (i % 2) - 1, j)
     near_y, far_y = lambda i, j: (i, j ^ 1), lambda i, j: (i, j + 2 * (j % 2) - 1)
-    to_near, to_far = call(pack_x_kernel, (velocity,), [shaped(3, 5, 16, 512, kind=bf16)] * 2, [])
-    x_first, x_second = send(to_near, near_x), send(to_far, far_x)
+    to_far, to_near = call(pack_x_kernel, (velocity,), [shaped(3, 5, 16, 512, kind=bf16)] * 2, [])
+    x_first, x_second = send(to_far, far_x), send(to_near, near_x)
     weights, totals = call(
         interior_kernel,
         (offsets, velocity, first_weight, mid_weight, last_weight, table),
-        [WEIGHTS, TOTALS], columns_scratch(4, 2, 16)
+        [WEIGHTS, TOTALS], columns_scratch(4, 2, 28)
         + [pltpu.VMEM(n, bf16) for n in ((64, 81), (64, 64), (6, 64))] + [pltpu.SemaphoreType.DMA((4,))],
-        1, 6, 16, 4,
+        1, 6, 28, 4,
     )
     x_first, x_second, totals = lax.optimization_barrier((x_first, x_second, totals))
-    to_near, to_far = call(
-        pack_y_kernel, (velocity, x_first, x_second), [shaped(3, 14, 4, 512, kind=bf16)] * 2, []
+    to_far, to_near = call(
+        pack_y_kernel, (velocity, x_first, x_second), [shaped(3, 9, 4, 512, kind=bf16)] * 2, []
     )
-    y_first, y_second = send(to_near, near_y), send(to_far, far_y)
+    y_first, y_second = send(to_far, far_y), send(to_near, near_y)
     (totals,) = call(
         side_kernel,
         (offsets, velocity, x_first, x_second, weights, totals, table),
-        [TOTALS], columns_scratch(6, 1, 16) + [pltpu.SemaphoreType.DMA((1,))], 1, 6, 16, 1,
+        [TOTALS], columns_scratch(6, 2, 28) + [pltpu.SemaphoreType.DMA((1,))], 1, 6, 28, 1,
     )
     middle, packed = call(
         middle_kernel,

time: 61.6 us -> 61.4 us (level)
  waiting for transfers between devices: 8.41 us -> 11.9 us
  starting transfers between devices: 22.7 us -> 19.8 us
  Pallas kernels: 28.4 us -> 27.7 us
    ppermute x14, waiting for transfers between devices: 8.41 us -> 11.9 us  [send(): return lax.ppermute(value, AXES, pairs(move))]
    ppermute x14, starting transfers between devices: 22.7 us -> 19.8 us  [send(): return lax.ppermute(value, AXES, pairs(move))]
    pallas_call x7, Pallas kernels: 28.4 us -> 27.7 us  [call(): pl.pallas_call(kernel, in_specs=[scalar] * smem + [vmem] * (len(args) - s...]
  transfers between devices with their start and end apart: 14 -> 14, of which waited for: 9 -> 10; matrix products, arithmetic and copies ran while one was open for 0% -> 0% of each run, Pallas kernels for 21% -> 20%
where the time goes in v5:
time: 61.4 us; the launch traced here: 61.2 us
  Pallas kernels  27.7 us (45%)
  starting transfers between devices  19.8 us (32%)
  waiting for transfers between devices  11.9 us (19%)
  local copies, waits for them, and re-layouts  1.01 us (2%)
  between operations  0.78 us (1%)
    pallas_call x7, Pallas kernels, call(): pl.pallas_call(kernel, in_specs=[scalar] * smem + [vmem] * (len(args) - s...  27.7 us
    ppermute x14, starting transfers between devices, send(): return lax.ppermute(value, AXES, pairs(move))  19.8 us
    ppermute x14, waiting for transfers between devices, send(): return lax.ppermute(value, AXES, pairs(move))  11.9 us
  transfers between devices with their start and end apart: 14, of which 10 were waited for; matrix products, arithmetic and copies ran while one was open for 0% of the time, Pallas kernels for 20%

profile of v5, /device:TPU:0, one launch (start us, length us, event | category | flops | bytes accessed | tf_op | source)
XLA Modules:
  0.0 61.2 jit_solution(17778912613815540497)
XLA Ops:
  0.6 1.0 %copy-done = f32[3,4,16,512]{3,2,1,0:T(8,128)S(1)} copy-done((f32[3,4,16,512]{3,2,1,0:T(8,128)S(1)}, f32[3,4,16,512]{3,2,1,0:T(8,128)}, u32[]{:S(2)}) %copy-start) | copy-done | bytes 393240
  1.7 4.5 %collective-permute-start = (bf16[3,5,16,512]{3,2,1,0:T(8,128)(2,1)S(1)}, bf16[3,5,16,512]{3,2,1,0:T(8,128)(2,1)S(1)}, u32[]{:S(2)}, u32[]{:S(2)}) collective-permute-start(bf16[3,5,16,512]{3,2,1,0:T(8,128)(2,1)S(1)} %get-tuple-element.18), channel_id=1, source_target_pairs={{0,112},{1,113},{2,114},{3,115},{4,116},{5,117},{6,118},{7,119},{8... | collective-permute-start | bytes 737288 | tf_op jit(solution)/shard_map/ppermute | solution.py:510
  6.3 4.8 %shard_map.94 = (bf16[480,128]{1,0:T(8,128)(2,1)S(1)}, f32[144,128]{1,0:T(8,128)S(1)}) custom-call(s32[4,16]{1,0:T(4,128)S(1)} %copy-done.5, f32[3,4,16,512]{3,2,1,0:T(8,128)S(1)} %copy-done.1, bf16[64,81]{1,0:T(8,128)(2,1)S(1)} %copy-done.2, bf16[64,64]{1,0:T(8,128)(2,1)S(1)} %copy-done.3, bf16[6,64]{1,0:T(8,128)(2,1)S(1)} %copy-done.4, ...), custom_call_target="tpu_custom_call" | custom-call | flops 6899999744 | bytes 22140000 | tf_op jit(solution)/shard_map/pallas_call | solution.py:465
  11.1 1.1 %collective-permute-done.x_first = bf16[3,5,16,512]{3,2,1,0:T(8,128)(2,1)S(1)} collective-permute-done((bf16[3,5,16,512]{3,2,1,0:T(8,128)(2,1)S(1)}, bf16[3,5,16,512]{3,2,1,0:T(8,128)(2,1)S(1)}, u32[]{:S(2)}, u32[]{:S(2)}) %collective-permute-start) | collective-permute-done | bytes 245792 | tf_op jit(solution)/shard_map/ppermute | solution.py:510
  12.2 1.5 %collective-permute-done.1.x_second = bf16[3,5,16,512]{3,2,1,0:T(8,128)(2,1)S(1)} collective-permute-done((bf16[3,5,16,512]{3,2,1,0:T(8,128)(2,1)S(1)}, bf16[3,5,16,512]{3,2,1,0:T(8,128)(2,1)S(1)}, u32[]{:S(2)}, u32[]{:S(2)}) %collective-permute-start.1) | collective-permute-done | bytes 245792 | tf_op jit(solution)/shard_map/ppermute | solution.py:510
  13.8 4.1 %collective-permute-start.2 = (bf16[3,9,4,512]{3,2,1,0:T(4,128)(2,1)S(1)}, bf16[3,9,4,512]{3,2,1,0:T(4,128)(2,1)S(1)}, u32[]{:S(2)}, u32[]{:S(2)}) collective-permute-start(bf16[3,9,4,512]{3,2,1,0:T(4,128)(2,1)S(1)} %get-tuple-element.23), channel_id=1, source_target_pairs={{0,15},{1,2},{2,1},{3,4},{4,3},{5,6},{6,5},{7,8},{8,7},{9,10},{10,... | collective-permute-start | bytes 331784 | tf_op jit(solution)/shard_map/ppermute | solution.py:510
  18.0 4.7 %shard_map.96.before = f32[144,128]{1,0:T(8,128)S(1)} custom-call(s32[4,16]{1,0:T(4,128)S(1)} %copy-done.5, f32[3,4,16,512]{3,2,1,0:T(8,128)S(1)} %copy-done.1, bf16[3,5,16,512]{3,2,1,0:T(8,128)(2,1)S(1)} %collective-permute-done.x_first, bf16[3,5,16,512]{3,2,1,0:T(8,128)(2,1)S(1)} %collective-permute-done.1.x_second, ...), custom_call_target="tpu_custom_call" | custom-call | flops 6899999744 | bytes 22140000 | tf_op jit(solution)/shard_map/pallas_call | solution.py:465
  22.7 14.5 %shard_map.97 = (f32[3,8,40,512]{3,2,1,0:T(8,128)S(1)}, f32[88,128]{1,0:T(8,128)S(1)}) custom-call(s32[4,16]{1,0:T(4,128)S(1)} %copy-done.5, f32[3,4,16,512]{3,2,1,0:T(8,128)S(1)} %copy-done.1, bf16[3,5,16,512]{3,2,1,0:T(8,128)(2,1)S(1)} %collective-permute-done.x_first, bf16[3,5,16,512]{3,2,1,0:T(8,128)(2,1)S(1)} %collective-permute-done.1.x_second, ...), custom_call_target="tpu_custom_call" | custom-call | flops 18400000000 | bytes 59040000 | tf_op jit(solution)/shard_map/pallas_call | solution.py:465
  37.3 0.6 collective-permute-start.4
  37.8 0.9 %collective-permute-done.4 = f32[88,128]{1,0:T(8,128)S(1)} collective-permute-done((f32[88,128]{1,0:T(8,128)S(1)}, f32[88,128]{1,0:T(8,128)S(1)}, u32[]{:S(2)}, u32[]{:S(2)}) %collective-permute-start.4) | collective-permute-done | bytes 45088 | tf_op jit(solution)/shard_map/ppermute | solution.py:510
  38.7 0.3 collective-permute-start.7
  39.0 3.0 %collective-permute-start.6 = (f32[88,128]{1,0:T(8,128)S(1)}, f32[88,128]{1,0:T(8,128)S(1)}, u32[]{:S(2)}, u32[]{:S(2)}) collective-permute-start(f32[88,128]{1,0:T(8,128)S(1)} %add.21), channel_id=1, source_target_pairs={{0,48},{1,49},{2,50},{3,51},{4,52},{5,53},{6,54},{7,55},{8,56},{9,... | collective-permute-start | bytes 135176 | tf_op jit(solution)/shard_map/ppermute | solution.py:510
  42.2 2.2 %collective-permute-done.7 = f32[88,128]{1,0:T(8,128)S(1)} collective-permute-done((f32[88,128]{1,0:T(8,128)S(1)}, f32[88,128]{1,0:T(8,128)S(1)}, u32[]{:S(2)}, u32[]{:S(2)}) %collective-permute-start.7) | collective-permute-done | bytes 45088 | tf_op jit(solution)/shard_map/ppermute | solution.py:510
  44.4 0.6 collective-permute-done.6
  45.0 1.1 %collective-permute-done.5 = f32[88,128]{1,0:T(8,128)S(1)} collective-permute-done((f32[88,128]{1,0:T(8,128)S(1)}, f32[88,128]{1,0:T(8,128)S(1)}, u32[]{:S(2)}, u32[]{:S(2)}) %collective-permute-start.5) | collective-permute-done | bytes 45088 | tf_op jit(solution)/shard_map/ppermute | solution.py:510
  46.1 2.0 %collective-permute-start.9 = (f32[88,128]{1,0:T(8,128)S(1)}, f32[88,128]{1,0:T(8,128)S(1)}, u32[]{:S(2)}, u32[]{:S(2)}) collective-permute-start(f32[88,128]{1,0:T(8,128)S(1)} %add_add_fusion.1), channel_id=1, source_target_pairs={{0,6},{1,7},{2,4},{3,5},{4,2},{5,3},{6,0},{7,1},{8,14},{9,15},{10,... | collective-permute-start | bytes 135176 | tf_op jit(solution)/shard_map/ppermute | solution.py:510
  48.2 1.5 %collective-permute-start.8 = (f32[88,128]{1,0:T(8,128)S(1)}, f32[88,128]{1,0:T(8,128)S(1)}, u32[]{:S(2)}, u32[]{:S(2)}) collective-permute-start(f32[88,128]{1,0:T(8,128)S(1)} %add_add_fusion.1), channel_id=1, source_target_pairs={{0,2},{1,3},{2,0},{3,1},{4,6},{5,7},{6,4},{7,5},{8,10},{9,11},{10,... | collective-permute-start | bytes 135176 | tf_op jit(solution)/shard_map/ppermute | solution.py:510
  49.6 2.2 %collective-permute-done.10 = f32[88,128]{1,0:T(8,128)S(1)} collective-permute-done((f32[88,128]{1,0:T(8,128)S(1)}, f32[88,128]{1,0:T(8,128)S(1)}, u32[]{:S(2)}, u32[]{:S(2)}) %collective-permute-start.10) | collective-permute-done | bytes 45088 | tf_op jit(solution)/shard_map/ppermute | solution.py:510
  52.0 0.2 collective-permute-done.8
  52.2 3.0 %collective-permute-start.13 = (f32[88,128]{1,0:T(8,128)S(1)}, f32[88,128]{1,0:T(8,128)S(1)}, u32[]{:S(2)}, u32[]{:S(2)}) collective-permute-start(f32[88,128]{1,0:T(8,128)S(1)} %add_add_fusion.a), channel_id=1, source_target_pairs={{0,8},{1,9},{2,10},{3,11},{4,12},{5,13},{6,14},{7,15},{8,0},{9,1},... | collective-permute-start | bytes 135176 | tf_op jit(solution)/shard_map/ppermute | solution.py:510
  55.2 0.6 collective-permute-start.11
  55.8 2.6 %shard_map.98 = f32[3,4,16,512]{3,2,1,0:T(8,128)} custom-call(f32[3,8,40,512]{3,2,1,0:T(8,128)S(1)} %get-tuple-element.27.middle), custom_call_target="tpu_custom_call" | custom-call | flops 3449999872 | bytes 11070000 | tf_op jit(solution)/shard_map/pallas_call | solution.py:465
  58.4 2.1 %collective-permute-done.12.c = f32[88,128]{1,0:T(8,128)S(1)} collective-permute-done((f32[88,128]{1,0:T(8,128)S(1)}, f32[88,128]{1,0:T(8,128)S(1)}, u32[]{:S(2)}, u32[]{:S(2)}) %collective-permute-start.12) | collective-permute-done | bytes 45088 | tf_op jit(solution)/shard_map/ppermute | solution.py:510
  60.5 0.8 %shard_map.99 = (f32[64,81]{1,0:T(8,128)}, f32[64,64]{1,0:T(8,128)}, f32[6,64]{1,0:T(8,128)}) custom-call(f32[88,128]{1,0:T(8,128)S(1)} %add_add_fusion.a, f32[88,128]{1,0:T(8,128)S(1)} %collective-permute-done.11.b, f32[88,128]{1,0:T(8,128)S(1)} %collective-permute-done.12.c, f32[88,128]{1,0:T(8,128)S(1)} %collective-permute-done.13.d), custom_call_target="tpu_custom_call" | custom-call | flops 1150000000 | bytes 3690000 | tf_op jit(solution)/shard_map/pallas_call | solution.py:465
  (28 shorter events, 0.8 us)
Async XLA Ops:
  0.6 1.0 %copy-start = (f32[3,4,16,512]{3,2,1,0:T(8,128)S(1)}, f32[3,4,16,512]{3,2,1,0:T(8,128)}, u32[]{:S(2)}) copy-start(f32[3,4,16,512]{3,2,1,0:T(8,128)} %own.9) | copy-start | bytes 1179652
  1.6 4.6 %copy-start.1 = (f32[3,4,16,512]{3,2,1,0:T(8,128)S(1)}, f32[3,4,16,512]{3,2,1,0:T(8,128)}, u32[]{:S(2)}) copy-start(f32[3,4,16,512]{3,2,1,0:T(8,128)} %own.9) | copy-start | bytes 1179652
  1.6 4.6 %copy-start.2 = (bf16[64,81]{1,0:T(8,128)(2,1)S(1)}, bf16[64,81]{1,0:T(8,128)(2,1)}, u32[]{:S(2)}) copy-start(bf16[64,81]{1,0:T(8,128)(2,1)} %first.1) | copy-start | bytes 31108
  1.6 4.6 %copy-start.3 = (bf16[64,64]{1,0:T(8,128)(2,1)S(1)}, bf16[64,64]{1,0:T(8,128)(2,1)}, u32[]{:S(2)}) copy-start(bf16[64,64]{1,0:T(8,128)(2,1)} %mid.1) | copy-start | bytes 24580
  1.6 4.6 %copy-start.4 = (bf16[6,64]{1,0:T(8,128)(2,1)S(1)}, bf16[6,64]{1,0:T(8,128)(2,1)}, u32[]{:S(2)}) copy-start(bf16[6,64]{1,0:T(8,128)(2,1)} %last.1) | copy-start | bytes 2308
  1.6 4.7 %copy-start.5 = (s32[4,16]{1,0:T(4,128)S(1)}, s32[4,16]{1,0:T(4,128)}, u32[]{:S(2)}) copy-start(s32[4,16]{1,0:T(4,128)} %offs.5) | copy-start | bytes 772
  1.6 4.7 %copy-start.6 = (bf16[960,216]{1,0:T(8,128)(2,1)S(1)}, bf16[960,216]{1,0:T(8,128)(2,1)}, u32[]{:S(2)}) copy-start(bf16[960,216]{1,0:T(8,128)(2,1)} %constant.2.clone.table) | copy-start | bytes 1244164
  1.7 10.5 %collective-permute-start = (bf16[3,5,16,512]{3,2,1,0:T(8,128)(2,1)S(1)}, bf16[3,5,16,512]{3,2,1,0:T(8,128)(2,1)S(1)}, u32[]{:S(2)}, u32[]{:S(2)}) collective-permute-start(bf16[3,5,16,512]{3,2,1,0:T(8,128)(2,1)S(1)} %get-tuple-element.18), channel_id=1, source_target_pairs={{0,112},{1,113},{2,114},{3,115},{4,116},{5,117},{6,118},{7,119},{8... | collective-permute-start | bytes 737288 | tf_op jit(solution)/shard_map/ppermute | solution.py:510
  6.3 7.4 %collective-permute-start.1 = (bf16[3,5,16,512]{3,2,1,0:T(8,128)(2,1)S(1)}, bf16[3,5,16,512]{3,2,1,0:T(8,128)(2,1)S(1)}, u32[]{:S(2)}, u32[]{:S(2)}) collective-permute-start(bf16[3,5,16,512]{3,2,1,0:T(8,128)(2,1)S(1)} %get-tuple-element.19), channel_id=1, source_target_pairs={{0,16},{1,17},{2,18},{3,19},{4,20},{5,21},{6,22},{7,23},{8,24},{9,... | collective-permute-start | bytes 737288 | tf_op jit(solution)/shard_map/ppermute | solution.py:510
  13.8 8.9 %collective-permute-start.2 = (bf16[3,9,4,512]{3,2,1,0:T(4,128)(2,1)S(1)}, bf16[3,9,4,512]{3,2,1,0:T(4,128)(2,1)S(1)}, u32[]{:S(2)}, u32[]{:S(2)}) collective-permute-start(bf16[3,9,4,512]{3,2,1,0:T(4,128)(2,1)S(1)} %get-tuple-element.23), channel_id=1, source_target_pairs={{0,15},{1,2},{2,1},{3,4},{4,3},{5,6},{6,5},{7,8},{8,7},{9,10},{10,... | collective-permute-start | bytes 331784 | tf_op jit(solution)/shard_map/ppermute | solution.py:510
  17.9 4.8 %collective-permute-start.3 = (bf16[3,9,4,512]{3,2,1,0:T(4,128)(2,1)S(1)}, bf16[3,9,4,512]{3,2,1,0:T(4,128)(2,1)S(1)}, u32[]{:S(2)}, u32[]{:S(2)}) collective-permute-start(bf16[3,9,4,512]{3,2,1,0:T(4,128)(2,1)S(1)} %get-tuple-element.24), channel_id=1, source_target_pairs={{0,1},{1,0},{2,3},{3,2},{4,5},{5,4},{6,7},{7,6},{8,9},{9,8},{10,11... | collective-permute-start | bytes 331784 | tf_op jit(solution)/shard_map/ppermute | solution.py:510
  37.3 1.5 %collective-permute-start.4 = (f32[88,128]{1,0:T(8,128)S(1)}, f32[88,128]{1,0:T(8,128)S(1)}, u32[]{:S(2)}, u32[]{:S(2)}) collective-permute-start(f32[88,128]{1,0:T(8,128)S(1)} %get-tuple-element.28), channel_id=1, source_target_pairs={{0,1},{1,0},{2,3},{3,2},{4,5},{5,4},{6,7},{7,6},{8,9},{9,8},{10,11... | collective-permute-start | bytes 135176 | tf_op jit(solution)/shard_map/ppermute | solution.py:510
  38.7 5.7 %collective-permute-start.7 = (f32[88,128]{1,0:T(8,128)S(1)}, f32[88,128]{1,0:T(8,128)S(1)}, u32[]{:S(2)}, u32[]{:S(2)}) collective-permute-start(f32[88,128]{1,0:T(8,128)S(1)} %add.21), channel_id=1, source_target_pairs={{0,32},{1,33},{2,34},{3,35},{4,36},{5,37},{6,38},{7,39},{8,40},{9,... | collective-permute-start | bytes 135176 | tf_op jit(solution)/shard_map/ppermute | solution.py:510
  39.0 6.0 %collective-permute-start.6 = (f32[88,128]{1,0:T(8,128)S(1)}, f32[88,128]{1,0:T(8,128)S(1)}, u32[]{:S(2)}, u32[]{:S(2)}) collective-permute-start(f32[88,128]{1,0:T(8,128)S(1)} %add.21), channel_id=1, source_target_pairs={{0,48},{1,49},{2,50},{3,51},{4,52},{5,53},{6,54},{7,55},{8,56},{9,... | collective-permute-start | bytes 135176 | tf_op jit(solution)/shard_map/ppermute | solution.py:510
  42.0 4.0 %collective-permute-start.5 = (f32[88,128]{1,0:T(8,128)S(1)}, f32[88,128]{1,0:T(8,128)S(1)}, u32[]{:S(2)}, u32[]{:S(2)}) collective-permute-start(f32[88,128]{1,0:T(8,128)S(1)} %add.21), channel_id=1, source_target_pairs={{0,16},{1,17},{2,18},{3,19},{4,20},{5,21},{6,22},{7,23},{8,24},{9,... | collective-permute-start | bytes 135176 | tf_op jit(solution)/shard_map/ppermute | solution.py:510
  46.1 5.7 %collective-permute-start.10 = (f32[88,128]{1,0:T(8,128)S(1)}, f32[88,128]{1,0:T(8,128)S(1)}, u32[]{:S(2)}, u32[]{:S(2)}) collective-permute-start(f32[88,128]{1,0:T(8,128)S(1)} %add_add_fusion.1), channel_id=1, source_target_pairs={{0,4},{1,5},{2,6},{3,7},{4,0},{5,1},{6,2},{7,3},{8,12},{9,13},{10,... | collective-permute-start | bytes 135176 | tf_op jit(solution)/shard_map/ppermute | solution.py:510
  46.1 5.8 %collective-permute-start.9 = (f32[88,128]{1,0:T(8,128)S(1)}, f32[88,128]{1,0:T(8,128)S(1)}, u32[]{:S(2)}, u32[]{:S(2)}) collective-permute-start(f32[88,128]{1,0:T(8,128)S(1)} %add_add_fusion.1), channel_id=1, source_target_pairs={{0,6},{1,7},{2,4},{3,5},{4,2},{5,3},{6,0},{7,1},{8,14},{9,15},{10,... | collective-permute-start | bytes 135176 | tf_op jit(solution)/shard_map/ppermute | solution.py:510
  48.2 4.0 %collective-permute-start.8 = (f32[88,128]{1,0:T(8,128)S(1)}, f32[88,128]{1,0:T(8,128)S(1)}, u32[]{:S(2)}, u32[]{:S(2)}) collective-permute-start(f32[88,128]{1,0:T(8,128)S(1)} %add_add_fusion.1), channel_id=1, source_target_pairs={{0,2},{1,3},{2,0},{3,1},{4,6},{5,7},{6,4},{7,5},{8,10},{9,11},{10,... | collective-permute-start | bytes 135176 | tf_op jit(solution)/shard_map/ppermute | solution.py:510
  52.2 6.2 %collective-permute-start.13 = (f32[88,128]{1,0:T(8,128)S(1)}, f32[88,128]{1,0:T(8,128)S(1)}, u32[]{:S(2)}, u32[]{:S(2)}) collective-permute-start(f32[88,128]{1,0:T(8,128)S(1)} %add_add_fusion.a), channel_id=1, source_target_pairs={{0,8},{1,9},{2,10},{3,11},{4,12},{5,13},{6,14},{7,15},{8,0},{9,1},... | collective-permute-start | bytes 135176 | tf_op jit(solution)/shard_map/ppermute | solution.py:510
  55.2 5.3 %collective-permute-start.12 = (f32[88,128]{1,0:T(8,128)S(1)}, f32[88,128]{1,0:T(8,128)S(1)}, u32[]{:S(2)}, u32[]{:S(2)}) collective-permute-start(f32[88,128]{1,0:T(8,128)S(1)} %add_add_fusion.a), channel_id=1, source_target_pairs={{0,72},{1,73},{2,74},{3,75},{4,76},{5,77},{6,78},{7,79},{8,64},{9,... | collective-permute-start | bytes 135176 | tf_op jit(solution)/shard_map/ppermute | solution.py:510
  55.2 5.3 %collective-permute-start.11 = (f32[88,128]{1,0:T(8,128)S(1)}, f32[88,128]{1,0:T(8,128)S(1)}, u32[]{:S(2)}, u32[]{:S(2)}) collective-permute-start(f32[88,128]{1,0:T(8,128)S(1)} %add_add_fusion.a), channel_id=1, source_target_pairs={{0,64},{1,65},{2,66},{3,67},{4,68},{5,69},{6,70},{7,71},{8,72},{9,... | collective-permute-start | bytes 135176 | tf_op jit(solution)/shard_map/ppermute | solution.py:510

commit v6 on v5

--- a/solution.py
+++ b/solution.py
@@ -249,8 +249,11 @@
     return high, (value - high.astype(f32)).astype(bf16)
 
 
+FAR_FIRST = {"px": False, "py": True}
+
+
 def in_order(axis, step, first, second):
-    odd = lax.axis_index(axis) % 2
+    odd = (lax.axis_index(axis) + (0 if FAR_FIRST[axis] else 1)) % 2
 
     @pl.when(odd == 0)
     def _():
@@ -514,8 +517,8 @@
     table = jnp.asarray(selections(), bf16)
     near_x, far_x = lambda i, j: (i ^ 1, j), lambda i, j: (i + 2 * (i % 2) - 1, j)
     near_y, far_y = lambda i, j: (i, j ^ 1), lambda i, j: (i, j + 2 * (j % 2) - 1)
-    to_far, to_near = call(pack_x_kernel, (velocity,), [shaped(3, 5, 16, 512, kind=bf16)] * 2, [])
-    x_first, x_second = send(to_far, far_x), send(to_near, near_x)
+    to_near, to_far = call(pack_x_kernel, (velocity,), [shaped(3, 5, 16, 512, kind=bf16)] * 2, [])
+    x_first, x_second = send(to_near, near_x), send(to_far, far_x)
     weights, totals = call(
         interior_kernel,
         (offsets, velocity, first_weight, mid_weight, last_weight, table),

time: 61.4 us -> 60.3 us (0.982)
  waiting for transfers between devices: 11.9 us -> 9.38 us
  starting transfers between devices: 19.8 us -> 21.3 us
    ppermute x14, waiting for transfers between devices: 11.9 us -> 9.38 us  [send(): return lax.ppermute(value, AXES, pairs(move))]
    ppermute x14, starting transfers between devices: 19.8 us -> 21.3 us  [send(): return lax.ppermute(value, AXES, pairs(move))]
  transfers between devices with their start and end apart: 14 -> 14, of which waited for: 10 -> 7; matrix products, arithmetic and copies ran while one was open for 0% -> 0% of each run, Pallas kernels for 20% -> 20%
where the time goes in v6:
time: 60.3 us; the launch traced here: 60.2 us
  Pallas kernels  27.7 us (46%)
  starting transfers between devices  21.3 us (35%)
  waiting for transfers between devices  9.38 us (16%)
  local copies, waits for them, and re-layouts  1.01 us (2%)
  between operations  0.77 us (1%)
    pallas_call x7, Pallas kernels, call(): pl.pallas_call(kernel, in_specs=[scalar] * smem + [vmem] * (len(args) - s...  27.7 us
    ppermute x14, starting transfers between devices, send(): return lax.ppermute(value, AXES, pairs(move))  21.3 us
    ppermute x14, waiting for transfers between devices, send(): return lax.ppermute(value, AXES, pairs(move))  9.38 us
  transfers between devices with their start and end apart: 14, of which 7 were waited for; matrix products, arithmetic and copies ran while one was open for 0% of the time, Pallas kernels for 20%

profile of v6, /device:TPU:0, one launch (start us, length us, event | category | flops | bytes accessed | tf_op | source)
XLA Modules:
  0.0 60.2 jit_solution(9338784879274558474)
XLA Ops:
  0.6 1.0 %copy-done = f32[3,4,16,512]{3,2,1,0:T(8,128)S(1)} copy-done((f32[3,4,16,512]{3,2,1,0:T(8,128)S(1)}, f32[3,4,16,512]{3,2,1,0:T(8,128)}, u32[]{:S(2)}) %copy-start) | copy-done | bytes 393240
  1.7 1.7 %collective-permute-start = (bf16[3,5,16,512]{3,2,1,0:T(8,128)(2,1)S(1)}, bf16[3,5,16,512]{3,2,1,0:T(8,128)(2,1)S(1)}, u32[]{:S(2)}, u32[]{:S(2)}) collective-permute-start(bf16[3,5,16,512]{3,2,1,0:T(8,128)(2,1)S(1)} %get-tuple-element.18), channel_id=1, source_target_pairs={{0,16},{1,17},{2,18},{3,19},{4,20},{5,21},{6,22},{7,23},{8,24},{9,... | collective-permute-start | bytes 737288 | tf_op jit(solution)/shard_map/ppermute | solution.py:513
  3.5 3.5 %collective-permute-start.1 = (bf16[3,5,16,512]{3,2,1,0:T(8,128)(2,1)S(1)}, bf16[3,5,16,512]{3,2,1,0:T(8,128)(2,1)S(1)}, u32[]{:S(2)}, u32[]{:S(2)}) collective-permute-start(bf16[3,5,16,512]{3,2,1,0:T(8,128)(2,1)S(1)} %get-tuple-element.19), channel_id=1, source_target_pairs={{0,112},{1,113},{2,114},{3,115},{4,116},{5,117},{6,118},{7,119},{8... | collective-permute-start | bytes 737288 | tf_op jit(solution)/shard_map/ppermute | solution.py:513
  7.0 4.8 %shard_map.94 = (bf16[480,128]{1,0:T(8,128)(2,1)S(1)}, f32[144,128]{1,0:T(8,128)S(1)}) custom-call(s32[4,16]{1,0:T(4,128)S(1)} %copy-done.5, f32[3,4,16,512]{3,2,1,0:T(8,128)S(1)} %copy-done.1, bf16[64,81]{1,0:T(8,128)(2,1)S(1)} %copy-done.2, bf16[64,64]{1,0:T(8,128)(2,1)S(1)} %copy-done.3, bf16[6,64]{1,0:T(8,128)(2,1)S(1)} %copy-done.4, ...), custom_call_target="tpu_custom_call" | custom-call | flops 6899999744 | bytes 22140000 | tf_op jit(solution)/shard_map/pallas_call | solution.py:468
  11.9 1.1 %collective-permute-done.1.x_second = bf16[3,5,16,512]{3,2,1,0:T(8,128)(2,1)S(1)} collective-permute-done((bf16[3,5,16,512]{3,2,1,0:T(8,128)(2,1)S(1)}, bf16[3,5,16,512]{3,2,1,0:T(8,128)(2,1)S(1)}, u32[]{:S(2)}, u32[]{:S(2)}) %collective-permute-start.1) | collective-permute-done | bytes 245792 | tf_op jit(solution)/shard_map/ppermute | solution.py:513
  13.2 4.4 %collective-permute-start.2 = (bf16[3,9,4,512]{3,2,1,0:T(4,128)(2,1)S(1)}, bf16[3,9,4,512]{3,2,1,0:T(4,128)(2,1)S(1)}, u32[]{:S(2)}, u32[]{:S(2)}) collective-permute-start(bf16[3,9,4,512]{3,2,1,0:T(4,128)(2,1)S(1)} %get-tuple-element.23), channel_id=1, source_target_pairs={{0,15},{1,2},{2,1},{3,4},{4,3},{5,6},{6,5},{7,8},{8,7},{9,10},{10,... | collective-permute-start | bytes 331784 | tf_op jit(solution)/shard_map/ppermute | solution.py:513
  17.6 4.8 %shard_map.96.before = f32[144,128]{1,0:T(8,128)S(1)} custom-call(s32[4,16]{1,0:T(4,128)S(1)} %copy-done.5, f32[3,4,16,512]{3,2,1,0:T(8,128)S(1)} %copy-done.1, bf16[3,5,16,512]{3,2,1,0:T(8,128)(2,1)S(1)} %collective-permute-done.x_first, bf16[3,5,16,512]{3,2,1,0:T(8,128)(2,1)S(1)} %collective-permute-done.1.x_second, ...), custom_call_target="tpu_custom_call" | custom-call | flops 6899999744 | bytes 22140000 | tf_op jit(solution)/shard_map/pallas_call | solution.py:468
  22.3 14.5 %shard_map.97 = (f32[3,8,40,512]{3,2,1,0:T(8,128)S(1)}, f32[88,128]{1,0:T(8,128)S(1)}) custom-call(s32[4,16]{1,0:T(4,128)S(1)} %copy-done.5, f32[3,4,16,512]{3,2,1,0:T(8,128)S(1)} %copy-done.1, bf16[3,5,16,512]{3,2,1,0:T(8,128)(2,1)S(1)} %collective-permute-done.x_first, bf16[3,5,16,512]{3,2,1,0:T(8,128)(2,1)S(1)} %collective-permute-done.1.x_second, ...), custom_call_target="tpu_custom_call" | custom-call | flops 18400000000 | bytes 59040000 | tf_op jit(solution)/shard_map/pallas_call | solution.py:468
  36.9 0.6 collective-permute-start.4
  37.4 0.9 %collective-permute-done.4 = f32[88,128]{1,0:T(8,128)S(1)} collective-permute-done((f32[88,128]{1,0:T(8,128)S(1)}, f32[88,128]{1,0:T(8,128)S(1)}, u32[]{:S(2)}, u32[]{:S(2)}) %collective-permute-start.4) | collective-permute-done | bytes 45088 | tf_op jit(solution)/shard_map/ppermute | solution.py:513
  38.3 0.8 %collective-permute-start.7 = (f32[88,128]{1,0:T(8,128)S(1)}, f32[88,128]{1,0:T(8,128)S(1)}, u32[]{:S(2)}, u32[]{:S(2)}) collective-permute-start(f32[88,128]{1,0:T(8,128)S(1)} %add.21), channel_id=1, source_target_pairs={{0,32},{1,33},{2,34},{3,35},{4,36},{5,37},{6,38},{7,39},{8,40},{9,... | collective-permute-start | bytes 135176 | tf_op jit(solution)/shard_map/ppermute | solution.py:513
  39.1 1.5 %collective-permute-start.6 = (f32[88,128]{1,0:T(8,128)S(1)}, f32[88,128]{1,0:T(8,128)S(1)}, u32[]{:S(2)}, u32[]{:S(2)}) collective-permute-start(f32[88,128]{1,0:T(8,128)S(1)} %add.21), channel_id=1, source_target_pairs={{0,48},{1,49},{2,50},{3,51},{4,52},{5,53},{6,54},{7,55},{8,56},{9,... | collective-permute-start | bytes 135176 | tf_op jit(solution)/shard_map/ppermute | solution.py:513
  40.6 1.2 %collective-permute-start.5 = (f32[88,128]{1,0:T(8,128)S(1)}, f32[88,128]{1,0:T(8,128)S(1)}, u32[]{:S(2)}, u32[]{:S(2)}) collective-permute-start(f32[88,128]{1,0:T(8,128)S(1)} %add.21), channel_id=1, source_target_pairs={{0,16},{1,17},{2,18},{3,19},{4,20},{5,21},{6,22},{7,23},{8,24},{9,... | collective-permute-start | bytes 135176 | tf_op jit(solution)/shard_map/ppermute | solution.py:513
  41.8 2.1 %collective-permute-done.7 = f32[88,128]{1,0:T(8,128)S(1)} collective-permute-done((f32[88,128]{1,0:T(8,128)S(1)}, f32[88,128]{1,0:T(8,128)S(1)}, u32[]{:S(2)}, u32[]{:S(2)}) %collective-permute-start.7) | collective-permute-done | bytes 45088 | tf_op jit(solution)/shard_map/ppermute | solution.py:513
  43.9 0.9 %collective-permute-done.6 = f32[88,128]{1,0:T(8,128)S(1)} collective-permute-done((f32[88,128]{1,0:T(8,128)S(1)}, f32[88,128]{1,0:T(8,128)S(1)}, u32[]{:S(2)}, u32[]{:S(2)}) %collective-permute-start.6) | collective-permute-done | bytes 45088 | tf_op jit(solution)/shard_map/ppermute | solution.py:513
  44.9 2.2 %collective-permute-start.9 = (f32[88,128]{1,0:T(8,128)S(1)}, f32[88,128]{1,0:T(8,128)S(1)}, u32[]{:S(2)}, u32[]{:S(2)}) collective-permute-start(f32[88,128]{1,0:T(8,128)S(1)} %add_add_fusion.1), channel_id=1, source_target_pairs={{0,6},{1,7},{2,4},{3,5},{4,2},{5,3},{6,0},{7,1},{8,14},{9,15},{10,... | collective-permute-start | bytes 135176 | tf_op jit(solution)/shard_map/ppermute | solution.py:513
  47.1 1.3 %collective-permute-start.8 = (f32[88,128]{1,0:T(8,128)S(1)}, f32[88,128]{1,0:T(8,128)S(1)}, u32[]{:S(2)}, u32[]{:S(2)}) collective-permute-start(f32[88,128]{1,0:T(8,128)S(1)} %add_add_fusion.1), channel_id=1, source_target_pairs={{0,2},{1,3},{2,0},{3,1},{4,6},{5,7},{6,4},{7,5},{8,10},{9,11},{10,... | collective-permute-start | bytes 135176 | tf_op jit(solution)/shard_map/ppermute | solution.py:513
  48.4 2.5 %collective-permute-done.10 = f32[88,128]{1,0:T(8,128)S(1)} collective-permute-done((f32[88,128]{1,0:T(8,128)S(1)}, f32[88,128]{1,0:T(8,128)S(1)}, u32[]{:S(2)}, u32[]{:S(2)}) %collective-permute-start.10) | collective-permute-done | bytes 45088 | tf_op jit(solution)/shard_map/ppermute | solution.py:513
  50.9 0.3 collective-permute-done.8
  51.2 3.0 %collective-permute-start.13 = (f32[88,128]{1,0:T(8,128)S(1)}, f32[88,128]{1,0:T(8,128)S(1)}, u32[]{:S(2)}, u32[]{:S(2)}) collective-permute-start(f32[88,128]{1,0:T(8,128)S(1)} %add_add_fusion.a), channel_id=1, source_target_pairs={{0,8},{1,9},{2,10},{3,11},{4,12},{5,13},{6,14},{7,15},{8,0},{9,1},... | collective-permute-start | bytes 135176 | tf_op jit(solution)/shard_map/ppermute | solution.py:513
  54.1 0.8 %collective-permute-start.12 = (f32[88,128]{1,0:T(8,128)S(1)}, f32[88,128]{1,0:T(8,128)S(1)}, u32[]{:S(2)}, u32[]{:S(2)}) collective-permute-start(f32[88,128]{1,0:T(8,128)S(1)} %add_add_fusion.a), channel_id=1, source_target_pairs={{0,72},{1,73},{2,74},{3,75},{4,76},{5,77},{6,78},{7,79},{8,64},{9,... | collective-permute-start | bytes 135176 | tf_op jit(solution)/shard_map/ppermute | solution.py:513
  55.2 2.6 %shard_map.98 = f32[3,4,16,512]{3,2,1,0:T(8,128)} custom-call(f32[3,8,40,512]{3,2,1,0:T(8,128)S(1)} %get-tuple-element.27.middle), custom_call_target="tpu_custom_call" | custom-call | flops 3449999872 | bytes 11070000 | tf_op jit(solution)/shard_map/pallas_call | solution.py:468
  57.8 1.6 %collective-permute-done.12.c = f32[88,128]{1,0:T(8,128)S(1)} collective-permute-done((f32[88,128]{1,0:T(8,128)S(1)}, f32[88,128]{1,0:T(8,128)S(1)}, u32[]{:S(2)}, u32[]{:S(2)}) %collective-permute-start.12) | collective-permute-done | bytes 45088 | tf_op jit(solution)/shard_map/ppermute | solution.py:513
  59.4 0.8 %shard_map.99 = (f32[64,81]{1,0:T(8,128)}, f32[64,64]{1,0:T(8,128)}, f32[6,64]{1,0:T(8,128)}) custom-call(f32[88,128]{1,0:T(8,128)S(1)} %add_add_fusion.a, f32[88,128]{1,0:T(8,128)S(1)} %collective-permute-done.11.b, f32[88,128]{1,0:T(8,128)S(1)} %collective-permute-done.12.c, f32[88,128]{1,0:T(8,128)S(1)} %collective-permute-done.13.d), custom_call_target="tpu_custom_call" | custom-call | flops 1150000000 | bytes 3690000 | tf_op jit(solution)/shard_map/pallas_call | solution.py:468
  (28 shorter events, 0.6 us)
Async XLA Ops:
  0.6 1.0 %copy-start = (f32[3,4,16,512]{3,2,1,0:T(8,128)S(1)}, f32[3,4,16,512]{3,2,1,0:T(8,128)}, u32[]{:S(2)}) copy-start(f32[3,4,16,512]{3,2,1,0:T(8,128)} %own.9) | copy-start | bytes 1179652
  1.6 5.4 %copy-start.1 = (f32[3,4,16,512]{3,2,1,0:T(8,128)S(1)}, f32[3,4,16,512]{3,2,1,0:T(8,128)}, u32[]{:S(2)}) copy-start(f32[3,4,16,512]{3,2,1,0:T(8,128)} %own.9) | copy-start | bytes 1179652
  1.6 5.4 %copy-start.2 = (bf16[64,81]{1,0:T(8,128)(2,1)S(1)}, bf16[64,81]{1,0:T(8,128)(2,1)}, u32[]{:S(2)}) copy-start(bf16[64,81]{1,0:T(8,128)(2,1)} %first.1) | copy-start | bytes 31108
  1.6 5.4 %copy-start.3 = (bf16[64,64]{1,0:T(8,128)(2,1)S(1)}, bf16[64,64]{1,0:T(8,128)(2,1)}, u32[]{:S(2)}) copy-start(bf16[64,64]{1,0:T(8,128)(2,1)} %mid.1) | copy-start | bytes 24580
  1.6 5.4 %copy-start.4 = (bf16[6,64]{1,0:T(8,128)(2,1)S(1)}, bf16[6,64]{1,0:T(8,128)(2,1)}, u32[]{:S(2)}) copy-start(bf16[6,64]{1,0:T(8,128)(2,1)} %last.1) | copy-start | bytes 2308
  1.6 5.4 %copy-start.5 = (s32[4,16]{1,0:T(4,128)S(1)}, s32[4,16]{1,0:T(4,128)}, u32[]{:S(2)}) copy-start(s32[4,16]{1,0:T(4,128)} %offs.5) | copy-start | bytes 772
  1.6 5.4 %copy-start.6 = (bf16[960,216]{1,0:T(8,128)(2,1)S(1)}, bf16[960,216]{1,0:T(8,128)(2,1)}, u32[]{:S(2)}) copy-start(bf16[960,216]{1,0:T(8,128)(2,1)} %constant.2.clone.table) | copy-start | bytes 1244164
  1.7 10.1 %collective-permute-start = (bf16[3,5,16,512]{3,2,1,0:T(8,128)(2,1)S(1)}, bf16[3,5,16,512]{3,2,1,0:T(8,128)(2,1)S(1)}, u32[]{:S(2)}, u32[]{:S(2)}) collective-permute-start(bf16[3,5,16,512]{3,2,1,0:T(8,128)(2,1)S(1)} %get-tuple-element.18), channel_id=1, source_target_pairs={{0,16},{1,17},{2,18},{3,19},{4,20},{5,21},{6,22},{7,23},{8,24},{9,... | collective-permute-start | bytes 737288 | tf_op jit(solution)/shard_map/ppermute | solution.py:513
  3.5 9.5 %collective-permute-start.1 = (bf16[3,5,16,512]{3,2,1,0:T(8,128)(2,1)S(1)}, bf16[3,5,16,512]{3,2,1,0:T(8,128)(2,1)S(1)}, u32[]{:S(2)}, u32[]{:S(2)}) collective-permute-start(bf16[3,5,16,512]{3,2,1,0:T(8,128)(2,1)S(1)} %get-tuple-element.19), channel_id=1, source_target_pairs={{0,112},{1,113},{2,114},{3,115},{4,116},{5,117},{6,118},{7,119},{8... | collective-permute-start | bytes 737288 | tf_op jit(solution)/shard_map/ppermute | solution.py:513
  13.2 9.2 %collective-permute-start.2 = (bf16[3,9,4,512]{3,2,1,0:T(4,128)(2,1)S(1)}, bf16[3,9,4,512]{3,2,1,0:T(4,128)(2,1)S(1)}, u32[]{:S(2)}, u32[]{:S(2)}) collective-permute-start(bf16[3,9,4,512]{3,2,1,0:T(4,128)(2,1)S(1)} %get-tuple-element.23), channel_id=1, source_target_pairs={{0,15},{1,2},{2,1},{3,4},{4,3},{5,6},{6,5},{7,8},{8,7},{9,10},{10,... | collective-permute-start | bytes 331784 | tf_op jit(solution)/shard_map/ppermute | solution.py:513
  17.6 4.8 %collective-permute-start.3 = (bf16[3,9,4,512]{3,2,1,0:T(4,128)(2,1)S(1)}, bf16[3,9,4,512]{3,2,1,0:T(4,128)(2,1)S(1)}, u32[]{:S(2)}, u32[]{:S(2)}) collective-permute-start(bf16[3,9,4,512]{3,2,1,0:T(4,128)(2,1)S(1)} %get-tuple-element.24), channel_id=1, source_target_pairs={{0,1},{1,0},{2,3},{3,2},{4,5},{5,4},{6,7},{7,6},{8,9},{9,8},{10,11... | collective-permute-start | bytes 331784 | tf_op jit(solution)/shard_map/ppermute | solution.py:513
  36.9 1.5 %collective-permute-start.4 = (f32[88,128]{1,0:T(8,128)S(1)}, f32[88,128]{1,0:T(8,128)S(1)}, u32[]{:S(2)}, u32[]{:S(2)}) collective-permute-start(f32[88,128]{1,0:T(8,128)S(1)} %get-tuple-element.28), channel_id=1, source_target_pairs={{0,1},{1,0},{2,3},{3,2},{4,5},{5,4},{6,7},{7,6},{8,9},{9,8},{10,11... | collective-permute-start | bytes 135176 | tf_op jit(solution)/shard_map/ppermute | solution.py:513
  38.3 5.6 %collective-permute-start.7 = (f32[88,128]{1,0:T(8,128)S(1)}, f32[88,128]{1,0:T(8,128)S(1)}, u32[]{:S(2)}, u32[]{:S(2)}) collective-permute-start(f32[88,128]{1,0:T(8,128)S(1)} %add.21), channel_id=1, source_target_pairs={{0,32},{1,33},{2,34},{3,35},{4,36},{5,37},{6,38},{7,39},{8,40},{9,... | collective-permute-start | bytes 135176 | tf_op jit(solution)/shard_map/ppermute | solution.py:513
  39.1 5.7 %collective-permute-start.6 = (f32[88,128]{1,0:T(8,128)S(1)}, f32[88,128]{1,0:T(8,128)S(1)}, u32[]{:S(2)}, u32[]{:S(2)}) collective-permute-start(f32[88,128]{1,0:T(8,128)S(1)} %add.21), channel_id=1, source_target_pairs={{0,48},{1,49},{2,50},{3,51},{4,52},{5,53},{6,54},{7,55},{8,56},{9,... | collective-permute-start | bytes 135176 | tf_op jit(solution)/shard_map/ppermute | solution.py:513
  40.6 4.2 %collective-permute-start.5 = (f32[88,128]{1,0:T(8,128)S(1)}, f32[88,128]{1,0:T(8,128)S(1)}, u32[]{:S(2)}, u32[]{:S(2)}) collective-permute-start(f32[88,128]{1,0:T(8,128)S(1)} %add.21), channel_id=1, source_target_pairs={{0,16},{1,17},{2,18},{3,19},{4,20},{5,21},{6,22},{7,23},{8,24},{9,... | collective-permute-start | bytes 135176 | tf_op jit(solution)/shard_map/ppermute | solution.py:513
  44.8 6.1 %collective-permute-start.10 = (f32[88,128]{1,0:T(8,128)S(1)}, f32[88,128]{1,0:T(8,128)S(1)}, u32[]{:S(2)}, u32[]{:S(2)}) collective-permute-start(f32[88,128]{1,0:T(8,128)S(1)} %add_add_fusion.1), channel_id=1, source_target_pairs={{0,4},{1,5},{2,6},{3,7},{4,0},{5,1},{6,2},{7,3},{8,12},{9,13},{10,... | collective-permute-start | bytes 135176 | tf_op jit(solution)/shard_map/ppermute | solution.py:513
  44.9 6.0 %collective-permute-start.9 = (f32[88,128]{1,0:T(8,128)S(1)}, f32[88,128]{1,0:T(8,128)S(1)}, u32[]{:S(2)}, u32[]{:S(2)}) collective-permute-start(f32[88,128]{1,0:T(8,128)S(1)} %add_add_fusion.1), channel_id=1, source_target_pairs={{0,6},{1,7},{2,4},{3,5},{4,2},{5,3},{6,0},{7,1},{8,14},{9,15},{10,... | collective-permute-start | bytes 135176 | tf_op jit(solution)/shard_map/ppermute | solution.py:513
  47.1 4.0 %collective-permute-start.8 = (f32[88,128]{1,0:T(8,128)S(1)}, f32[88,128]{1,0:T(8,128)S(1)}, u32[]{:S(2)}, u32[]{:S(2)}) collective-permute-start(f32[88,128]{1,0:T(8,128)S(1)} %add_add_fusion.1), channel_id=1, source_target_pairs={{0,2},{1,3},{2,0},{3,1},{4,6},{5,7},{6,4},{7,5},{8,10},{9,11},{10,... | collective-permute-start | bytes 135176 | tf_op jit(solution)/shard_map/ppermute | solution.py:513
  51.2 6.6 %collective-permute-start.13 = (f32[88,128]{1,0:T(8,128)S(1)}, f32[88,128]{1,0:T(8,128)S(1)}, u32[]{:S(2)}, u32[]{:S(2)}) collective-permute-start(f32[88,128]{1,0:T(8,128)S(1)} %add_add_fusion.a), channel_id=1, source_target_pairs={{0,8},{1,9},{2,10},{3,11},{4,12},{5,13},{6,14},{7,15},{8,0},{9,1},... | collective-permute-start | bytes 135176 | tf_op jit(solution)/shard_map/ppermute | solution.py:513
  54.1 5.3 %collective-permute-start.12 = (f32[88,128]{1,0:T(8,128)S(1)}, f32[88,128]{1,0:T(8,128)S(1)}, u32[]{:S(2)}, u32[]{:S(2)}) collective-permute-start(f32[88,128]{1,0:T(8,128)S(1)} %add_add_fusion.a), channel_id=1, source_target_pairs={{0,72},{1,73},{2,74},{3,75},{4,76},{5,77},{6,78},{7,79},{8,64},{9,... | collective-permute-start | bytes 135176 | tf_op jit(solution)/shard_map/ppermute | solution.py:513
  54.9 4.5 %collective-permute-start.11 = (f32[88,128]{1,0:T(8,128)S(1)}, f32[88,128]{1,0:T(8,128)S(1)}, u32[]{:S(2)}, u32[]{:S(2)}) collective-permute-start(f32[88,128]{1,0:T(8,128)S(1)} %add_add_fusion.a), channel_id=1, source_target_pairs={{0,64},{1,65},{2,66},{3,67},{4,68},{5,69},{6,70},{7,71},{8,72},{9,... | collective-permute-start | bytes 135176 | tf_op jit(solution)/shard_map/ppermute | solution.py:513

commit v7 on v6

--- a/solution.py
+++ b/solution.py
@@ -43,7 +43,7 @@
 
 
 def table_parts(table):
-    return Part(table, 0, 512, 216), Part(table, 512, 768, 96), Part(table, 768, 849, 96)
+    return Part(table, 0, 512, 216), Part(table, 512, 768, 96), Part(table, 768, 864, 96)
 
 
 def edge_parts(table):
@@ -205,10 +205,10 @@
 
 
 def interior_kernel(
-    offs, own, first, mid, last, table, packed_weights, packed_totals, field, tau, tile, tile_target,
-    local_table, local_first, local_mid, local_last, sems,
+    offs, own, last, first, mid, table, packed_weights, packed_totals, field, tau, tile, tile_target,
+    local_table, local_first, local_mid, sems,
 ):
-    pairs_in = ((first, local_first), (mid, local_mid), (last, local_last), (table, local_table))
+    pairs_in = ((first, local_first), (mid, local_mid), (table, local_table))
     copies = [pltpu.make_async_copy(a, b, sems.at[k]) for k, (a, b) in enumerate(pairs_in)]
     for copy in copies:
         copy.start()
@@ -219,13 +219,13 @@
             field[c, p, 12:28, 0:512] = own[c, p]
     for copy in copies:
         copy.wait()
-    first, mid, last = local_first, local_mid, local_last
+    first, mid = local_first, local_mid
     pick, pick_target, order = table_parts(local_table)
     weights, totals = weight_parts(packed_weights), total_parts(packed_totals)
     w1, w2, w2t, w3, w3t = weights
     rows, cols = lax.broadcasted_iota(jnp.int32, (64, 64), 0), lax.broadcasted_iota(jnp.int32, (64, 64), 1)
     half = jnp.where(rows == cols, 0.5, 0.0).astype(bf16)
-    w1[...] = (0.5 * dot(first[...], order[...])).astype(bf16)
+    w1[...] = (0.5 * dot(first[...], order[...].astype(f32)[0:81].astype(bf16))).astype(bf16)
     w2[...] = twice(0.5 * mid[...].astype(f32)).astype(bf16)
     w2t[...] = twice(dot_cells(half, mid[...])).astype(bf16)
     last_rows = jnp.concatenate([last[...].astype(f32), jnp.zeros((10, 64), f32)], 0)
@@ -420,7 +420,7 @@
     lax.fori_loop(0, 4, step, 0)
     scale = 0.5**22
     ordered = lax.dot_general(
-        g1[...], order[...].astype(f32), NT, preferred_element_type=f32, precision=lax.Precision.HIGHEST
+        g1[...], order[...].astype(f32)[0:81], NT, preferred_element_type=f32, precision=lax.Precision.HIGHEST
     )
     mids = g2[...]
     packed[0:64, :] = scale * jnp.concatenate([ordered, jnp.zeros((64, 15), f32), mids[:, 0:32]], 1)
@@ -521,10 +521,10 @@
     x_first, x_second = send(to_near, near_x), send(to_far, far_x)
     weights, totals = call(
         interior_kernel,
-        (offsets, velocity, first_weight, mid_weight, last_weight, table),
+        (offsets, velocity, last_weight, first_weight, mid_weight, table),
         [WEIGHTS, TOTALS], columns_scratch(4, 2, 28)
-        + [pltpu.VMEM(n, bf16) for n in ((64, 81), (64, 64), (6, 64))] + [pltpu.SemaphoreType.DMA((4,))],
-        1, 6, 28, 4,
+        + [pltpu.VMEM(n, bf16) for n in ((64, 81), (64, 64))] + [pltpu.SemaphoreType.DMA((3,))],
+        1, 6, 28, 3,
     )
     x_first, x_second, totals = lax.optimization_barrier((x_first, x_second, totals))
     to_far, to_near = call(

time: 60.3 us -> 60.3 us (level)
  no operation moved by 1% of the time
where the time goes in v7:
time: 60.3 us; the launch traced here: 60.2 us
  Pallas kernels  27.6 us (46%)
  starting transfers between devices  21.3 us (35%)
  waiting for transfers between devices  9.45 us (16%)
  local copies, waits for them, and re-layouts  1.01 us (2%)
  between operations  0.77 us (1%)
    pallas_call x7, Pallas kernels, call(): pl.pallas_call(kernel, in_specs=[scalar] * smem + [vmem] * (len(args) - s...  27.6 us
    ppermute x14, starting transfers between devices, send(): return lax.ppermute(value, AXES, pairs(move))  21.3 us
    ppermute x14, waiting for transfers between devices, send(): return lax.ppermute(value, AXES, pairs(move))  9.45 us
  transfers between devices with their start and end apart: 14, of which 7 were waited for; matrix products, arithmetic and copies ran while one was open for 0% of the time, Pallas kernels for 20%

profile of v7, /device:TPU:0, one launch (start us, length us, event | category | flops | bytes accessed | tf_op | source)
XLA Modules:
  0.0 60.2 jit_solution(1834014180048542622)
XLA Ops:
  0.6 1.0 %copy-done = f32[3,4,16,512]{3,2,1,0:T(8,128)S(1)} copy-done((f32[3,4,16,512]{3,2,1,0:T(8,128)S(1)}, f32[3,4,16,512]{3,2,1,0:T(8,128)}, u32[]{:S(2)}) %copy-start) | copy-done | bytes 393240
  1.7 1.7 %collective-permute-start = (bf16[3,5,16,512]{3,2,1,0:T(8,128)(2,1)S(1)}, bf16[3,5,16,512]{3,2,1,0:T(8,128)(2,1)S(1)}, u32[]{:S(2)}, u32[]{:S(2)}) collective-permute-start(bf16[3,5,16,512]{3,2,1,0:T(8,128)(2,1)S(1)} %get-tuple-element.18), channel_id=1, source_target_pairs={{0,16},{1,17},{2,18},{3,19},{4,20},{5,21},{6,22},{7,23},{8,24},{9,... | collective-permute-start | bytes 737288 | tf_op jit(solution)/shard_map/ppermute | solution.py:513
  3.5 3.5 %collective-permute-start.1 = (bf16[3,5,16,512]{3,2,1,0:T(8,128)(2,1)S(1)}, bf16[3,5,16,512]{3,2,1,0:T(8,128)(2,1)S(1)}, u32[]{:S(2)}, u32[]{:S(2)}) collective-permute-start(bf16[3,5,16,512]{3,2,1,0:T(8,128)(2,1)S(1)} %get-tuple-element.19), channel_id=1, source_target_pairs={{0,112},{1,113},{2,114},{3,115},{4,116},{5,117},{6,118},{7,119},{8... | collective-permute-start | bytes 737288 | tf_op jit(solution)/shard_map/ppermute | solution.py:513
  7.0 4.8 %shard_map.94 = (bf16[480,128]{1,0:T(8,128)(2,1)S(1)}, f32[144,128]{1,0:T(8,128)S(1)}) custom-call(s32[4,16]{1,0:T(4,128)S(1)} %copy-done.5, f32[3,4,16,512]{3,2,1,0:T(8,128)S(1)} %copy-done.1, bf16[6,64]{1,0:T(8,128)(2,1)S(1)} %copy-done.4, bf16[64,81]{1,0:T(8,128)(2,1)S(1)} %copy-done.2, bf16[64,64]{1,0:T(8,128)(2,1)S(1)} %copy-done.3, ...), custom_call_target="tpu_custom_call" | custom-call | flops 6899999744 | bytes 22140000 | tf_op jit(solution)/shard_map/pallas_call | solution.py:468
  11.8 1.2 %collective-permute-done.1.x_second = bf16[3,5,16,512]{3,2,1,0:T(8,128)(2,1)S(1)} collective-permute-done((bf16[3,5,16,512]{3,2,1,0:T(8,128)(2,1)S(1)}, bf16[3,5,16,512]{3,2,1,0:T(8,128)(2,1)S(1)}, u32[]{:S(2)}, u32[]{:S(2)}) %collective-permute-start.1) | collective-permute-done | bytes 245792 | tf_op jit(solution)/shard_map/ppermute | solution.py:513
  13.2 4.4 %collective-permute-start.2 = (bf16[3,9,4,512]{3,2,1,0:T(4,128)(2,1)S(1)}, bf16[3,9,4,512]{3,2,1,0:T(4,128)(2,1)S(1)}, u32[]{:S(2)}, u32[]{:S(2)}) collective-permute-start(bf16[3,9,4,512]{3,2,1,0:T(4,128)(2,1)S(1)} %get-tuple-element.23), channel_id=1, source_target_pairs={{0,15},{1,2},{2,1},{3,4},{4,3},{5,6},{6,5},{7,8},{8,7},{9,10},{10,... | collective-permute-start | bytes 331784 | tf_op jit(solution)/shard_map/ppermute | solution.py:513
  17.6 4.8 %shard_map.96.before = f32[144,128]{1,0:T(8,128)S(1)} custom-call(s32[4,16]{1,0:T(4,128)S(1)} %copy-done.5, f32[3,4,16,512]{3,2,1,0:T(8,128)S(1)} %copy-done.1, bf16[3,5,16,512]{3,2,1,0:T(8,128)(2,1)S(1)} %collective-permute-done.x_first, bf16[3,5,16,512]{3,2,1,0:T(8,128)(2,1)S(1)} %collective-permute-done.1.x_second, ...), custom_call_target="tpu_custom_call" | custom-call | flops 6899999744 | bytes 22140000 | tf_op jit(solution)/shard_map/pallas_call | solution.py:468
  22.3 14.5 %shard_map.97 = (f32[3,8,40,512]{3,2,1,0:T(8,128)S(1)}, f32[88,128]{1,0:T(8,128)S(1)}) custom-call(s32[4,16]{1,0:T(4,128)S(1)} %copy-done.5, f32[3,4,16,512]{3,2,1,0:T(8,128)S(1)} %copy-done.1, bf16[3,5,16,512]{3,2,1,0:T(8,128)(2,1)S(1)} %collective-permute-done.x_first, bf16[3,5,16,512]{3,2,1,0:T(8,128)(2,1)S(1)} %collective-permute-done.1.x_second, ...), custom_call_target="tpu_custom_call" | custom-call | flops 18400000000 | bytes 59040000 | tf_op jit(solution)/shard_map/pallas_call | solution.py:468
  36.9 0.6 collective-permute-start.4
  37.4 0.9 %collective-permute-done.4 = f32[88,128]{1,0:T(8,128)S(1)} collective-permute-done((f32[88,128]{1,0:T(8,128)S(1)}, f32[88,128]{1,0:T(8,128)S(1)}, u32[]{:S(2)}, u32[]{:S(2)}) %collective-permute-start.4) | collective-permute-done | bytes 45088 | tf_op jit(solution)/shard_map/ppermute | solution.py:513
  38.3 0.8 %collective-permute-start.7 = (f32[88,128]{1,0:T(8,128)S(1)}, f32[88,128]{1,0:T(8,128)S(1)}, u32[]{:S(2)}, u32[]{:S(2)}) collective-permute-start(f32[88,128]{1,0:T(8,128)S(1)} %add.21), channel_id=1, source_target_pairs={{0,32},{1,33},{2,34},{3,35},{4,36},{5,37},{6,38},{7,39},{8,40},{9,... | collective-permute-start | bytes 135176 | tf_op jit(solution)/shard_map/ppermute | solution.py:513
  39.1 1.5 %collective-permute-start.6 = (f32[88,128]{1,0:T(8,128)S(1)}, f32[88,128]{1,0:T(8,128)S(1)}, u32[]{:S(2)}, u32[]{:S(2)}) collective-permute-start(f32[88,128]{1,0:T(8,128)S(1)} %add.21), channel_id=1, source_target_pairs={{0,48},{1,49},{2,50},{3,51},{4,52},{5,53},{6,54},{7,55},{8,56},{9,... | collective-permute-start | bytes 135176 | tf_op jit(solution)/shard_map/ppermute | solution.py:513
  40.6 1.2 %collective-permute-start.5 = (f32[88,128]{1,0:T(8,128)S(1)}, f32[88,128]{1,0:T(8,128)S(1)}, u32[]{:S(2)}, u32[]{:S(2)}) collective-permute-start(f32[88,128]{1,0:T(8,128)S(1)} %add.21), channel_id=1, source_target_pairs={{0,16},{1,17},{2,18},{3,19},{4,20},{5,21},{6,22},{7,23},{8,24},{9,... | collective-permute-start | bytes 135176 | tf_op jit(solution)/shard_map/ppermute | solution.py:513
  41.8 2.1 %collective-permute-done.7 = f32[88,128]{1,0:T(8,128)S(1)} collective-permute-done((f32[88,128]{1,0:T(8,128)S(1)}, f32[88,128]{1,0:T(8,128)S(1)}, u32[]{:S(2)}, u32[]{:S(2)}) %collective-permute-start.7) | collective-permute-done | bytes 45088 | tf_op jit(solution)/shard_map/ppermute | solution.py:513
  43.9 0.9 %collective-permute-done.6 = f32[88,128]{1,0:T(8,128)S(1)} collective-permute-done((f32[88,128]{1,0:T(8,128)S(1)}, f32[88,128]{1,0:T(8,128)S(1)}, u32[]{:S(2)}, u32[]{:S(2)}) %collective-permute-start.6) | collective-permute-done | bytes 45088 | tf_op jit(solution)/shard_map/ppermute | solution.py:513
  44.9 2.2 %collective-permute-start.9 = (f32[88,128]{1,0:T(8,128)S(1)}, f32[88,128]{1,0:T(8,128)S(1)}, u32[]{:S(2)}, u32[]{:S(2)}) collective-permute-start(f32[88,128]{1,0:T(8,128)S(1)} %add_add_fusion.1), channel_id=1, source_target_pairs={{0,6},{1,7},{2,4},{3,5},{4,2},{5,3},{6,0},{7,1},{8,14},{9,15},{10,... | collective-permute-start | bytes 135176 | tf_op jit(solution)/shard_map/ppermute | solution.py:513
  47.1 1.3 %collective-permute-start.8 = (f32[88,128]{1,0:T(8,128)S(1)}, f32[88,128]{1,0:T(8,128)S(1)}, u32[]{:S(2)}, u32[]{:S(2)}) collective-permute-start(f32[88,128]{1,0:T(8,128)S(1)} %add_add_fusion.1), channel_id=1, source_target_pairs={{0,2},{1,3},{2,0},{3,1},{4,6},{5,7},{6,4},{7,5},{8,10},{9,11},{10,... | collective-permute-start | bytes 135176 | tf_op jit(solution)/shard_map/ppermute | solution.py:513
  48.4 2.5 %collective-permute-done.10 = f32[88,128]{1,0:T(8,128)S(1)} collective-permute-done((f32[88,128]{1,0:T(8,128)S(1)}, f32[88,128]{1,0:T(8,128)S(1)}, u32[]{:S(2)}, u32[]{:S(2)}) %collective-permute-start.10) | collective-permute-done | bytes 45088 | tf_op jit(solution)/shard_map/ppermute | solution.py:513
  50.9 0.3 collective-permute-done.8
  51.2 3.0 %collective-permute-start.13 = (f32[88,128]{1,0:T(8,128)S(1)}, f32[88,128]{1,0:T(8,128)S(1)}, u32[]{:S(2)}, u32[]{:S(2)}) collective-permute-start(f32[88,128]{1,0:T(8,128)S(1)} %add_add_fusion.a), channel_id=1, source_target_pairs={{0,8},{1,9},{2,10},{3,11},{4,12},{5,13},{6,14},{7,15},{8,0},{9,1},... | collective-permute-start | bytes 135176 | tf_op jit(solution)/shard_map/ppermute | solution.py:513
  54.1 0.8 %collective-permute-start.12 = (f32[88,128]{1,0:T(8,128)S(1)}, f32[88,128]{1,0:T(8,128)S(1)}, u32[]{:S(2)}, u32[]{:S(2)}) collective-permute-start(f32[88,128]{1,0:T(8,128)S(1)} %add_add_fusion.a), channel_id=1, source_target_pairs={{0,72},{1,73},{2,74},{3,75},{4,76},{5,77},{6,78},{7,79},{8,64},{9,... | collective-permute-start | bytes 135176 | tf_op jit(solution)/shard_map/ppermute | solution.py:513
  55.2 2.6 %shard_map.98 = f32[3,4,16,512]{3,2,1,0:T(8,128)} custom-call(f32[3,8,40,512]{3,2,1,0:T(8,128)S(1)} %get-tuple-element.27.middle), custom_call_target="tpu_custom_call" | custom-call | flops 3449999872 | bytes 11070000 | tf_op jit(solution)/shard_map/pallas_call | solution.py:468
  57.8 1.6 %collective-permute-done.12.c = f32[88,128]{1,0:T(8,128)S(1)} collective-permute-done((f32[88,128]{1,0:T(8,128)S(1)}, f32[88,128]{1,0:T(8,128)S(1)}, u32[]{:S(2)}, u32[]{:S(2)}) %collective-permute-start.12) | collective-permute-done | bytes 45088 | tf_op jit(solution)/shard_map/ppermute | solution.py:513
  59.4 0.8 %shard_map.99 = (f32[64,81]{1,0:T(8,128)}, f32[64,64]{1,0:T(8,128)}, f32[6,64]{1,0:T(8,128)}) custom-call(f32[88,128]{1,0:T(8,128)S(1)} %add_add_fusion.a, f32[88,128]{1,0:T(8,128)S(1)} %collective-permute-done.11.b, f32[88,128]{1,0:T(8,128)S(1)} %collective-permute-done.12.c, f32[88,128]{1,0:T(8,128)S(1)} %collective-permute-done.13.d), custom_call_target="tpu_custom_call" | custom-call | flops 1150000000 | bytes 3690000 | tf_op jit(solution)/shard_map/pallas_call | solution.py:468
  (28 shorter events, 0.6 us)
Async XLA Ops:
  0.6 1.0 %copy-start = (f32[3,4,16,512]{3,2,1,0:T(8,128)S(1)}, f32[3,4,16,512]{3,2,1,0:T(8,128)}, u32[]{:S(2)}) copy-start(f32[3,4,16,512]{3,2,1,0:T(8,128)} %own.9) | copy-start | bytes 1179652
  1.6 5.4 %copy-start.1 = (f32[3,4,16,512]{3,2,1,0:T(8,128)S(1)}, f32[3,4,16,512]{3,2,1,0:T(8,128)}, u32[]{:S(2)}) copy-start(f32[3,4,16,512]{3,2,1,0:T(8,128)} %own.9) | copy-start | bytes 1179652
  1.6 5.4 %copy-start.2 = (bf16[64,81]{1,0:T(8,128)(2,1)S(1)}, bf16[64,81]{1,0:T(8,128)(2,1)}, u32[]{:S(2)}) copy-start(bf16[64,81]{1,0:T(8,128)(2,1)} %first.1) | copy-start | bytes 31108
  1.6 5.4 %copy-start.3 = (bf16[64,64]{1,0:T(8,128)(2,1)S(1)}, bf16[64,64]{1,0:T(8,128)(2,1)}, u32[]{:S(2)}) copy-start(bf16[64,64]{1,0:T(8,128)(2,1)} %mid.1) | copy-start | bytes 24580
  1.6 5.4 %copy-start.4 = (bf16[6,64]{1,0:T(8,128)(2,1)S(1)}, bf16[6,64]{1,0:T(8,128)(2,1)}, u32[]{:S(2)}) copy-start(bf16[6,64]{1,0:T(8,128)(2,1)} %last.1) | copy-start | bytes 2308
  1.6 5.4 %copy-start.5 = (s32[4,16]{1,0:T(4,128)S(1)}, s32[4,16]{1,0:T(4,128)}, u32[]{:S(2)}) copy-start(s32[4,16]{1,0:T(4,128)} %offs.5) | copy-start | bytes 772
  1.6 5.4 %copy-start.6 = (bf16[960,216]{1,0:T(8,128)(2,1)S(1)}, bf16[960,216]{1,0:T(8,128)(2,1)}, u32[]{:S(2)}) copy-start(bf16[960,216]{1,0:T(8,128)(2,1)} %constant.2.clone.table) | copy-start | bytes 1244164
  1.7 10.1 %collective-permute-start = (bf16[3,5,16,512]{3,2,1,0:T(8,128)(2,1)S(1)}, bf16[3,5,16,512]{3,2,1,0:T(8,128)(2,1)S(1)}, u32[]{:S(2)}, u32[]{:S(2)}) collective-permute-start(bf16[3,5,16,512]{3,2,1,0:T(8,128)(2,1)S(1)} %get-tuple-element.18), channel_id=1, source_target_pairs={{0,16},{1,17},{2,18},{3,19},{4,20},{5,21},{6,22},{7,23},{8,24},{9,... | collective-permute-start | bytes 737288 | tf_op jit(solution)/shard_map/ppermute | solution.py:513
  3.5 9.5 %collective-permute-start.1 = (bf16[3,5,16,512]{3,2,1,0:T(8,128)(2,1)S(1)}, bf16[3,5,16,512]{3,2,1,0:T(8,128)(2,1)S(1)}, u32[]{:S(2)}, u32[]{:S(2)}) collective-permute-start(bf16[3,5,16,512]{3,2,1,0:T(8,128)(2,1)S(1)} %get-tuple-element.19), channel_id=1, source_target_pairs={{0,112},{1,113},{2,114},{3,115},{4,116},{5,117},{6,118},{7,119},{8... | collective-permute-start | bytes 737288 | tf_op jit(solution)/shard_map/ppermute | solution.py:513
  13.2 9.2 %collective-permute-start.2 = (bf16[3,9,4,512]{3,2,1,0:T(4,128)(2,1)S(1)}, bf16[3,9,4,512]{3,2,1,0:T(4,128)(2,1)S(1)}, u32[]{:S(2)}, u32[]{:S(2)}) collective-permute-start(bf16[3,9,4,512]{3,2,1,0:T(4,128)(2,1)S(1)} %get-tuple-element.23), channel_id=1, source_target_pairs={{0,15},{1,2},{2,1},{3,4},{4,3},{5,6},{6,5},{7,8},{8,7},{9,10},{10,... | collective-permute-start | bytes 331784 | tf_op jit(solution)/shard_map/ppermute | solution.py:513
  17.6 4.8 %collective-permute-start.3 = (bf16[3,9,4,512]{3,2,1,0:T(4,128)(2,1)S(1)}, bf16[3,9,4,512]{3,2,1,0:T(4,128)(2,1)S(1)}, u32[]{:S(2)}, u32[]{:S(2)}) collective-permute-start(bf16[3,9,4,512]{3,2,1,0:T(4,128)(2,1)S(1)} %get-tuple-element.24), channel_id=1, source_target_pairs={{0,1},{1,0},{2,3},{3,2},{4,5},{5,4},{6,7},{7,6},{8,9},{9,8},{10,11... | collective-permute-start | bytes 331784 | tf_op jit(solution)/shard_map/ppermute | solution.py:513
  36.9 1.5 %collective-permute-start.4 = (f32[88,128]{1,0:T(8,128)S(1)}, f32[88,128]{1,0:T(8,128)S(1)}, u32[]{:S(2)}, u32[]{:S(2)}) collective-permute-start(f32[88,128]{1,0:T(8,128)S(1)} %get-tuple-element.28), channel_id=1, source_target_pairs={{0,1},{1,0},{2,3},{3,2},{4,5},{5,4},{6,7},{7,6},{8,9},{9,8},{10,11... | collective-permute-start | bytes 135176 | tf_op jit(solution)/shard_map/ppermute | solution.py:513
  38.3 5.6 %collective-permute-start.7 = (f32[88,128]{1,0:T(8,128)S(1)}, f32[88,128]{1,0:T(8,128)S(1)}, u32[]{:S(2)}, u32[]{:S(2)}) collective-permute-start(f32[88,128]{1,0:T(8,128)S(1)} %add.21), channel_id=1, source_target_pairs={{0,32},{1,33},{2,34},{3,35},{4,36},{5,37},{6,38},{7,39},{8,40},{9,... | collective-permute-start | bytes 135176 | tf_op jit(solution)/shard_map/ppermute | solution.py:513
  39.1 5.7 %collective-permute-start.6 = (f32[88,128]{1,0:T(8,128)S(1)}, f32[88,128]{1,0:T(8,128)S(1)}, u32[]{:S(2)}, u32[]{:S(2)}) collective-permute-start(f32[88,128]{1,0:T(8,128)S(1)} %add.21), channel_id=1, source_target_pairs={{0,48},{1,49},{2,50},{3,51},{4,52},{5,53},{6,54},{7,55},{8,56},{9,... | collective-permute-start | bytes 135176 | tf_op jit(solution)/shard_map/ppermute | solution.py:513
  40.6 4.2 %collective-permute-start.5 = (f32[88,128]{1,0:T(8,128)S(1)}, f32[88,128]{1,0:T(8,128)S(1)}, u32[]{:S(2)}, u32[]{:S(2)}) collective-permute-start(f32[88,128]{1,0:T(8,128)S(1)} %add.21), channel_id=1, source_target_pairs={{0,16},{1,17},{2,18},{3,19},{4,20},{5,21},{6,22},{7,23},{8,24},{9,... | collective-permute-start | bytes 135176 | tf_op jit(solution)/shard_map/ppermute | solution.py:513
  44.8 6.1 %collective-permute-start.10 = (f32[88,128]{1,0:T(8,128)S(1)}, f32[88,128]{1,0:T(8,128)S(1)}, u32[]{:S(2)}, u32[]{:S(2)}) collective-permute-start(f32[88,128]{1,0:T(8,128)S(1)} %add_add_fusion.1), channel_id=1, source_target_pairs={{0,4},{1,5},{2,6},{3,7},{4,0},{5,1},{6,2},{7,3},{8,12},{9,13},{10,... | collective-permute-start | bytes 135176 | tf_op jit(solution)/shard_map/ppermute | solution.py:513
  44.9 6.0 %collective-permute-start.9 = (f32[88,128]{1,0:T(8,128)S(1)}, f32[88,128]{1,0:T(8,128)S(1)}, u32[]{:S(2)}, u32[]{:S(2)}) collective-permute-start(f32[88,128]{1,0:T(8,128)S(1)} %add_add_fusion.1), channel_id=1, source_target_pairs={{0,6},{1,7},{2,4},{3,5},{4,2},{5,3},{6,0},{7,1},{8,14},{9,15},{10,... | collective-permute-start | bytes 135176 | tf_op jit(solution)/shard_map/ppermute | solution.py:513
  47.1 4.0 %collective-permute-start.8 = (f32[88,128]{1,0:T(8,128)S(1)}, f32[88,128]{1,0:T(8,128)S(1)}, u32[]{:S(2)}, u32[]{:S(2)}) collective-permute-start(f32[88,128]{1,0:T(8,128)S(1)} %add_add_fusion.1), channel_id=1, source_target_pairs={{0,2},{1,3},{2,0},{3,1},{4,6},{5,7},{6,4},{7,5},{8,10},{9,11},{10,... | collective-permute-start | bytes 135176 | tf_op jit(solution)/shard_map/ppermute | solution.py:513
  51.2 6.6 %collective-permute-start.13 = (f32[88,128]{1,0:T(8,128)S(1)}, f32[88,128]{1,0:T(8,128)S(1)}, u32[]{:S(2)}, u32[]{:S(2)}) collective-permute-start(f32[88,128]{1,0:T(8,128)S(1)} %add_add_fusion.a), channel_id=1, source_target_pairs={{0,8},{1,9},{2,10},{3,11},{4,12},{5,13},{6,14},{7,15},{8,0},{9,1},... | collective-permute-start | bytes 135176 | tf_op jit(solution)/shard_map/ppermute | solution.py:513
  54.1 5.3 %collective-permute-start.12 = (f32[88,128]{1,0:T(8,128)S(1)}, f32[88,128]{1,0:T(8,128)S(1)}, u32[]{:S(2)}, u32[]{:S(2)}) collective-permute-start(f32[88,128]{1,0:T(8,128)S(1)} %add_add_fusion.a), channel_id=1, source_target_pairs={{0,72},{1,73},{2,74},{3,75},{4,76},{5,77},{6,78},{7,79},{8,64},{9,... | collective-permute-start | bytes 135176 | tf_op jit(solution)/shard_map/ppermute | solution.py:513
  54.9 4.5 %collective-permute-start.11 = (f32[88,128]{1,0:T(8,128)S(1)}, f32[88,128]{1,0:T(8,128)S(1)}, u32[]{:S(2)}, u32[]{:S(2)}) collective-permute-start(f32[88,128]{1,0:T(8,128)S(1)} %add_add_fusion.a), channel_id=1, source_target_pairs={{0,64},{1,65},{2,66},{3,67},{4,68},{5,69},{6,70},{7,71},{8,72},{9,... | collective-permute-start | bytes 135176 | tf_op jit(solution)/shard_map/ppermute | solution.py:513
